TPU v7x, 128 devices: a whole 4x4x4 slice. The times are simulated.
128 devices in a mesh: seq: 64 (over y, z, x_hi, core), rep: 2 (over x_lo).
Axes of the slice: x: 4 (x_hi: 2, x_lo: 2; x = x_hi * 2 + x_lo), y: 4, z: 4, core: 2. Of those that a mesh axis runs over, the one named last changes fastest.
Arguments:
- inputs: bfloat16 [2, 8192, 1152], P('rep', 'seq'), may hold values from -6 to 6
- out_grad: bfloat16 [2, 8192, 1152], P('rep', 'seq'), may hold values from -6 to 6
- doc_ids: int32 [2, 128], P('rep'), may hold values from 0 to 2, as said below
- owners: int32 [91], replicated, may hold values from 0 to 127, as said below
- masters: float32 [128, 1152, 256], P(('seq', 'rep')), may hold values from -0.1875 to 0.1875
- first_old: float32 [128, 1152, 256], P(('seq', 'rep'))
- second_old: float32 [128, 1152, 256], P(('seq', 'rep')), as said below
- left_basis: float32 [128, 1152, 1152], P(('seq', 'rep')), may hold values from -1 to 1, as said below
- right_basis: float32 [128, 256, 256], P(('seq', 'rep')), may hold values from -1 to 1, as said below
- gains: float32 [5120], replicated, may hold values from 0.5 to 1.5
- gain_first: float32 [5120], replicated, may hold values from -384 to 384
- gain_second: float32 [5120], replicated, may hold values from 16384 to 65536
Outputs:
- layer_out: bfloat16 [2, 8192, 1152], P('rep', 'seq')
- input_grad: float32 [2, 8192, 1152], P('rep', 'seq')
- new_masters: float32 [128, 1152, 256], P(('seq', 'rep'))
- new_first: float32 [128, 1152, 256], P(('seq', 'rep'))
- new_second: float32 [128, 1152, 256], P(('seq', 'rep'))
- new_gains: float32 [5120], replicated
- new_gain_first: float32 [5120], replicated
- new_gain_second: float32 [5120], replicated
Inputs may be any that keep to these rules, and one draw needn't show every extreme that they name: `doc_ids`: along each sequence the ids never fall; they start at 0 and end at 2. `owners`: no two tiles share a slot. `second_old`: Positive. `left_basis`: each slot's matrix is orthogonal. `right_basis`: each slot's matrix is orthogonal.
All inputs are finite; a program needn't handle non-finite values.
Results may differ from a plain program's by a relative error of at most 0.02.
Values may be sent and summed in bfloat16 or wider, within the bound.
A program may use at most 512 MiB of HBM per device.

v0:
```python
import jax
import jax.numpy as jnp
from jax import lax
from jax.sharding import PartitionSpec as P

FF = 6912
HEADS = 4
WINDOW = 512
BLK = 64
STEP = 10


NORM_EPS = 1e-06
THETA = 10000.0
BETA_ONE = 0.5
BETA_TWO = 0.5
RATE = 0.02
GAIN_RATE = 0.4
DECAY = 0.01
ADAM_EPS = 1e-08
HIGH = lax.Precision.HIGHEST


def passed_along(block, axis, distance):
    devices = range(lax.axis_size(axis))
    route = [(i - distance, i) for i in devices if i - distance in devices]
    return lax.ppermute(block, axis, route)


def rms_norm(values, gain):
    return values * lax.rsqrt(jnp.mean(values * values, axis=-1, keepdims=True) + NORM_EPS) * gain


def rotary(values, positions):
    half = values.shape[-1] // 2
    freq = jnp.exp(-jnp.log(THETA) * jnp.arange(half, dtype=jnp.float32) * 2.0 / values.shape[-1])
    angle = positions.astype(jnp.float32)[:, None] * freq[None, :]
    shape = (values.shape[0],) + (1,) * (values.ndim - 2) + (half,)
    cosine = jnp.cos(angle).reshape(shape)
    sine = jnp.sin(angle).reshape(shape)
    first = values[..., :half]
    second = values[..., half:]
    return jnp.concatenate(
        [first * cosine - second * sine, second * cosine + first * sine], axis=-1
    )


def gate_product(gate_pre, up_pre):
    return jax.nn.gelu(gate_pre, approximate=True) * up_pre


def doc_lookup(table, positions):
    block_index = jnp.clip(positions // BLK, 0, table.shape[0] - 1)
    match = jnp.arange(table.shape[0], dtype=jnp.int32)[None, :] == block_index[:, None]
    return jnp.sum(jnp.where(match, table[None, :], 0), axis=1)


def local(
    inputs,
    out_grad,
    doc_ids,
    owners,
    masters,
    first_old,
    second_old,
    left_basis,
    right_basis,
    gains,
    gain_first,
    gain_second,
):
    tok_rows = inputs.shape[1]
    model_width = inputs.shape[2]
    head_dim = right_basis.shape[1]
    slot_count = masters.shape[0]
    tile_total = owners.shape[0]
    ff_tiles = FF // head_dim
    rep_count = lax.axis_size("rep")
    seq_index = lax.axis_index("seq")
    rep_index = lax.axis_index("rep")
    low_masters = masters.astype(jnp.bfloat16)
    gathered = lax.all_gather(low_masters, ("seq", "rep"), axis=0, tiled=True)
    tiles = jnp.take(gathered, owners, axis=0)
    w_query = tiles[0:HEADS]
    w_key = tiles[HEADS]
    w_value = tiles[HEADS + 1]
    w_out = tiles[HEADS + 2 : 2 * HEADS + 2]
    base = 2 * HEADS + 2
    w_gate = tiles[base : base + ff_tiles]
    w_up = tiles[base + ff_tiles : base + 2 * ff_tiles]
    w_down = tiles[base + 2 * ff_tiles : base + 3 * ff_tiles]
    g_apre = gains[0:model_width]
    g_apost = gains[model_width : 2 * model_width]
    g_fpre = gains[2 * model_width : 3 * model_width]
    g_fpost = gains[3 * model_width : 4 * model_width]
    g_query = gains[4 * model_width : 4 * model_width + head_dim]
    g_key = gains[4 * model_width + head_dim :]
    activ = inputs[0].astype(jnp.float32)
    local_pos = seq_index * tok_rows + jnp.arange(tok_rows, dtype=jnp.int32)
    normed_in = rms_norm(activ, g_apre).astype(jnp.bfloat16)
    queries_raw = jnp.einsum("td,hdc->thc", normed_in, w_query, preferred_element_type=jnp.float32)
    keys_raw = jnp.dot(normed_in, w_key, preferred_element_type=jnp.float32)
    values_raw = jnp.dot(normed_in, w_value, preferred_element_type=jnp.float32)

    def query_path(raw, gain):
        return rotary(rms_norm(raw, gain), local_pos)

    queries_low = query_path(queries_raw, g_query).astype(jnp.bfloat16)
    keys_low = query_path(keys_raw, g_key).astype(jnp.bfloat16)
    values_low = values_raw.astype(jnp.bfloat16)
    hop_count = -(-WINDOW // tok_rows)
    local_pair = jnp.stack([keys_low, values_low])
    far_pieces = []
    for step_back in range(hop_count, 0, -1):
        far_pieces.append(passed_along(local_pair, "seq", step_back))
    all_pairs = jnp.concatenate(far_pieces + [local_pair], axis=1)
    all_keys = all_pairs[0]
    all_values = all_pairs[1]
    key_pos = seq_index * tok_rows - WINDOW + jnp.arange(WINDOW + tok_rows, dtype=jnp.int32)
    doc_table = doc_ids[0]
    query_docs = doc_lookup(doc_table, local_pos)
    key_docs = doc_lookup(doc_table, key_pos)
    visible = (key_docs[None, :] == query_docs[:, None]) & (key_pos[None, :] <= local_pos[:, None])
    visible = visible & (local_pos[:, None] - key_pos[None, :] < WINDOW) & (key_pos[None, :] >= 0)
    score_scale = head_dim ** (-0.5)
    scores = (
        jnp.einsum("thc,kc->thk", queries_low, all_keys, preferred_element_type=jnp.float32)
        * score_scale
    )
    scores = jnp.where(visible[:, None, :], scores, -1e30)
    row_top = jnp.max(scores, axis=-1, keepdims=True)
    expo = jnp.exp(scores - row_top)
    probs = expo / jnp.sum(expo, axis=-1, keepdims=True)
    probs_low = probs.astype(jnp.bfloat16)
    attended = jnp.einsum(
        "thk,kc->thc", probs_low, all_values, preferred_element_type=jnp.float32
    ).astype(jnp.bfloat16)
    projected = jnp.einsum("thc,hdc->td", attended, w_out, preferred_element_type=jnp.float32)
    residual_one = activ + rms_norm(projected, g_apost)
    normed_ffn = rms_norm(residual_one, g_fpre).astype(jnp.bfloat16)
    gate_pre = jnp.einsum("td,kdc->tkc", normed_ffn, w_gate, preferred_element_type=jnp.float32)
    up_pre = jnp.einsum("td,kdc->tkc", normed_ffn, w_up, preferred_element_type=jnp.float32)
    hidden = gate_product(gate_pre, up_pre).astype(jnp.bfloat16)
    down = jnp.einsum("tkc,kdc->td", hidden, w_down, preferred_element_type=jnp.float32)
    result = residual_one + rms_norm(down, g_fpost)
    layer_out = result.astype(jnp.bfloat16)[None]
    cotangent = out_grad[0].astype(jnp.float32)
    unused, pull = jax.vjp(rms_norm, down, g_fpost)
    d_down, d_gfpost = pull(cotangent)
    d_down_low = d_down.astype(jnp.bfloat16)
    d_hidden = jnp.einsum("td,kdc->tkc", d_down_low, w_down, preferred_element_type=jnp.float32)
    unused, pull = jax.vjp(gate_product, gate_pre, up_pre)
    d_gate, d_up = pull(d_hidden)
    d_gate_low = d_gate.astype(jnp.bfloat16)
    d_up_low = d_up.astype(jnp.bfloat16)
    d_normed_ffn = jnp.einsum("tkc,kdc->td", d_gate_low, w_gate, preferred_element_type=jnp.float32)
    d_normed_ffn = d_normed_ffn + jnp.einsum(
        "tkc,kdc->td", d_up_low, w_up, preferred_element_type=jnp.float32
    )
    unused, pull = jax.vjp(rms_norm, residual_one, g_fpre)
    d_res_part, d_gfpre = pull(d_normed_ffn)
    d_residual = cotangent + d_res_part
    unused, pull = jax.vjp(rms_norm, projected, g_apost)
    d_projected, d_gapost = pull(d_residual)
    d_proj_low = d_projected.astype(jnp.bfloat16)
    d_mixed = jnp.einsum(
        "td,hdc->thc", d_proj_low, w_out, preferred_element_type=jnp.float32
    ).astype(jnp.bfloat16)
    d_probs = jnp.einsum("thc,kc->thk", d_mixed, all_values, preferred_element_type=jnp.float32)
    inner_sum = jnp.sum(probs * d_probs, axis=-1, keepdims=True)
    d_scores = (probs * (d_probs - inner_sum) * score_scale).astype(jnp.bfloat16)
    d_queries = jnp.einsum("thk,kc->thc", d_scores, all_keys, preferred_element_type=jnp.float32)
    d_keys_all = jnp.einsum(
        "thk,thc->kc", d_scores, queries_low, preferred_element_type=jnp.float32
    )
    d_values_all = jnp.einsum("thk,thc->kc", probs_low, d_mixed, preferred_element_type=jnp.float32)
    full_len = hop_count * tok_rows + tok_rows
    pad_rows = full_len - (WINDOW + tok_rows)
    d_pairs = jnp.stack([d_keys_all, d_values_all])
    d_pairs = jnp.concatenate([jnp.zeros((2, pad_rows, head_dim), jnp.float32), d_pairs], axis=1)
    d_local = d_pairs[:, hop_count * tok_rows :]
    for step_back in range(hop_count, 0, -1):
        piece_index = hop_count - step_back
        piece = d_pairs[:, piece_index * tok_rows : (piece_index + 1) * tok_rows]
        d_local = d_local + passed_along(piece.astype(jnp.bfloat16), "seq", -step_back).astype(
            piece.dtype
        )
    unused, pull = jax.vjp(query_path, keys_raw, g_key)
    d_keys_raw, d_gkey = pull(d_local[0])
    unused, pull = jax.vjp(query_path, queries_raw, g_query)
    d_queries_raw, d_gquery = pull(d_queries)
    d_queries_low = d_queries_raw.astype(jnp.bfloat16)
    d_keys_low = d_keys_raw.astype(jnp.bfloat16)
    d_values_low = d_local[1].astype(jnp.bfloat16)
    d_normed_in = jnp.einsum(
        "thc,hdc->td", d_queries_low, w_query, preferred_element_type=jnp.float32
    )
    d_normed_in = d_normed_in + jnp.einsum(
        "tc,dc->td", d_keys_low, w_key, preferred_element_type=jnp.float32
    )
    d_normed_in = d_normed_in + jnp.einsum(
        "tc,dc->td", d_values_low, w_value, preferred_element_type=jnp.float32
    )
    unused, pull = jax.vjp(rms_norm, activ, g_apre)
    d_in_part, d_gapre = pull(d_normed_in)
    input_grad = (d_residual + d_in_part)[None]
    gain_local = jnp.concatenate([d_gapre, d_gapost, d_gfpre, d_gfpost, d_gquery, d_gkey])
    gain_grads = lax.psum(gain_local, ("seq", "rep"))
    lefts = jnp.stack([normed_in, d_proj_low, normed_ffn, d_down_low])
    rights = jnp.concatenate(
        [
            d_queries_low.reshape(tok_rows, HEADS * head_dim),
            d_keys_low,
            d_values_low,
            attended.reshape(tok_rows, HEADS * head_dim),
            d_gate_low.reshape(tok_rows, FF),
            d_up_low.reshape(tok_rows, FF),
            hidden.reshape(tok_rows, FF),
        ],
        axis=1,
    )
    rights = rights.reshape(tok_rows, tile_total, head_dim)
    tile_ids = jnp.arange(tile_total, dtype=jnp.int32)
    my_linear = seq_index * rep_count + rep_index
    my_slots = my_linear * slot_count + jnp.arange(slot_count, dtype=jnp.int32)
    match = (
        owners[None, :]
        == jnp.arange(lax.axis_size(("seq", "rep")) * slot_count, dtype=jnp.int32)[:, None]
    )
    present = jnp.any(match, axis=1)
    tile_of = jnp.sum(jnp.where(match, tile_ids[None, :], 0), axis=1)
    present, tile_of = (present, tile_of)
    kind = (tile_of >= HEADS + 2).astype(jnp.int32) + (tile_of >= 2 * HEADS + 2).astype(jnp.int32)
    kind = kind + (tile_of >= 2 * HEADS + 2 + 2 * ff_tiles).astype(jnp.int32)
    left_sel = jnp.take(lefts, kind, axis=0)
    right_sel = jnp.take(rights, tile_of, axis=1)
    grads = lax.psum_scatter(
        jnp.where(
            present[:, None, None],
            jnp.einsum("std,tsc->sdc", left_sel, right_sel, preferred_element_type=jnp.float32),
            0.0,
        ),
        ("seq", "rep"),
        scatter_dimension=0,
        tiled=True,
    )
    owned = jnp.any(owners[None, :] == my_slots[:, None], axis=1)[:, None, None]
    rotated = jnp.einsum("sdi,sdc->sic", left_basis, grads, precision=HIGH)
    rotated = jnp.einsum("sic,scj->sij", rotated, right_basis, precision=HIGH)
    first_new = BETA_ONE * first_old + (1.0 - BETA_ONE) * rotated
    second_new = BETA_TWO * second_old + (1.0 - BETA_TWO) * rotated * rotated
    normed_step = (
        first_new
        / (1.0 - BETA_ONE**STEP)
        / (jnp.sqrt(second_new / (1.0 - BETA_TWO**STEP)) + ADAM_EPS)
    )
    back = jnp.einsum("sdi,sij->sdj", left_basis, normed_step, precision=HIGH)
    back = jnp.einsum("sdj,scj->sdc", back, right_basis, precision=HIGH)
    weight_new = masters - RATE * (back + DECAY * masters)
    new_masters = jnp.where(owned, weight_new, masters)
    new_first = jnp.where(owned, first_new, first_old)
    new_second = jnp.where(owned, second_new, second_old)
    new_gain_first = BETA_ONE * gain_first + (1.0 - BETA_ONE) * gain_grads
    new_gain_second = BETA_TWO * gain_second + (1.0 - BETA_TWO) * gain_grads * gain_grads
    gain_step = (
        new_gain_first
        / (1.0 - BETA_ONE**STEP)
        / (jnp.sqrt(new_gain_second / (1.0 - BETA_TWO**STEP)) + ADAM_EPS)
    )
    new_gains = gains - GAIN_RATE * gain_step
    return (
        layer_out,
        input_grad,
        new_masters,
        new_first,
        new_second,
        new_gains,
        new_gain_first,
        new_gain_second,
    )


def solution(mesh):
    return jax.shard_map(
        local,
        mesh=mesh,
        in_specs=(
            P("rep", "seq", None),
            P("rep", "seq", None),
            P("rep", None),
            P(),
            P(("seq", "rep"), None, None),
            P(("seq", "rep"), None, None),
            P(("seq", "rep"), None, None),
            P(("seq", "rep"), None, None),
            P(("seq", "rep"), None, None),
            P(),
            P(),
            P(),
        ),
        out_specs=(
            P("rep", "seq", None),
            P("rep", "seq", None),
            P(("seq", "rep"), None, None),
            P(("seq", "rep"), None, None),
            P(("seq", "rep"), None, None),
            P(),
            P(),
            P(),
        ),
        check_vma=False,
    )
```

profile of v0, /device:TPU:1, one launch (start us, length us, event | category | flops | bytes accessed | tf_op | source)
XLA Modules:
  0.0 3216.1 jit_solution(15287953517059289162)
XLA Ops:
  7.3 2.2 convert_element_type.159
  13.4 418.5 %all-gather.2.cloned.1.call-done = bf16[128,1152,256]{2,1,0:T(8,128)(2,1)} async-done(((bf16[1,1152,256]{2,1,0:T(8,128)(2,1)}), bf16[128,1152,256]{2,1,0:T(8,128)(2,1)}) %all-gather.2.cloned.1.call-update) | async-done | bytes 75497488 | tf_op jit(solution)/shard_map/all_gather | solution.py:82
  431.8 36.3 %gather_fusion = bf16[91,1152,256]{2,1,0:T(8,128)(2,1)} fusion(bf16[128,1152,256]{2,1,0:T(8,128)(2,1)} %all-gather.2.cloned.1.call-done, s32[1024]{0:T(1024)S(1)} %pad_clamp_fusion.2), kind=kCustom, calls=%fused_computation | custom fusion | bytes 107348336 | tf_op jit(solution)/shard_map/jit(_take)/gather | solution.py:83
  468.2 36.1 %broadcast_select_fusion = bf16[91,1152,256]{2,1,0:T(8,128)(2,1)} fusion(bf16[91,1152,256]{2,1,0:T(8,128)(2,1)} %gather_fusion, pred[91]{0:T(512)(128)(4,1)S(1)} %get-tuple-element.55), kind=kLoop, calls=%fused_computation.6 | loop fusion | flops 26836992 | bytes 107348056 | tf_op jit(solution)/shard_map/jit(_take)/select_n | solution.py:83
  504.3 1.3 fusion.81
  505.6 1.4 multiply_reduce_fusion.13
  507.9 3.0 collective-permute-start
  511.0 3.6 collective-permute-start.1
  514.5 4.0 collective-permute-start.2
  518.5 5.7 collective-permute-start.3
  524.2 2.3 multiply_reduce_fusion.10
  526.9 1.7 fusion.198
  528.7 1.2 convolution_convert_fusion
  529.9 2.7 multiply_reduce_fusion.7
  533.0 7.0 fusion.15
  540.0 10.0 multiply_convert_fusion.1
  550.0 9.1 multiply_reduce_fusion.5
  560.9 11.3 fusion.31
  572.2 8.9 fusion.42
  581.2 21.4 multiply_reduce_fusion.1
  603.7 2.5 fusion.68
  608.1 4.5 fusion.66
  612.5 5.8 convolution_bitcast_fusion.4
  618.3 2.7 convolution_bitcast_fusion.3
  623.0 1.9 collective-permute-start.7
  624.9 1.3 collective-permute-start.6
  626.2 1.3 collective-permute-start.5
  627.5 1.3 collective-permute-start.4
  630.8 3.9 copy.57
  634.7 2.3 copy.58
  636.9 2.7 copy.59
  640.8 14.0 gather_fusion.1
  655.6 1.3 fusion.135
  659.8 2.9 constant_dynamic-update-slice_fusion.7
  662.7 1.3 constant_dynamic-update-slice_fusion.6
  664.0 1.3 constant_dynamic-update-slice_fusion.5
  665.4 8.6 copy.62
  674.0 9.4 gather_fusion.2
  683.4 67.6 %convolution_select_fusion = f32[128,1152,256]{2,1,0:T(8,128)} fusion(pred[128]{0:T(512)(128)(4,1)S(1)} %copy-done.35, bf16[128,128,1152]{2,1,0:T(8,128)(2,1)} %gather_fusion.1, pred[128]{0:T(512)(128)(4,1)S(1)} %copy-done.37, bf16[128,128,256]{2,1,0:T(8,128)(2,1)} %gather_fusion.2, pred[128]{0:T(512)(128)(4,1)S(1)} %copy-done.36), kind=kOutput, calls=%fused_computation.5 | convolution fusion | flops 9724493824 | bytes 197132672 | tf_op jit(solution)/shard_map/std,tsc->sdc/dot_general | solution.py:240
  752.0 2.6 convolution_bitcast_fusion.1
  754.7 1.5 convolution_add_fusion.1
  756.2 1.5 fusion.99
  757.8 79.0 %psum.7 = f32[5120]{0:T(1024)S(1)} all-reduce(f32[5120]{0:T(1024)S(1)} %constant_dynamic-update-slice_fusion.13), channel_id=1, replica_groups=mesh['seq'=64,'rep'=2] {'seq','rep'}, use_global_device_ids=true, to_apply=%region_27.28 | all-reduce | flops 5120 | bytes 40960 | tf_op jit(solution)/shard_map/psum | solution.py:208
  838.5 2341.1 %reduce-scatter.2.cloned.1.call-done = f32[1,1152,256]{2,1,0:T(8,128)} async-done(((f32[128,1152,256]{2,1,0:T(8,128)}), f32[1,1152,256]{2,1,0:T(8,128)}) %reduce-scatter.2.cloned.1.call-update) | async-done | bytes 1179664 | tf_op jit(solution)/shard_map/reduce_scatter | solution.py:237
  3179.6 8.4 fusion.22
  3188.1 4.3 fusion.82
  3192.4 13.0 fusion.20
  3205.4 3.7 fusion.35
  (226 shorter events, 21.3 us)
Async XLA Ops:
  7.2 3180.9 %copy-start = (f32[1,256,256]{2,1,0:T(8,128)S(1)}, f32[1,256,256]{2,1,0:T(8,128)}, u32[]{:S(2)}) copy-start(f32[1,256,256]{2,1,0:T(8,128)} %param.20) | copy-start | bytes 786436
  7.2 4.4 copy-start.1
  7.2 5.8 copy-start.29
  7.2 424.6 %all-gather.2.cloned.1.call-start = ((), (), s32[]{:S(2)}) async-start(), calls=%async_computation.1 | async-start | bytes 76087296 | tf_op jit(solution)/shard_map/all_gather | solution.py:82
  9.5 3170.1 %reduce-scatter.2.cloned.1.call-start = ((), (), s32[]{:S(2)}) async-start(), calls=%async_computation.2 | async-start | bytes 152174592 | tf_op jit(solution)/shard_map/reduce_scatter | solution.py:237
  9.6 498.0 %copy-start.53 = (f32[128]{0:T(128)}, f32[128]{0:T(128)S(1)}, u32[]{:S(2)}) copy-start(f32[128]{0:T(128)S(1)} %multiply_exponential_fusion) | copy-start | bytes 1540
  9.6 497.9 %copy-start.55 = (f32[128]{0:T(128)}, f32[128]{0:T(128)S(1)}, u32[]{:S(2)}) copy-start(f32[128]{0:T(128)S(1)} %get-tuple-element.78) | copy-start | bytes 1540
  11.7 456.4 %copy-start.59 = (f32[128]{0:T(128)}, f32[128]{0:T(128)S(1)}, u32[]{:S(2)}) copy-start(f32[128]{0:T(128)S(1)} %fusion.100) | copy-start | bytes 1540
  12.4 511.8 %copy-start.50 = (f32[128]{0:T(128)}, f32[128]{0:T(128)S(1)}, u32[]{:S(2)}) copy-start(f32[128]{0:T(128)S(1)} %fusion.174) | copy-start | bytes 1540
  13.0 513.5 %copy-start.42 = (f32[256]{0:T(256)}, f32[256]{0:T(256)S(1)}, u32[]{:S(2)}) copy-start(f32[256]{0:T(256)S(1)} %get-tuple-element.48) | copy-start | bytes 3076
  13.0 511.2 %copy-start.31 = (f32[1152]{0:T(1024)}, f32[1152]{0:T(1024)S(1)}, u32[]{:S(2)}) copy-start(f32[1152]{0:T(1024)S(1)} %get-tuple-element.47) | copy-start | bytes 13828
  13.2 515.5 %copy-start.34 = (pred[128,640]{1,0:T(8,128)(4,1)}, pred[128,640]{1,0:T(8,128)(4,1)S(1)}, u32[]{:S(2)}) copy-start(pred[128,640]{1,0:T(8,128)(4,1)S(1)} %fusion.118) | copy-start | bytes 245764
  13.4 492.2 %copy-start.18 = (bf16[1,128,1152]{2,1,0:T(8,128)(2,1)}, bf16[1,128,1152]{2,1,0:T(8,128)(2,1)S(1)}, u32[]{:S(2)}) copy-start(bf16[1,128,1152]{2,1,0:T(8,128)(2,1)S(1)} %fusion.103) | copy-start | bytes 884740
  507.0 19.5 copy-start.20
  507.0 19.5 copy-start.48
  507.9 18.9 collective-permute-start
  511.0 15.9 collective-permute-start.1
  514.5 12.3 collective-permute-start.2
  518.5 8.4 collective-permute-start.3
  532.9 69.6 %copy-start.57 = (f32[128]{0:T(128)}, f32[128]{0:T(128)S(1)}, u32[]{:S(2)}) copy-start(f32[128]{0:T(128)S(1)} %fusion.177) | copy-start | bytes 1540
  540.0 10.0 copy-start.65
  550.0 9.2 copy-start.9
  560.9 11.3 copy-start.14
  603.7 4.3 copy-start.67
  621.2 7.7 copy-start.15
  621.2 7.7 copy-start.17
  621.2 7.7 copy-start.19
  622.1 7.0 copy-start.44
  622.2 7.8 copy-start.27
  623.0 32.6 %collective-permute-start.7 = (bf16[2,128,256]{2,1,0:T(8,128)(2,1)}, bf16[2,128,256]{2,1,0:T(8,128)(2,1)}, u32[]{:S(2)}, u32[]{:S(2)}) collective-permute-start(bf16[2,128,256]{2,1,0:T(8,128)(2,1)} %get-tuple-element.31), channel_id=1, source_target_pairs={{2,0},{4,2},{6,4},{8,6},{10,8},{12,10},{14,12},{16,14},{18,16},{20... | collective-permute-start | bytes 393224 | tf_op jit(solution)/shard_map/ppermute | solution.py:27
  624.9 30.7 collective-permute-start.6
  626.2 29.4 collective-permute-start.5
  627.5 28.1 collective-permute-start.4
  630.0 4.7 copy-start.12
  654.9 4.2 copy-start.22
  657.9 4.8 copy-start.3
  674.0 9.4 copy-start.35
  674.0 9.4 copy-start.36
  674.0 9.4 copy-start.37
  752.0 4.2 copy-start.51
  754.6 82.2 %copy-start.60 = (f32[128]{0:T(128)S(1)}, f32[128]{0:T(128)}, u32[]{:S(2)}) copy-start(f32[128]{0:T(128)} %copy-done.59) | copy-start | bytes 1540
  754.6 82.2 %copy-start.30 = (f32[5120]{0:T(1024)S(1)}, f32[5120]{0:T(1024)}, u32[]{:S(2)}) copy-start(f32[5120]{0:T(1024)} %param.21) | copy-start | bytes 61444
  754.6 82.2 %copy-start.40 = (f32[5120]{0:T(1024)S(1)}, f32[5120]{0:T(1024)}, u32[]{:S(2)}) copy-start(f32[5120]{0:T(1024)} %param.22) | copy-start | bytes 61444
  754.6 82.2 %copy-start.41 = (f32[5120]{0:T(1024)S(1)}, f32[5120]{0:T(1024)}, u32[]{:S(2)}) copy-start(f32[5120]{0:T(1024)} %param.23) | copy-start | bytes 61444
  754.6 82.8 %copy-start.5 = (f32[128,1152]{1,0:T(8,128)S(1)}, f32[128,1152]{1,0:T(8,128)}, u32[]{:S(2)}) copy-start(f32[128,1152]{1,0:T(8,128)} %copy-done.4) | copy-start | bytes 1769476
  838.5 2349.6 %copy-start.6 = (f32[1,1152,256]{2,1,0:T(8,128)S(1)}, f32[1,1152,256]{2,1,0:T(8,128)}, u32[]{:S(2)}) copy-start(f32[1,1152,256]{2,1,0:T(8,128)} %param.18) | copy-start | bytes 3538948
  838.5 2349.6 %copy-start.7 = (f32[1,1152,256]{2,1,0:T(8,128)S(1)}, f32[1,1152,256]{2,1,0:T(8,128)}, u32[]{:S(2)}) copy-start(f32[1,1152,256]{2,1,0:T(8,128)} %param.17) | copy-start | bytes 3538948
  3192.4 13.0 copy-start.8
  (30 other events, 75.1 us)
Sparse Core Ops, SparseCore 0:
  10.3 421.4 all-gather.1
  751.2 2428.3 reduce-scatter.1
where the time goes:
time: 3210 us; the launch traced here: 3220 us
  waiting for transfers between devices  2760 us (86%)
  matrix products  197 us (6%)
  local copies, waits for them, and re-layouts  91.6 us (3%)
  blocking collectives  79 us (2%)
  other arithmetic  51.5 us (2%)
    reduce_scatter x1, waiting for transfers between devices, local(): lax.psum_scatter(jnp.where(present[:, None, None], jnp.einsum('std,tsc->s...  2340 us
    all_gather x1, waiting for transfers between devices, local(): gathered = lax.all_gather(low_masters, ('seq', 'rep'), axis=0, tiled=True)  418 us
    psum x1, blocking collectives, local(): gain_grads = lax.psum(gain_local, ('seq', 'rep'))  79 us
    dot_general x1, matrix products, local(): jnp.einsum('std,tsc->sdc', left_sel, right_sel, preferred_element_type=jn...  67.6 us
  transfers between devices with their start and end apart: 10, of which 2 were waited for; matrix products, arithmetic and copies ran while one was open for 1% of the time, Pallas kernels for 0%

commit v1 on v0

v1 whole, which is shorter than its diff:
```python
import functools

import jax
import jax.numpy as jnp
from jax import lax
from jax.experimental import pallas as pl
from jax.experimental.pallas import tpu as pltpu
from jax.sharding import Mesh
from jax.sharding import PartitionSpec as P

FF = 6912
HEADS = 4
WINDOW = 512
BLK = 64
STEP = 10
D = 1152
HD = 256
TOK = 128
GROUP = 8
SLICE = HD // GROUP
ATT = 2 * HEADS + 2
FFT = FF // HD

NORM_EPS = 1e-06
THETA = 10000.0
BETA_ONE = 0.5
BETA_TWO = 0.5
RATE = 0.02
GAIN_RATE = 0.4
DECAY = 0.01
ADAM_EPS = 1e-08

MESH = pl.DeviceIdType.MESH
AXES = ("y", "z", "xh", "core", "xl")
VMEM_LIMIT = 56 * 1024 * 1024
BF = jnp.bfloat16
F32 = jnp.float32


def here():
    y, z, xh, c, xl = [lax.axis_index(a) for a in AXES]
    return y, z, xh * 2 + xl, c


def place(y, z, x, c):
    return (y, z, x // 2, c, lax.rem(x, 2))


def member(x, c):
    return (x // 2) * 4 + c * 2 + lax.rem(x, 2)


def of_member(q):
    return (q // 4) * 2 + q % 2, (q // 2) % 2


def turn(a, d):
    return lax.rem(a + d, 4)


def greet(places):
    sem = pltpu.get_barrier_semaphore()
    for p in places:
        pl.semaphore_signal(sem, inc=1, device_id=p, device_id_type=MESH)
    pl.semaphore_wait(sem, len(places))


def remote(src, dst, send, recv, where):
    return pltpu.make_async_remote_copy(src, dst, send, recv, device_id=where, device_id_type=MESH)


def params(cid):
    return pltpu.CompilerParams(
        collective_id=cid, has_side_effects=True, vmem_limit_bytes=VMEM_LIMIT
    )


ANY = pl.BlockSpec(memory_space=pl.ANY)
INV = pl.BlockSpec(memory_space=pltpu.VMEM)
DMA = pltpu.SemaphoreType.DMA


def gather_body(x_ref, o_ref, own_sem, xs, xr, cs, cr):
    y, z, x, c = here()
    peers = [place(y, z, turn(x, d), c) for d in (1, 2, 3)]
    twin = place(y, z, x, 1 - c)
    greet(peers + [twin])
    mine = o_ref.at[:, member(x, c)]
    own = pltpu.make_async_copy(x_ref, mine, own_sem)
    far = [remote(x_ref, mine, xs.at[i], xr.at[i], p) for i, p in enumerate(peers)]
    for i in (1, 0, 2):
        far[i].start()
    near = [remote(x_ref, mine, cs.at[3], cr.at[3], twin)]
    near[0].start()
    own.start()
    for i in (0, 2, 1):
        far[i].wait_recv()
        src = o_ref.at[:, member(turn(x, 3 - i), c)]
        step = remote(src, src, cs.at[i], cr.at[i], twin)
        step.start()
        near.append(step)
    own.wait()
    for step in near:
        step.wait()
    for step in far:
        step.wait_send()


def gather_group(x, cid):
    n, r, w = x.shape
    return pl.pallas_call(
        gather_body,
        out_shape=jax.ShapeDtypeStruct((n, GROUP, r, w), x.dtype),
        in_specs=[ANY],
        out_specs=ANY,
        scratch_shapes=[DMA, DMA((3,)), DMA((3,)), DMA((4,)), DMA((4,))],
        compiler_params=params(cid),
    )(x)


def sum_body(x_ref, o_ref, own, near, part, far, own_sem, cs, cr, xs, xr):
    y, z, x, c = here()
    peers = [place(y, z, turn(x, d), c) for d in (1, 2, 3)]
    twin = place(y, z, x, 1 - c)
    greet(peers + [twin])
    n = x_ref.shape[0]
    swap, load = [], []
    for k, d in enumerate((2, 1, 3, 0)):
        xd = turn(x, d)
        swap.append(remote(x_ref.at[:, xd // 2, 1 - c, lax.rem(xd, 2)], near.at[k], cs.at[k], cr.at[k], twin))
        load.append(pltpu.make_async_copy(x_ref.at[:, xd // 2, c, lax.rem(xd, 2)], own.at[k], own_sem.at[k]))
        swap[-1].start()
        load[-1].start()
    sends = []
    for k, d in enumerate((2, 1, 3, 0)):
        load[k].wait()
        swap[k].wait_recv()

        def add(i, carry, k=k):
            part[k, i] = (own[k, i].astype(F32) + near[k, i].astype(F32)).astype(BF)
            return carry

        if d:
            lax.fori_loop(0, n, add, 0)
            step = remote(part.at[k], far.at[k], xs.at[k], xr.at[k], peers[d - 1])
            step.start()
            sends.append(step)
    for step in sends:
        step.wait_recv()

    def total(i, carry):
        first = own[3, i].astype(F32) + near[3, i].astype(F32)
        o_ref[i] = ((first + far[0, i].astype(F32)) + far[1, i].astype(F32)) + far[2, i].astype(F32)
        return carry

    lax.fori_loop(0, n, total, 0)
    for step in swap + sends:
        step.wait_send()


def sum_group(x, cid):
    n, _, r, w = x.shape
    blk = (n, r, w)
    return pl.pallas_call(
        sum_body,
        out_shape=jax.ShapeDtypeStruct(blk, F32),
        in_specs=[ANY],
        out_specs=INV,
        scratch_shapes=[
            pltpu.VMEM((4,) + blk, BF),
            pltpu.VMEM((4,) + blk, BF),
            pltpu.VMEM((3,) + blk, BF),
            pltpu.VMEM((3,) + blk, BF),
            DMA((4,)),
            DMA((4,)),
            DMA((4,)),
            DMA((3,)),
            DMA((3,)),
        ],
        compiler_params=params(cid),
    )(x.reshape(n, 2, 2, 2, r, w))


def weights_body(t_ref, o_ref, own_sem, gs, gr, s1, r1, s2, r2):
    y, z, x, c = here()
    me = member(x, c)
    friends = []
    for dx in range(4):
        for dc in range(2):
            if dx or dc:
                friends.append((turn(x, dx), lax.rem(c + dc, 2)))
    ring_z = [place(y, turn(z, d), x, c) for d in (1, 2, 3)]
    ring_y = [place(turn(y, d), z, x, c) for d in (1, 2, 3)]
    greet([place(y, z, *f) for f in friends] + ring_z + ring_y)
    mine = o_ref.at[y, z, me // 4, lax.rem(me, 4)]
    spread = []
    for i, f in enumerate(friends):
        step = remote(t_ref.at[member(*f)], mine, gs.at[i], gr.at[i], place(y, z, *f))
        step.start()
        spread.append(step)
    own = pltpu.make_async_copy(t_ref.at[me], mine, own_sem)
    own.start()
    own.wait()
    for step in spread:
        step.wait_recv()
    first = []
    for i in (1, 0, 2):
        a = remote(o_ref.at[y, z, 0], o_ref.at[y, z, 0], s1.at[0, i], r1.at[0, i], ring_z[i])
        b = remote(o_ref.at[y, z, 1], o_ref.at[y, z, 1], s1.at[1, i], r1.at[1, i], ring_y[i])
        a.start()
        b.start()
        first.append((i, a, b))
    second = []

    def onward(j, yy, zz):
        for i in (1, 0, 2):
            ra = o_ref.at[y, zz, 0]
            rb = o_ref.at[yy, z, 1]
            a = remote(ra, ra, s2.at[0, j, i], r2.at[0, j, i], ring_y[i])
            b = remote(rb, rb, s2.at[1, j, i], r2.at[1, j, i], ring_z[i])
            a.start()
            b.start()
            second.extend([a, b])

    onward(3, y, z)
    order = sorted(first, key=lambda f: (f[0] == 1, f[0]))
    for i, a, b in order:
        a.wait_recv()
        b.wait_recv()
        onward(i, turn(y, 3 - i), turn(z, 3 - i))
    for step in second:
        step.wait()
    for i, a, b in first:
        a.wait_send()
        b.wait_send()
    for step in spread:
        step.wait_send()


def gather_slices(tile, cid):
    return pl.pallas_call(
        weights_body,
        out_shape=jax.ShapeDtypeStruct((4, 4, 2, 4, SLICE, D), BF),
        in_specs=[ANY],
        out_specs=ANY,
        scratch_shapes=[
            DMA,
            DMA((7,)),
            DMA((7,)),
            DMA((2, 3)),
            DMA((2, 3)),
            DMA((2, 4, 3)),
            DMA((2, 4, 3)),
        ],
        compiler_params=params(cid),
    )(tile)


def grads_body(
    d_ref, g_ref, o_ref, go_ref,
    own1, in1, mid, in2, fin, gin, gmid, gin2,
    own_sem, s1, r1, s2, r2, gs, gr, gas, gar, gbs, gbr,
):
    y, z, x, c = here()
    me = member(x, c)
    friends = []
    for dx in range(4):
        for dc in range(2):
            if dx or dc:
                friends.append((turn(x, dx), lax.rem(c + dc, 2)))
    ring_z = [place(y, turn(z, d), x, c) for d in (1, 2, 3)]
    ring_y = [place(turn(y, d), z, x, c) for d in (1, 2, 3)]
    group = [place(y, z, *f) for f in friends]
    greet(group + ring_z + ring_y)
    first = []
    for i in (1, 0, 2):
        a = remote(d_ref.at[turn(y, i + 1), :, 0], in1.at[0, i], s1.at[0, i], r1.at[0, i], ring_y[i])
        b = remote(d_ref.at[:, turn(z, i + 1), 1], in1.at[1, i], s1.at[1, i], r1.at[1, i], ring_z[i])
        a.start()
        b.start()
        first.extend([a, b])
    la = pltpu.make_async_copy(d_ref.at[y, :, 0], own1.at[0], own_sem.at[0])
    lb = pltpu.make_async_copy(d_ref.at[:, z, 1], own1.at[1], own_sem.at[1])
    la.start()
    lb.start()
    gains = []
    for i, p in enumerate(group):
        step = remote(g_ref, gin.at[i], gas.at[i], gar.at[i], p)
        step.start()
        gains.append(step)
    for step in gains:
        step.wait_recv()
    acc = g_ref[...]
    for i in range(7):
        acc = acc + gin[i]
    gmid[0] = acc
    more = []
    for i, p in enumerate(ring_z):
        step = remote(gmid.at[0], gin2.at[0, i], gbs.at[0, i], gbr.at[0, i], p)
        step.start()
        more.append(step)
    for step in more:
        step.wait_recv()
    gmid[1] = gmid[0] + gin2[0, 0] + gin2[0, 1] + gin2[0, 2]
    for i, p in enumerate(ring_y):
        step = remote(gmid.at[1], gin2.at[1, i], gbs.at[1, i], gbr.at[1, i], p)
        step.start()
        more.append(step)
    for step in more[3:]:
        step.wait_recv()
    go_ref[...] = gmid[1] + gin2[1, 0] + gin2[1, 1] + gin2[1, 2]
    la.wait()
    lb.wait()
    for step in first:
        step.wait_recv()
    second = []
    for i in (1, 0, 2, 3):
        za = turn(z, i + 1)
        yb = turn(y, i + 1)
        for half, at in ((0, za), (1, yb)):
            def add(k, carry, half=half, at=at, i=i):
                t = own1[half, at, k].astype(F32) + in1[half, 0, at, k].astype(F32)
                t = t + in1[half, 1, at, k].astype(F32)
                mid[half, i, k] = (t + in1[half, 2, at, k].astype(F32)).astype(BF)
                return carry

            lax.fori_loop(0, 4, add, 0)
        if i < 3:
            a = remote(mid.at[0, i], in2.at[0, i], s2.at[0, i], r2.at[0, i], ring_z[i])
            b = remote(mid.at[1, i], in2.at[1, i], s2.at[1, i], r2.at[1, i], ring_y[i])
            a.start()
            b.start()
            second.extend([a, b])
    for step in second:
        step.wait_recv()
    for half in range(2):
        def add(k, carry, half=half):
            t = mid[half, 3, k].astype(F32) + in2[half, 0, k].astype(F32)
            t = t + in2[half, 1, k].astype(F32)
            fin[half * 4 + k] = (t + in2[half, 2, k].astype(F32)).astype(BF)
            return carry

        lax.fori_loop(0, 4, add, 0)
    spread = []
    for i, f in enumerate(friends):
        step = remote(fin.at[member(*f)], o_ref.at[me], gs.at[i], gr.at[i], place(y, z, *f))
        step.start()
        spread.append(step)
    last = pltpu.make_async_copy(fin.at[me], o_ref.at[me], own_sem.at[2])
    last.start()
    last.wait()
    for step in spread:
        step.wait()
    for step in first + second + gains + more:
        step.wait_send()


def sum_slices(slices, gains, cid):
    return pl.pallas_call(
        grads_body,
        out_shape=(
            jax.ShapeDtypeStruct((GROUP, SLICE, D), BF),
            jax.ShapeDtypeStruct(gains.shape, F32),
        ),
        in_specs=[ANY, INV],
        out_specs=(INV, INV),
        scratch_shapes=[
            pltpu.VMEM((2, 4, 4, SLICE, D), BF),
            pltpu.VMEM((2, 3, 4, 4, SLICE, D), BF),
            pltpu.VMEM((2, 4, 4, SLICE, D), BF),
            pltpu.VMEM((2, 3, 4, SLICE, D), BF),
            pltpu.VMEM((8, SLICE, D), BF),
            pltpu.VMEM((7,) + gains.shape, F32),
            pltpu.VMEM((2,) + gains.shape, F32),
            pltpu.VMEM((2, 3) + gains.shape, F32),
            DMA((3,)),
            DMA((2, 3)),
            DMA((2, 3)),
            DMA((2, 3)),
            DMA((2, 3)),
            DMA((7,)),
            DMA((7,)),
            DMA((7,)),
            DMA((7,)),
            DMA((2, 3)),
            DMA((2, 3)),
        ],
        compiler_params=params(cid),
    )(slices, gains)


def seq_place(s):
    return (s // 16, lax.rem(s // 4, 4), lax.rem(s // 2, 2), lax.rem(s, 2), lax.axis_index("xl"))


def seq_index():
    y, z, xh, c, xl = [lax.axis_index(a) for a in AXES]
    return ((y * 4 + z) * 2 + xh) * 2 + c


def ahead_body(x_ref, o_ref, own_sem, ss, rs):
    s = seq_index()
    sem = pltpu.get_barrier_semaphore()
    for d in range(1, 5):
        pl.semaphore_signal(sem, inc=1, device_id=seq_place(lax.rem(s + 64 - d, 64)), device_id_type=MESH)
    pl.semaphore_wait(sem, 4)
    steps = []
    for d in (4, 3, 2, 1):
        step = remote(x_ref, o_ref.at[4 - d], ss.at[d - 1], rs.at[d - 1], seq_place(lax.rem(s + d, 64)))
        step.start()
        steps.append(step)
    own = pltpu.make_async_copy(x_ref, o_ref.at[4], own_sem)
    own.start()
    own.wait()
    for step in steps:
        step.wait()


def send_ahead(kv, cid):
    return pl.pallas_call(
        ahead_body,
        out_shape=jax.ShapeDtypeStruct((5,) + kv.shape, kv.dtype),
        in_specs=[ANY],
        out_specs=ANY,
        scratch_shapes=[DMA, DMA((4,)), DMA((4,))],
        compiler_params=params(cid),
    )(kv)


def back_body(x_ref, o_ref, ss, rs):
    s = seq_index()
    sem = pltpu.get_barrier_semaphore()
    for d in range(1, 5):
        pl.semaphore_signal(sem, inc=1, device_id=seq_place(lax.rem(s + d, 64)), device_id_type=MESH)
    pl.semaphore_wait(sem, 4)
    steps = []
    for d in (4, 3, 2, 1):
        step = remote(x_ref.at[4 - d], o_ref.at[d - 1], ss.at[d - 1], rs.at[d - 1], seq_place(lax.rem(s + 64 - d, 64)))
        step.start()
        steps.append(step)
    for step in steps:
        step.wait()


def send_back(pieces, cid):
    return pl.pallas_call(
        back_body,
        out_shape=jax.ShapeDtypeStruct((4,) + pieces.shape[1:], pieces.dtype),
        in_specs=[ANY],
        out_specs=ANY,
        scratch_shapes=[DMA((4,)), DMA((4,))],
        compiler_params=params(cid),
    )(pieces)


def rms_norm(values, gain):
    return values * lax.rsqrt(jnp.mean(values * values, axis=-1, keepdims=True) + NORM_EPS) * gain


def rotary(values, positions):
    half = values.shape[-1] // 2
    freq = jnp.exp(-jnp.log(THETA) * jnp.arange(half, dtype=F32) * 2.0 / values.shape[-1])
    angle = positions.astype(F32)[:, None] * freq[None, :]
    shape = (values.shape[0],) + (1,) * (values.ndim - 2) + (half,)
    cosine = jnp.cos(angle).reshape(shape)
    sine = jnp.sin(angle).reshape(shape)
    first = values[..., :half]
    second = values[..., half:]
    return jnp.concatenate(
        [first * cosine - second * sine, second * cosine + first * sine], axis=-1
    )


def gate_product(gate_pre, up_pre):
    return jax.nn.gelu(gate_pre, approximate=True) * up_pre


def doc_lookup(table, positions):
    block_index = jnp.clip(positions // BLK, 0, table.shape[0] - 1)
    match = jnp.arange(table.shape[0], dtype=jnp.int32)[None, :] == block_index[:, None]
    return jnp.sum(jnp.where(match, table[None, :], 0), axis=1)


def dot(a, b, da, db):
    return lax.dot_general(a, b, (((da,), (db,)), ((), ())), preferred_element_type=F32)


def local(
    inputs,
    out_grad,
    doc_ids,
    owners,
    masters,
    first_old,
    second_old,
    left_basis,
    right_basis,
    gains,
    gain_first,
    gain_second,
):
    g_apre = gains[0:D]
    g_apost = gains[D : 2 * D]
    g_fpre = gains[2 * D : 3 * D]
    g_fpost = gains[3 * D : 4 * D]
    g_query = gains[4 * D : 4 * D + HD]
    g_key = gains[4 * D + HD :]
    my_seq = seq_index()
    my_slot = my_seq * 2 + lax.axis_index("xl")

    tile = masters[0].T.astype(BF).reshape(GROUP, SLICE, D)
    slots = gather_slices(tile, 1).reshape(128, SLICE, D)
    w_att = gather_group(jnp.take(slots, owners[:ATT], axis=0), 2).reshape(ATT, HD, D)
    w_ffn = jnp.take(slots, owners[ATT:], axis=0).reshape(3, FFT * SLICE, D)
    w_gate, w_up, w_down = w_ffn[0], w_ffn[1], w_ffn[2]
    w_qkv = w_att[: HEADS + 2].reshape((HEADS + 2) * HD, D)
    w_out = w_att[HEADS + 2 :].reshape(HEADS * HD, D)

    activ = inputs[0].astype(F32)
    local_pos = my_seq * TOK + jnp.arange(TOK, dtype=jnp.int32)
    normed_in = rms_norm(activ, g_apre).astype(BF)
    raw = dot(normed_in, w_qkv, 1, 1)
    queries_raw = raw[:, : HEADS * HD].reshape(TOK, HEADS, HD)
    keys_raw = raw[:, HEADS * HD : HEADS * HD + HD]
    values_raw = raw[:, HEADS * HD + HD :]

    def query_path(values, gain):
        return rotary(rms_norm(values, gain), local_pos)

    queries_low = query_path(queries_raw, g_query).astype(BF)
    keys_low = query_path(keys_raw, g_key).astype(BF)
    values_low = values_raw.astype(BF)
    pairs = send_ahead(jnp.stack([keys_low, values_low]), 3)
    all_keys = pairs[:, 0].reshape(WINDOW + TOK, HD)
    all_values = pairs[:, 1].reshape(WINDOW + TOK, HD)
    key_pos = my_seq * TOK - WINDOW + jnp.arange(WINDOW + TOK, dtype=jnp.int32)
    doc_table = doc_ids[0]
    query_docs = doc_lookup(doc_table, local_pos)
    key_docs = doc_lookup(doc_table, key_pos)
    visible = (key_docs[None, :] == query_docs[:, None]) & (key_pos[None, :] <= local_pos[:, None])
    visible = visible & (local_pos[:, None] - key_pos[None, :] < WINDOW) & (key_pos[None, :] >= 0)
    score_scale = HD ** (-0.5)
    scores = (
        jnp.einsum("thc,kc->thk", queries_low, all_keys, preferred_element_type=F32) * score_scale
    )
    scores = jnp.where(visible[:, None, :], scores, -1e30)
    row_top = jnp.max(scores, axis=-1, keepdims=True)
    expo = jnp.exp(scores - row_top)
    probs = expo / jnp.sum(expo, axis=-1, keepdims=True)
    probs_low = probs.astype(BF)
    attended = jnp.einsum("thk,kc->thc", probs_low, all_values, preferred_element_type=F32)
    attended = attended.astype(BF).reshape(TOK, HEADS * HD)
    projected = dot(attended, w_out, 1, 0)
    residual_one = activ + rms_norm(projected, g_apost)
    normed_ffn = rms_norm(residual_one, g_fpre).astype(BF)

    xf = gather_group(normed_ffn[None], 4).reshape(GROUP * TOK, D)
    gate_pre = dot(xf, w_gate, 1, 1)
    up_pre = dot(xf, w_up, 1, 1)
    hidden = gate_product(gate_pre, up_pre).astype(BF)
    down_part = dot(hidden, w_down, 1, 0).astype(BF)
    down = sum_group(down_part.reshape(1, GROUP, TOK, D), 5)[0]
    result = residual_one + rms_norm(down, g_fpost)
    layer_out = result.astype(BF)[None]
    cotangent = out_grad[0].astype(F32)
    unused, pull = jax.vjp(rms_norm, down, g_fpost)
    d_down, d_gfpost = pull(cotangent)
    d_down_all = gather_group(d_down.astype(BF)[None], 6).reshape(GROUP * TOK, D)
    d_hidden = dot(d_down_all, w_down, 1, 1)
    unused, pull = jax.vjp(gate_product, gate_pre, up_pre)
    d_gate, d_up = pull(d_hidden)
    d_gate_low = d_gate.astype(BF)
    d_up_low = d_up.astype(BF)
    d_xf_part = (dot(d_gate_low, w_gate, 1, 0) + dot(d_up_low, w_up, 1, 0)).astype(BF)
    d_normed_ffn = sum_group(d_xf_part.reshape(1, GROUP, TOK, D), 7)[0]
    t_gate = dot(d_gate_low, xf, 0, 0).astype(BF)
    t_up = dot(d_up_low, xf, 0, 0).astype(BF)
    t_down = dot(hidden, d_down_all, 0, 0).astype(BF)

    unused, pull = jax.vjp(rms_norm, residual_one, g_fpre)
    d_res_part, d_gfpre = pull(d_normed_ffn)
    d_residual = cotangent + d_res_part
    unused, pull = jax.vjp(rms_norm, projected, g_apost)
    d_projected, d_gapost = pull(d_residual)
    d_proj_low = d_projected.astype(BF)
    d_mixed = dot(d_proj_low, w_out, 1, 1).astype(BF)
    d_mixed_heads = d_mixed.reshape(TOK, HEADS, HD)
    d_probs = jnp.einsum("thc,kc->thk", d_mixed_heads, all_values, preferred_element_type=F32)
    inner_sum = jnp.sum(probs * d_probs, axis=-1, keepdims=True)
    d_scores = (probs * (d_probs - inner_sum) * score_scale).astype(BF)
    d_queries = jnp.einsum("thk,kc->thc", d_scores, all_keys, preferred_element_type=F32)
    d_keys_all = jnp.einsum("thk,thc->kc", d_scores, queries_low, preferred_element_type=F32)
    d_values_all = jnp.einsum("thk,thc->kc", probs_low, d_mixed_heads, preferred_element_type=F32)
    d_pairs = jnp.stack([d_keys_all.reshape(5, TOK, HD), d_values_all.reshape(5, TOK, HD)], axis=1)
    others = send_back(d_pairs[:4].astype(BF), 8)
    d_local = d_pairs[4] + jnp.sum(others.astype(F32), axis=0)
    unused, pull = jax.vjp(query_path, keys_raw, g_key)
    d_keys_raw, d_gkey = pull(d_local[0])
    unused, pull = jax.vjp(query_path, queries_raw, g_query)
    d_queries_raw, d_gquery = pull(d_queries)
    d_qkv = jnp.concatenate(
        [d_queries_raw.reshape(TOK, HEADS * HD), d_keys_raw, d_local[1]], axis=1
    ).astype(BF)
    d_normed_in = dot(d_qkv, w_qkv, 1, 0)
    unused, pull = jax.vjp(rms_norm, activ, g_apre)
    d_in_part, d_gapre = pull(d_normed_in)
    input_grad = (d_residual + d_in_part)[None]

    t_att = jnp.concatenate(
        [dot(d_qkv, normed_in, 0, 0).astype(BF), dot(attended, d_proj_low, 0, 0).astype(BF)]
    )
    t_att = sum_group(t_att.reshape(ATT, GROUP, SLICE, D), 9).astype(BF)
    by_tile = jnp.concatenate(
        [
            t_att,
            t_gate.reshape(FFT, SLICE, D),
            t_up.reshape(FFT, SLICE, D),
            t_down.reshape(FFT, SLICE, D),
        ]
    )
    match = owners[None, :] == jnp.arange(128, dtype=jnp.int32)[:, None]
    tile_of = jnp.sum(jnp.where(match, jnp.arange(owners.shape[0], dtype=jnp.int32)[None, :], 0), axis=1)
    by_slot = jnp.take(by_tile, tile_of, axis=0).reshape(4, 4, 2, 4, SLICE, D)
    gain_local = jnp.concatenate([d_gapre, d_gapost, d_gfpre, d_gfpost, d_gquery, d_gkey])
    grad, gain_grads = sum_slices(by_slot, gain_local.reshape(40, 128), 10)
    grad = grad.reshape(HD, D)
    gain_grads = gain_grads.reshape(-1)

    owned = jnp.any(owners == my_slot)
    left = left_basis[0].astype(BF)
    right = right_basis[0].astype(BF)
    rotated = dot(left, grad, 0, 1)
    rotated = dot(rotated.astype(BF), right, 1, 0)
    first_new = BETA_ONE * first_old[0] + (1.0 - BETA_ONE) * rotated
    second_new = BETA_TWO * second_old[0] + (1.0 - BETA_TWO) * rotated * rotated
    normed_step = (
        first_new
        / (1.0 - BETA_ONE**STEP)
        / (jnp.sqrt(second_new / (1.0 - BETA_TWO**STEP)) + ADAM_EPS)
    )
    back = dot(normed_step.astype(BF), right, 1, 1)
    back = dot(left, back.astype(BF), 1, 0)
    weight_new = masters[0] - RATE * (back + DECAY * masters[0])
    new_masters = jnp.where(owned, weight_new, masters[0])[None]
    new_first = jnp.where(owned, first_new, first_old[0])[None]
    new_second = jnp.where(owned, second_new, second_old[0])[None]
    new_gain_first = BETA_ONE * gain_first + (1.0 - BETA_ONE) * gain_grads
    new_gain_second = BETA_TWO * gain_second + (1.0 - BETA_TWO) * gain_grads * gain_grads
    gain_step = (
        new_gain_first
        / (1.0 - BETA_ONE**STEP)
        / (jnp.sqrt(new_gain_second / (1.0 - BETA_TWO**STEP)) + ADAM_EPS)
    )
    new_gains = gains - GAIN_RATE * gain_step
    return (
        layer_out,
        input_grad,
        new_masters,
        new_first,
        new_second,
        new_gains,
        new_gain_first,
        new_gain_second,
    )


def solution(mesh):
    wide = Mesh(mesh.devices.reshape(4, 4, 2, 2, 2), AXES)
    tokens = P("xl", ("y", "z", "xh", "core"), None)
    held = P(AXES, None, None)
    return jax.shard_map(
        local,
        mesh=wide,
        in_specs=(tokens, tokens, P("xl", None), P(), held, held, held, held, held, P(), P(), P()),
        out_specs=(tokens, tokens, held, held, held, P(), P(), P()),
        check_vma=False,
    )
```

time: 3210 us -> 571 us (0.18)
  waiting for transfers between devices: 2760 us -> 0 us
  Pallas kernels: 0 us -> 357 us
  matrix products: 197 us -> 74.7 us
  blocking collectives: 79 us -> 0 us
    reduce_scatter x1 -> x0, waiting for transfers between devices: 2340 us -> none  [local(): lax.psum_scatter(jnp.where(present[:, None, None], jnp.einsum('std,tsc->s...]
    all_gather x1 -> x0, waiting for transfers between devices: 418 us -> none  [local(): gathered = lax.all_gather(low_masters, ('seq', 'rep'), axis=0, tiled=True)]
    pallas_call x0 -> x10, Pallas kernels: none -> 357 us  [the longest x1 86.5 us: sum_slices(): pl.pallas_call(grads_body, out_shape=(jax.ShapeDtypeStruct((GROUP, SLICE,...]
    dot_general x24 -> x23, matrix products: 195 us -> 74.7 us  [the longest x17 55.6 us: dot(): lax.dot_general(a, b, (((da,), (db,)), ((), ())), preferred_element_type=...]
    psum x1 -> x0, blocking collectives: 79 us -> none  [local(): gain_grads = lax.psum(gain_local, ('seq', 'rep'))]
    gather x3, local copies, waits for them, and re-layouts: 59.8 us -> 25 us  [the longest x1 10.6 us: local(): w_ffn = jnp.take(slots, owners[ATT:], axis=0).reshape(3, FFT * SLICE, D)]
  transfers between devices with their start and end apart: 10 -> 0, of which waited for: 2 -> 0; matrix products, arithmetic and copies ran while one was open for 1% -> 0% of each run, Pallas kernels for 0% -> 0%
where the time goes in v1:
time: 571 us; the launch traced here: 564 us
  Pallas kernels  357 us (63%)
  matrix products  74.7 us (13%)
  local copies, waits for them, and re-layouts  66.5 us (12%)
  other arithmetic  63.6 us (11%)
    pallas_call x1, Pallas kernels, sum_slices(): pl.pallas_call(grads_body, out_shape=(jax.ShapeDtypeStruct((GROUP, SLICE,...  86.5 us
    pallas_call x3, Pallas kernels, sum_group(): pl.pallas_call(sum_body, out_shape=jax.ShapeDtypeStruct(blk, F32), in_spe...  83.2 us
    pallas_call x1, Pallas kernels, gather_slices(): pl.pallas_call(weights_body, out_shape=jax.ShapeDtypeStruct((4, 4, 2, 4,...  83.1 us
    pallas_call x3, Pallas kernels, gather_group(): pl.pallas_call(gather_body, out_shape=jax.ShapeDtypeStruct((n, GROUP, r,...  81.1 us
    dot_general x17, matrix products, dot(): lax.dot_general(a, b, (((da,), (db,)), ((), ())), preferred_element_type=...  55.6 us
    pallas_call x1, Pallas kernels, send_ahead(): pl.pallas_call(ahead_body, out_shape=jax.ShapeDtypeStruct((5,) + kv.shape...  12.3 us
    unnamed x189, local copies, waits for them, and re-layouts  11.6 us

profile of v1, /device:TPU:1, one launch (start us, length us, event | category | flops | bytes accessed | tf_op | source)
XLA Modules:
  0.0 563.7 jit_solution(11830218256345164343)
XLA Ops:
  4.5 83.1 %shard_map.179 = bf16[4,4,2,4,32,1152]{5,4,3,2,1,0:T(8,128)(2,1)} custom-call(bf16[8,32,1152]{2,1,0:T(8,128)(2,1)} %bitcast.280), custom_call_target="tpu_custom_call" | custom-call | tf_op jit(solution)/shard_map/pallas_call | solution.py:241
  87.6 4.3 gather_fusion
  93.0 40.6 %shard_map.180 = bf16[10,8,32,1152]{3,2,1,0:T(8,128)(2,1)} custom-call(bf16[10,32,1152]{2,1,0:T(8,128)(2,1)} %broadcast_select_fusion.2.x_ref), custom_call_target="tpu_custom_call" | custom-call | tf_op jit(solution)/shard_map/pallas_call | solution.py:111
  133.6 2.4 slice.88
  140.8 1.9 multiply_cosine_fusion
  142.7 1.9 slice.118
  144.6 2.1 reshape.503
  146.6 1.9 multiply_reduce_fusion.7
  155.0 12.3 %shard_map.181 = bf16[5,2,128,256]{3,2,1,0:T(8,128)(2,1)} custom-call(bf16[2,128,256]{2,1,0:T(8,128)(2,1)} %pad_maximum_fusion.9.x_ref), custom_call_target="tpu_custom_call" | custom-call | tf_op jit(solution)/shard_map/pallas_call | solution.py:420
  167.3 2.0 fusion.169
  177.8 1.9 slice.100
  182.8 20.8 %shard_map.182 = bf16[1,8,128,1152]{3,2,1,0:T(8,128)(2,1)} custom-call(bf16[1,128,1152]{2,1,0:T(8,128)(2,1)} %fusion.88.x_ref), custom_call_target="tpu_custom_call" | custom-call | tf_op jit(solution)/shard_map/pallas_call | solution.py:111
  204.8 10.6 %gather_fusion.1 = bf16[81,32,1152]{2,1,0:T(8,128)(2,1)} fusion(bf16[128,32,1152]{2,1,0:T(8,128)(2,1)} %bitcast.270, s32[1024]{0:T(1024)} %pad_clamp_fusion.1), kind=kCustom, calls=%fused_computation.1 | custom fusion | bytes 11944260 | tf_op jit(solution)/shard_map/jit(_take)/gather | solution.py:514
  215.4 3.4 broadcast_select_fusion.1
  221.0 2.5 fusion.172
  223.5 4.7 multiply_convert_fusion.1
  228.2 4.3 convolution_convert_fusion.2
  232.6 20.8 %shard_map.183 = f32[1,128,1152]{2,1,0:T(8,128)} custom-call(bf16[1,2,2,2,128,1152]{5,4,3,2,1,0:T(8,128)(2,1)} %bitcast.288), custom_call_target="tpu_custom_call" | custom-call | tf_op jit(solution)/shard_map/pallas_call | solution.py:164
  254.7 2.6 fusion.66
  258.2 19.7 %shard_map.184 = bf16[1,8,128,1152]{3,2,1,0:T(8,128)(2,1)} custom-call(bf16[1,128,1152]{2,1,0:T(8,128)(2,1)} %fusion.68.x_ref), custom_call_target="tpu_custom_call" | custom-call | tf_op jit(solution)/shard_map/pallas_call | solution.py:111
  277.9 9.1 %multiply_convert_fusion = (bf16[1024,864]{0,1:T(8,128)(2,1)S(1)}, bf16[1024,864]{0,1:T(8,128)(2,1)S(1)}) fusion(f32[1024,864]{0,1:T(8,128)} %copy-done.85, f32[1024,864]{0,1:T(8,128)} %get-tuple-element.67, bf16[1024,1152]{1,0:T(8,128)(2,1)} %bitcast.285, bf16[864,1152]{1,0:T(8,128)(2,1)} %bitcast.299), kind=kOutput, calls=%fused_computation.21 | convolution fusion | flops 2059665408 | bytes 14966784 | tf_op jit(solution)/shard_map/dot_general | solution.py:485
  287.1 2.9 fusion.173
  290.1 4.4 add_convert_fusion
  294.5 19.9 %shard_map.185 = f32[1,128,1152]{2,1,0:T(8,128)} custom-call(bf16[1,2,2,2,128,1152]{5,4,3,2,1,0:T(8,128)(2,1)} %bitcast.287), custom_call_target="tpu_custom_call" | custom-call | tf_op jit(solution)/shard_map/pallas_call | solution.py:164
  314.5 1.8 fusion.73
  316.3 2.2 multiply_reduce_fusion.1
  322.6 6.4 %fusion.37 = f32[128,4,256]{2,0,1:T(8,128)} fusion(bf16[640,256,1]{1,0,2:T(8,128)(2,1)} %bitcast.308, f32[128,4,640]{2,0,1:T(8,128)} %fusion.101, f32[128,4,640]{2,0,1:T(8,128)} %copy-done.13, f32[128,4]{0,1:T(4,128)} %copy-done.57, f32[128,4]{0,1:T(4,128)} %copy-done.56, pred[128,640]{1,0:T(8,128)(4,1)} %copy-done.33), kind=kOutput, calls=%fused_computation.60 | convolution fusion | flops 171377792 | bytes 3559424 | tf_op jit(solution)/shard_map/thk,kc->thc/dot_general | solution.py:591
  330.3 1.8 multiply_reduce_fusion.6
  333.0 1.8 copy.99
  334.8 6.7 %fusion.34 = f32[640,256,1]{1,0,2:T(8,128)} fusion(f32[128,4,640]{2,0,1:T(8,128)} %fusion.101, bf16[128,4,128]{2,0,1:T(8,128)(2,1)} %get-tuple-element.44, bf16[128,4,128]{2,0,1:T(8,128)(2,1)} %get-tuple-element.43, f32[128,4,640]{2,0,1:T(8,128)} %copy-done.13, f32[128,4]{0,1:T(4,128)} %copy-done.57, f32[128,4]{0,1:T(4,128)} %copy-done.56, ...), kind=kOutput, calls=%fused_computation.59 | convolution fusion | flops 171902080 | bytes 3624960 | tf_op jit(solution)/shard_map/thk,thc->kc/dot_general | solution.py:592
  341.6 1.9 reshape.508
  344.3 2.5 fusion.28
  346.8 2.2 copy.101
  351.4 10.4 %shard_map.186 = bf16[4,2,128,256]{3,2,1,0:T(8,128)(2,1)} custom-call(bf16[4,2,128,256]{3,2,1,0:T(8,128)(2,1)} %fusion.44.x_ref), custom_call_target="tpu_custom_call" | custom-call | tf_op jit(solution)/shard_map/pallas_call | solution.py:446
  372.0 3.3 fusion.59
  379.3 2.3 convolution_convert_fusion
  382.4 3.0 pad_maximum_fusion.1
  385.4 42.4 %shard_map.187 = f32[10,32,1152]{2,1,0:T(8,128)} custom-call(bf16[10,2,2,2,32,1152]{5,4,3,2,1,0:T(8,128)(2,1)} %bitcast.271), custom_call_target="tpu_custom_call" | custom-call | tf_op jit(solution)/shard_map/pallas_call | solution.py:164
  429.7 2.5 convolution_convert_fusion.5
  432.2 2.5 convolution_convert_fusion.4
  434.7 2.5 convolution_convert_fusion.3
  437.2 3.6 pad_maximum_fusion
  440.9 10.1 %gather_fusion.2 = bf16[128,32,1152]{2,1,0:T(8,128)(2,1)} fusion(bf16[91,32,1152]{2,1,0:T(8,128)(2,1)} %pad_maximum_fusion, s32[1024]{0:T(1024)S(1)} %pad_clamp_fusion), kind=kCustom, calls=%fused_computation.2 | custom fusion | bytes 18874880 | tf_op jit(solution)/shard_map/jit(_take)/gather | solution.py:623
  451.1 8.4 %broadcast_select_fusion.d_ref = bf16[4,4,2,4,32,1152]{5,4,3,2,1,0:T(8,128)(2,1)} fusion(bf16[4,4,2,4,32,1152]{5,4,3,2,1,0:T(8,128)(2,1)} %bitcast.266, pred[4,4,2,4]{3,2,1,0:T(4,128)(4,1)S(1)} %compare_and_fusion), kind=kLoop, calls=%fused_computation.4 | loop fusion | flops 4718592 | bytes 18874496 | tf_op jit(solution)/shard_map/jit(_take)/select_n | solution.py:623
  459.5 86.5 %shard_map.188 = (bf16[8,32,1152]{2,1,0:T(8,128)(2,1)}, f32[40,128]{1,0:T(8,128)}) custom-call(bf16[4,4,2,4,32,1152]{5,4,3,2,1,0:T(8,128)(2,1)} %broadcast_select_fusion.d_ref, f32[40,128]{1,0:T(8,128)} %bitcast.309), custom_call_target="tpu_custom_call" | custom-call | tf_op jit(solution)/shard_map/pallas_call | solution.py:359
  546.1 4.0 fusion.30
  550.7 3.6 fusion.40
  554.4 7.1 %fusion.12 = f32[1,1152,256]{2,1,0:T(8,128)} fusion(f32[1,1152,1152]{2,1,0:T(8,128)} %param.19, f32[1,1152,256]{2,1,0:T(8,128)} %param.16, f32[1152,256]{1,0:T(8,128)S(1)} %fusion.30, f32[1,1152,256]{2,1,0:T(8,128)} %param.17, f32[1,1152,256]{2,1,0:T(8,128)} %param.18, pred[]{:T(512)} %compare_reduce_fusion, f32[1,256,256]{2,1,0:T(8,128)S(1)} %copy-done.34), kind=kOutput, calls=%fused_computation.32 | convolution fusion | flops 836878336 | bytes 11468801 | tf_op jit(solution)/shard_map/dot_general | solution.py:485
  (266 shorter events, 61.8 us)
Async XLA Ops:
  4.5 83.1 %copy-start.82 = (s32[91]{0:T(128)S(1)}, s32[91]{0:T(128)}, u32[]{:S(2)}) copy-start(s32[91]{0:T(128)} %param.15) | copy-start | bytes 1096
  149.9 4.4 copy-start.38
  149.9 4.4 copy-start.39
  169.3 5.5 copy-start.29
  181.2 22.5 %copy-start.83 = (s32[91]{0:T(128)S(1)}, s32[91]{0:T(128)}, u32[]{:S(2)}) copy-start(s32[91]{0:T(128)} %param.15) | copy-start | bytes 1096
  219.2 4.2 copy-start.26
  219.2 8.9 %copy-start.28 = (bf16[27,32,1152]{2,1,0:T(8,128)(2,1)}, bf16[27,32,1152]{2,1,0:T(8,128)(2,1)S(1)}, u32[]{:S(2)}) copy-start(bf16[27,32,1152]{2,1,0:T(8,128)(2,1)S(1)} %get-tuple-element.36) | copy-start | bytes 5971972
  223.5 4.7 copy-start.85
  228.2 4.4 copy-start.88
  232.5 22.2 %copy-start.3 = (f32[128,1152]{1,0:T(8,128)S(1)}, f32[128,1152]{1,0:T(8,128)}, u32[]{:S(2)}) copy-start(f32[128,1152]{1,0:T(8,128)} %copy-done.2) | copy-start | bytes 1769476
  232.6 22.2 %copy-start.15 = (bf16[1,128,1152]{2,1,0:T(8,128)(2,1)S(1)}, bf16[1,128,1152]{2,1,0:T(8,128)(2,1)}, u32[]{:S(2)}) copy-start(bf16[1,128,1152]{2,1,0:T(8,128)(2,1)} %param.13) | copy-start | bytes 884740
  232.6 22.2 %copy-start.40 = (f32[1152]{0:T(1024)S(1)}, f32[1152]{0:T(1024)}, u32[]{:S(2)}) copy-start(f32[1152]{0:T(1024)} %get-tuple-element.52) | copy-start | bytes 13828
  253.4 3.9 copy-start.8
  277.9 9.2 %copy-start.27 = (bf16[27,32,1152]{2,1,0:T(8,128)(2,1)S(1)}, bf16[27,32,1152]{2,1,0:T(8,128)(2,1)}, u32[]{:S(2)}) copy-start(bf16[27,32,1152]{2,1,0:T(8,128)(2,1)} %copy-done.26) | copy-start | bytes 5971972
  287.1 3.0 copy-start.86
  294.5 20.0 %copy-start.37 = (f32[1152]{0:T(1024)S(1)}, f32[1152]{0:T(1024)}, u32[]{:S(2)}) copy-start(f32[1152]{0:T(1024)} %get-tuple-element.53) | copy-start | bytes 13828
  294.5 20.0 %copy-start.65 = (f32[128]{0:T(128)S(1)}, f32[128]{0:T(128)}, u32[]{:S(2)}) copy-start(f32[128]{0:T(128)} %copy-done.64) | copy-start | bytes 1540
  294.5 21.8 %copy-start.74 = (f32[128]{0:T(128)S(1)}, f32[128]{0:T(128)}, u32[]{:S(2)}) copy-start(f32[128]{0:T(128)} %copy-done.73) | copy-start | bytes 1540
  294.5 21.8 %copy-start.10 = (f32[128,1152]{1,0:T(8,128)S(1)}, f32[128,1152]{1,0:T(8,128)}, u32[]{:S(2)}) copy-start(f32[128,1152]{1,0:T(8,128)} %copy-done.9) | copy-start | bytes 1769476
  294.5 21.8 %copy-start.61 = (f32[128]{0:T(128)S(1)}, f32[128]{0:T(128)}, u32[]{:S(2)}) copy-start(f32[128]{0:T(128)} %copy-done.60) | copy-start | bytes 1540
  314.4 4.1 copy-start.80
  316.3 3.2 copy-start.1
  322.6 7.6 %copy-start.46 = (f32[128,4]{0,1:T(4,128)S(1)}, f32[128,4]{0,1:T(4,128)}, u32[]{:S(2)}) copy-start(f32[128,4]{0,1:T(4,128)} %copy-done.45) | copy-start | bytes 6148
  322.6 7.6 %copy-start.55 = (f32[256]{0:T(256)S(1)}, f32[256]{0:T(256)}, u32[]{:S(2)}) copy-start(f32[256]{0:T(256)} %get-tuple-element.56) | copy-start | bytes 3076
  329.1 3.0 copy-start.52
  329.1 3.0 copy-start.4
  334.8 8.6 %copy-start.42 = (s32[640]{0:T(1024)S(1)}, s32[640]{0:T(1024)}, u32[]{:S(2)}) copy-start(s32[640]{0:T(1024)} %copy-done.41) | copy-start | bytes 7684
  334.8 8.6 %copy-start.44 = (s32[640]{0:T(1024)S(1)}, s32[640]{0:T(1024)}, u32[]{:S(2)}) copy-start(s32[640]{0:T(1024)} %copy-done.43) | copy-start | bytes 7684
  351.4 12.3 %copy-start.68 = (f32[128]{0:T(128)S(1)}, f32[128]{0:T(128)}, u32[]{:S(2)}) copy-start(f32[128]{0:T(128)} %copy-done.67) | copy-start | bytes 1540
  351.4 12.3 %copy-start.70 = (f32[128]{0:T(128)S(1)}, f32[128]{0:T(128)}, u32[]{:S(2)}) copy-start(f32[128]{0:T(128)} %copy-done.69) | copy-start | bytes 1540
  351.4 12.7 %copy-start.54 = (f32[256]{0:T(256)S(1)}, f32[256]{0:T(256)}, u32[]{:S(2)}) copy-start(f32[256]{0:T(256)} %copy-done.53) | copy-start | bytes 3076
  351.4 12.7 %copy-start.63 = (f32[128]{0:T(128)S(1)}, f32[128]{0:T(128)}, u32[]{:S(2)}) copy-start(f32[128]{0:T(128)} %copy-done.62) | copy-start | bytes 1540
  351.4 14.3 %copy-start.78 = (f32[128]{0:T(128)S(1)}, f32[128]{0:T(128)}, u32[]{:S(2)}) copy-start(f32[128]{0:T(128)} %copy-done.77) | copy-start | bytes 1540
  372.0 5.4 copy-start.47
  385.4 44.0 %copy-start.20 = (bf16[1,8,128,1152]{3,2,1,0:T(8,128)(2,1)S(1)}, bf16[1,8,128,1152]{3,2,1,0:T(8,128)(2,1)}, u32[]{:S(2)}) copy-start(bf16[1,8,128,1152]{3,2,1,0:T(8,128)(2,1)} %shard_map.182) | copy-start | bytes 7077892
  437.2 3.6 copy-start.84
  459.5 86.5 %copy-start.34 = (f32[1,256,256]{2,1,0:T(8,128)S(1)}, f32[1,256,256]{2,1,0:T(8,128)}, u32[]{:S(2)}) copy-start(f32[1,256,256]{2,1,0:T(8,128)} %param.20) | copy-start | bytes 786436
  546.0 4.7 copy-start.31
  554.3 7.2 %copy-start.35 = (f32[5120]{0:T(1024)S(1)}, f32[5120]{0:T(1024)}, u32[]{:S(2)}) copy-start(f32[5120]{0:T(1024)} %param.21) | copy-start | bytes 61444
  554.3 7.2 %copy-start.49 = (f32[5120]{0:T(1024)S(1)}, f32[5120]{0:T(1024)}, u32[]{:S(2)}) copy-start(f32[5120]{0:T(1024)} %param.22) | copy-start | bytes 61444
  554.3 7.2 %copy-start.50 = (f32[5120]{0:T(1024)S(1)}, f32[5120]{0:T(1024)}, u32[]{:S(2)}) copy-start(f32[5120]{0:T(1024)} %param.23) | copy-start | bytes 61444
  554.3 7.2 %copy-start.51 = (f32[40,128]{1,0:T(8,128)S(1)}, f32[40,128]{1,0:T(8,128)}, u32[]{:S(2)}) copy-start(f32[40,128]{1,0:T(8,128)} %get-tuple-element.11) | copy-start | bytes 61444
  554.4 7.8 %copy-start.76 = (f32[128]{0:T(128)S(1)}, f32[128]{0:T(128)}, u32[]{:S(2)}) copy-start(f32[128]{0:T(128)} %copy-done.75) | copy-start | bytes 1540
  554.4 7.8 %copy-start.81 = (f32[128]{0:T(128)S(1)}, f32[128]{0:T(128)}, u32[]{:S(2)}) copy-start(f32[128]{0:T(128)} %get-tuple-element.23) | copy-start | bytes 1540
  554.4 7.8 %copy-start.7 = (bf16[1,128,1152]{2,1,0:T(8,128)(2,1)S(1)}, bf16[1,128,1152]{2,1,0:T(8,128)(2,1)}, u32[]{:S(2)}) copy-start(bf16[1,128,1152]{2,1,0:T(8,128)(2,1)} %param.12) | copy-start | bytes 884740
  554.4 7.8 %copy-start.12 = (f32[128,1152]{1,0:T(8,128)S(1)}, f32[128,1152]{1,0:T(8,128)}, u32[]{:S(2)}) copy-start(f32[128,1152]{1,0:T(8,128)} %copy-done.11) | copy-start | bytes 1769476
  554.4 7.8 %copy-start.22 = (f32[128,1152]{1,0:T(8,128)S(1)}, f32[128,1152]{1,0:T(8,128)}, u32[]{:S(2)}) copy-start(f32[128,1152]{1,0:T(8,128)} %get-tuple-element.68) | copy-start | bytes 1769476
  554.4 7.8 %copy-start.59 = (f32[128]{0:T(128)S(1)}, f32[128]{0:T(128)}, u32[]{:S(2)}) copy-start(f32[128]{0:T(128)} %copy-done.58) | copy-start | bytes 1540
  (44 other events, 64.0 us)

commit v2 on v1

--- a/solution.py
+++ b/solution.py
@@ -32,7 +32,7 @@
 
 MESH = pl.DeviceIdType.MESH
 AXES = ("y", "z", "xh", "core", "xl")
-VMEM_LIMIT = 56 * 1024 * 1024
+VMEM_LIMIT = 63 * 1024 * 1024
 BF = jnp.bfloat16
 F32 = jnp.float32
 
@@ -195,10 +195,10 @@
     mine = o_ref.at[y, z, me // 4, lax.rem(me, 4)]
     spread = []
     for i, f in enumerate(friends):
-        step = remote(t_ref.at[member(*f)], mine, gs.at[i], gr.at[i], place(y, z, *f))
+        step = remote(t_ref.at[f[0] * 2 + f[1]], mine, gs.at[i], gr.at[i], place(y, z, *f))
         step.start()
         spread.append(step)
-    own = pltpu.make_async_copy(t_ref.at[me], mine, own_sem)
+    own = pltpu.make_async_copy(t_ref.at[x * 2 + c], mine, own_sem)
     own.start()
     own.wait()
     for step in spread:
@@ -343,10 +343,10 @@
         lax.fori_loop(0, 4, add, 0)
     spread = []
     for i, f in enumerate(friends):
-        step = remote(fin.at[member(*f)], o_ref.at[me], gs.at[i], gr.at[i], place(y, z, *f))
+        step = remote(fin.at[member(*f)], o_ref.at[x * 2 + c], gs.at[i], gr.at[i], place(y, z, *f))
         step.start()
         spread.append(step)
-    last = pltpu.make_async_copy(fin.at[me], o_ref.at[me], own_sem.at[2])
+    last = pltpu.make_async_copy(fin.at[me], o_ref.at[x * 2 + c], own_sem.at[2])
     last.start()
     last.wait()
     for step in spread:
@@ -453,6 +453,364 @@
     )(pieces)
 
 
+def norm_of(v, g):
+    return v * lax.rsqrt(jnp.mean(v * v, axis=-1, keepdims=True) + NORM_EPS) * g
+
+
+def norm_back(v, g, w):
+    r = lax.rsqrt(jnp.mean(v * v, axis=-1, keepdims=True) + NORM_EPS)
+    u = w * g
+    dg = jnp.sum(w * (v * r), axis=0, keepdims=True)
+    dv = r * u - v * (r * r * r * jnp.mean(u * v, axis=-1, keepdims=True))
+    return dv, dg
+
+
+def rope_norm(v, g, cos, sin):
+    n = v * lax.rsqrt(jnp.mean(v * v, axis=0, keepdims=True) + NORM_EPS) * g
+    a, b = n[: HD // 2], n[HD // 2 :]
+    return jnp.concatenate([a * cos - b * sin, b * cos + a * sin], axis=0)
+
+
+def gelu_parts(g):
+    k, a = 0.7978845608028654, 0.044715
+    sq = g * g
+    th = jnp.tanh(k * g * (1.0 + a * sq))
+    half = 0.5 * (1.0 + th)
+    slope = half + 0.5 * g * (1.0 - th * th) * (k * (1.0 + 3.0 * a * sq))
+    return g * half, slope
+
+
+def nn(a, b):
+    return jnp.dot(a, b, preferred_element_type=F32)
+
+
+def nt(a, b):
+    return lax.dot_general(a, b, (((1,), (1,)), ((), ())), preferred_element_type=F32)
+
+
+ORDER = (0, 3, 1, 2)
+
+
+def layer_body(
+    doc_ref, own_ref, wall_ref, xa_ref, x_ref, y_ref, g4_ref, gqk_ref, cos_ref, sin_ref,
+    lo_ref, dr1_ref, dap_ref, gg_ref, raw_ref, qt_ref, k_ref, vt_ref, pt_ref, wo_ref, osl_ref, tg_ref,
+    wall, wg, wu, wd, xa, sq, xf, dd, gb, ub, hb, dgb, dub, pbuf, sbuf, near, far, ptl, oto, dgt,
+    load_sem, as_, ar, wxs, wxr, wcs, wcr, hs, hr, os_, or_, fxs, fxr, fcs, fcr, bxs, bxr, bcs, bcr,
+    ss, sr, rs_, rr, out_sem,
+):
+    y, z, x, c = here()
+    me = x * 2 + c
+    twin = place(y, z, x, 1 - c)
+    s = seq_index()
+    chips = {d: turn(x, d) for d in range(4)}
+    peers = {d: place(y, z, chips[d], c) for d in (1, 2, 3)}
+    others = [(d, cc) for d in (1, 2, 3) for cc in range(2)]
+    greet(
+        [place(y, z, chips[d], cc) for d, cc in others]
+        + [twin]
+        + [seq_place(lax.rem(s + 64 + d, 64)) for d in (-4, -3, -2, -1, 1, 2, 3, 4)]
+    )
+    load_w = pltpu.make_async_copy(wall_ref, wall, load_sem.at[0])
+    load_x = pltpu.make_async_copy(xa_ref, xa, load_sem.at[1])
+    load_w.start()
+    load_x.start()
+    load_w.wait()
+
+    for h in range(HEADS):
+        wo_ref[h, me] = wall[own_ref[HEADS + 2 + h]]
+    w_far = {}
+    w_near = {}
+    mine = wo_ref.at[:, me]
+    for d in (1, 3, 2):
+        w_far[d] = remote(mine, mine, wxs.at[d - 1], wxr.at[d - 1], peers[d])
+    w_near[0] = remote(mine, mine, wcs.at[0], wcr.at[0], twin)
+
+    watt = [wall[own_ref[t]] for t in range(HEADS + 2)]
+    watt = jnp.concatenate(watt, axis=0)
+    load_x.wait()
+    qkv = []
+    for d in (2, 1, 3, 0):
+        part = nt(watt, xa[chips[d]].reshape(2 * TOK, D)).astype(BF)
+        for cc in range(2):
+            sq[d, cc] = part[:, cc * TOK : (cc + 1) * TOK].reshape(HEADS + 2, SLICE, TOK)
+        if d:
+            for cc in range(2):
+                step = remote(
+                    sq.at[d, cc], raw_ref.at[:, me], as_.at[d, cc], ar.at[d, c], place(y, z, chips[d], cc)
+                )
+                step.start()
+                qkv.append(step)
+    step = remote(sq.at[0, 1 - c], raw_ref.at[:, me], as_.at[0, 0], ar.at[0, c], twin)
+    step.start()
+    qkv.append(step)
+    raw_ref[:, me] = sq[0, c]
+    for d in (1, 3, 2):
+        w_far[d].start()
+    w_near[0].start()
+
+    def pack(t, carry):
+        rows = pl.ds(pl.multiple_of(t * SLICE, SLICE), SLICE)
+        wg[rows] = wall[own_ref[ATT + t]]
+        wu[rows] = wall[own_ref[ATT + FFT + t]]
+        wd[rows] = wall[own_ref[ATT + 2 * FFT + t]]
+        return carry
+
+    lax.fori_loop(0, FFT, pack, 0)
+    for d in (1, 2, 3):
+        for cc in range(2):
+            remote(sq.at[d, cc], raw_ref.at[:, me], as_.at[d, cc], ar.at[d, cc], twin).wait_recv()
+    remote(sq.at[0, 0], raw_ref.at[:, me], as_.at[0, 0], ar.at[0, 1 - c], twin).wait_recv()
+
+    cos, sin = cos_ref[...], sin_ref[...]
+    kt = rope_norm(
+        raw_ref[HEADS].reshape(HD, TOK).astype(F32), gqk_ref[:, 1:2], cos, sin
+    )
+    k_ref[4] = kt.T.astype(BF)
+    vt_ref[:, 4 * TOK :] = raw_ref[HEADS + 1].reshape(HD, TOK)
+    halo = []
+    for d in (4, 3, 2, 1):
+        to = seq_place(lax.rem(s + d, 64))
+        a = remote(k_ref.at[4], k_ref.at[4 - d], hs.at[0, d - 1], hr.at[0, d - 1], to)
+        b = remote(
+            vt_ref.at[:, 4 * TOK :], vt_ref.at[:, (4 - d) * TOK : (5 - d) * TOK], hs.at[1, d - 1], hr.at[1, d - 1], to
+        )
+        a.start()
+        b.start()
+        halo.extend([a, b])
+    for h in range(HEADS):
+        q = rope_norm(raw_ref[h].reshape(HD, TOK).astype(F32), gqk_ref[:, 0:1], cos, sin)
+        qt_ref[:, h * TOK : (h + 1) * TOK] = q.astype(BF)
+    row = lax.broadcasted_iota(jnp.int32, (WINDOW + TOK, TOK), 0)
+    col = lax.broadcasted_iota(jnp.int32, (WINDOW + TOK, TOK), 1)
+    seen = (row <= col + WINDOW) & (row > col) & (row >= WINDOW - s * TOK)
+    half = lax.broadcasted_iota(jnp.int32, (BLK, TOK), 1) < BLK
+    q_doc = jnp.where(half, doc_ref[0, 2 * s], doc_ref[0, 2 * s + 1])
+    k_doc = jnp.concatenate(
+        [
+            jnp.full((BLK, TOK), doc_ref[0, jnp.maximum(2 * s - 8 + b, 0)], jnp.int32)
+            for b in range(10)
+        ],
+        axis=0,
+    )
+    seen = seen & (k_doc == jnp.concatenate([q_doc] * 10, axis=0))
+    for step in halo:
+        step.wait_recv()
+    keys = k_ref[...].reshape(WINDOW + TOK, HD)
+    for h in range(HEADS):
+        lanes = slice(h * TOK, (h + 1) * TOK)
+        sc = nn(keys, qt_ref[:, lanes]) * (HD**-0.5)
+        sc = jnp.where(seen, sc, -1e30)
+        ex = jnp.exp(sc - jnp.max(sc, axis=0, keepdims=True))
+        pr = ex / jnp.sum(ex, axis=0, keepdims=True)
+        pt_ref[:, lanes] = pr
+        ptl[:, lanes] = pr.astype(BF)
+    ot = nn(vt_ref[...], ptl[...])
+    oto[...] = ot.astype(BF)
+    o_steps = []
+    for d, cc in others:
+        to = chips[d] * 2 + cc
+        rows = pl.ds(pl.multiple_of(to * SLICE, SLICE), SLICE)
+        step = remote(
+            oto.at[rows], osl_ref.at[me], os_.at[d, cc], or_.at[d, c], place(y, z, chips[d], cc)
+        )
+        step.start()
+        o_steps.append(step)
+    rows = pl.ds(pl.multiple_of((x * 2 + 1 - c) * SLICE, SLICE), SLICE)
+    step = remote(oto.at[rows], osl_ref.at[me], os_.at[0, 0], or_.at[0, c], twin)
+    step.start()
+    o_steps.append(step)
+    osl_ref[me] = oto[pl.ds(pl.multiple_of(me * SLICE, SLICE), SLICE)]
+
+    for d in (1, 3, 2):
+        w_far[d].wait_recv()
+        src = wo_ref.at[:, chips[4 - d] * 2 + c]
+        w_near[d] = remote(src, src, wcs.at[d], wcr.at[d], twin)
+        w_near[d].start()
+    for step in w_near.values():
+        step.wait()
+    ap = jnp.zeros((TOK, D), F32)
+    for h in range(HEADS):
+        o = ot[:, h * TOK : (h + 1) * TOK].T.astype(BF)
+        ap = ap + nn(o, wo_ref[h].reshape(HD, D))
+    act = x_ref[...].astype(F32)
+    r1 = act + norm_of(ap, g4_ref[1:2])
+    xf[x, c] = norm_of(r1, g4_ref[2:3]).astype(BF)
+
+    def gather_start(buf, xs, xr, cs, cr):
+        own = buf.at[x, c]
+        sends = {d: remote(own, own, xs.at[d - 1], xr.at[d - 1], peers[d]) for d in (1, 3, 2)}
+        near_ = {0: remote(own, own, cs.at[0], cr.at[0], twin)}
+        near_[0].start()
+        for d in (1, 3, 2):
+            sends[d].start()
+        return sends, near_
+
+    def gather_wait(buf, e, sends, near_, cs, cr):
+        if e:
+            d = 4 - e
+            sends[d].wait_recv()
+            src = buf.at[chips[e], c]
+            near_[d] = remote(src, src, cs.at[d], cr.at[d], twin)
+            near_[d].start()
+            near_[d].wait_recv()
+        else:
+            near_[0].wait_recv()
+
+    def gather_end(sends, near_):
+        for step in list(sends.values()) + list(near_.values()):
+            step.wait_send()
+
+    def sum_swap(ph, e):
+        step = remote(pbuf.at[e, 1 - c], near.at[ph, e], ss.at[ph, e], sr.at[ph, e], twin)
+        step.start()
+        return step
+
+    def sum_send(ph, e, swap):
+        swap.wait_recv()
+        both = pbuf[e, c].astype(F32) + near[ph, e].astype(F32)
+        if not e:
+            return None, both
+        sbuf[e - 1] = both.astype(BF)
+        step = remote(sbuf.at[e - 1], far.at[ph, e - 1], rs_.at[ph, e - 1], rr.at[ph, e - 1], peers[e])
+        step.start()
+        return step, None
+
+    def pipeline(ph, buf, xs, xr, cs, cr, block):
+        sends, near_ = gather_start(buf, xs, xr, cs, cr)
+        swaps, outs = {}, []
+        for n, e in enumerate(ORDER):
+            gather_wait(buf, e, sends, near_, cs, cr)
+            pbuf[e] = block(e).astype(BF).reshape(2, TOK, D)
+            swaps[e] = sum_swap(ph, e)
+            if n >= 2:
+                outs.append(sum_send(ph, ORDER[n - 1], swaps[ORDER[n - 1]])[0])
+        outs.append(sum_send(ph, ORDER[3], swaps[ORDER[3]])[0])
+        return sends, near_, swaps, outs
+
+    def finish(ph, sends, near_, swaps, outs):
+        _, total = sum_send(ph, 0, swaps[0])
+        for step in outs:
+            step.wait_recv()
+        total = ((total + far[ph, 0].astype(F32)) + far[ph, 1].astype(F32)) + far[ph, 2].astype(F32)
+        gather_end(sends, near_)
+        for step in list(swaps.values()) + outs:
+            step.wait_send()
+        return total
+
+    def forward(e):
+        v = xf[chips[e]].reshape(2 * TOK, D)
+        g = nt(v, wg[...])
+        u = nt(v, wu[...])
+        at = chips[e]
+        gb[at] = g
+        ub[at] = u
+        h, _ = gelu_parts(g)
+        hb[at] = (h * u).astype(BF)
+        return nn(hb[at], wd[...])
+
+    state = pipeline(0, xf, fxs, fxr, fcs, fcr, forward)
+    dn = finish(0, *state)
+    lo_ref[...] = (r1 + norm_of(dn, g4_ref[3:4])).astype(BF)
+    cot = y_ref[...].astype(F32)
+    ddn, d_fpost = norm_back(dn, g4_ref[3:4], cot)
+    dd[x, c] = ddn.astype(BF)
+
+    def backward(e):
+        v = dd[chips[e]].reshape(2 * TOK, D)
+        dh = nt(v, wd[...])
+        at = chips[e]
+        h, slope = gelu_parts(gb[at])
+        dgb[at] = (dh * ub[at] * slope).astype(BF)
+        dub[at] = (dh * h).astype(BF)
+        return nn(dgb[at], wg[...]) + nn(dub[at], wu[...])
+
+    state = pipeline(1, dd, bxs, bxr, bcs, bcr, backward)
+    for i, (lhs, rhs) in enumerate(((dgb, xf), (dub, xf), (hb, dd))):
+        for e in range(4):
+            dgt[:, e * 2 * TOK : (e + 1) * 2 * TOK] = lhs[e].T
+        for n in range(3):
+            cols = slice(n * 384, (n + 1) * 384)
+            g = nn(dgt[...], rhs[:, :, :, cols].reshape(GROUP * TOK, 384)).astype(BF)
+            wall[i * FFT : (i + 1) * FFT, :, cols] = g.reshape(FFT, SLICE, 384)
+    out = pltpu.make_async_copy(wall.at[0 : 3 * FFT], tg_ref, out_sem)
+    out.start()
+    dxf = finish(1, *state)
+    e1, d_fpre = norm_back(r1, g4_ref[2:3], dxf)
+    dr1 = cot + e1
+    dr1_ref[...] = dr1
+    dap, d_apost = norm_back(ap, g4_ref[1:2], dr1)
+    dap_ref[...] = dap.astype(BF)
+    gg_ref[0:1] = d_apost
+    gg_ref[1:2] = d_fpre
+    gg_ref[2:3] = d_fpost
+    for d in (1, 2, 3):
+        for cc in range(2):
+            remote(oto.at[0:SLICE], osl_ref.at[me], os_.at[d, cc], or_.at[d, cc], twin).wait_recv()
+    remote(oto.at[0:SLICE], osl_ref.at[me], os_.at[0, 0], or_.at[0, 1 - c], twin).wait_recv()
+    for step in qkv + halo + o_steps + list(w_far.values()):
+        step.wait_send()
+    out.wait()
+
+
+def run_layer(doc, owners, slots, xa, x, y, g4, gqk, cos, sin, cid):
+    f = jax.ShapeDtypeStruct
+    smem = pl.BlockSpec(memory_space=pltpu.SMEM)
+    vm = pltpu.VMEM
+    ffw = FFT * SLICE
+    outs = [
+        (f((TOK, D), BF), INV),
+        (f((TOK, D), F32), INV),
+        (f((TOK, D), BF), INV),
+        (f((3, D), F32), INV),
+        (f((HEADS + 2, GROUP, SLICE, TOK), BF), INV),
+        (f((HD, HEADS * TOK), BF), INV),
+        (f((5, TOK, HD), BF), INV),
+        (f((HD, WINDOW + TOK), BF), INV),
+        (f((WINDOW + TOK, HEADS * TOK), F32), INV),
+        (f((HEADS, GROUP, SLICE, D), BF), INV),
+        (f((GROUP, SLICE, HEADS * TOK), BF), INV),
+        (f((3 * FFT, SLICE, D), BF), ANY),
+    ]
+    return pl.pallas_call(
+        layer_body,
+        out_shape=tuple(o[0] for o in outs),
+        in_specs=[smem, smem, ANY, ANY, INV, INV, INV, INV, INV, INV],
+        out_specs=tuple(o[1] for o in outs),
+        scratch_shapes=[
+            vm((128, SLICE, D), BF),
+            vm((ffw, D), BF),
+            vm((ffw, D), BF),
+            vm((ffw, D), BF),
+            vm((4, 2, TOK, D), BF),
+            vm((4, 2, HEADS + 2, SLICE, TOK), BF),
+            vm((4, 2, TOK, D), BF),
+            vm((4, 2, TOK, D), BF),
+            vm((4, 2 * TOK, ffw), F32),
+            vm((4, 2 * TOK, ffw), F32),
+            vm((4, 2 * TOK, ffw), BF),
+            vm((4, 2 * TOK, ffw), BF),
+            vm((4, 2 * TOK, ffw), BF),
+            vm((4, 2, TOK, D), BF),
+            vm((3, TOK, D), BF),
+            vm((2, 4, TOK, D), BF),
+            vm((2, 3, TOK, D), BF),
+            vm((WINDOW + TOK, HEADS * TOK), BF),
+            vm((HD, HEADS * TOK), BF),
+            vm((ffw, GROUP * TOK), BF),
+            DMA((2,)),
+            DMA((4, 2)), DMA((4, 2)),
+            DMA((3,)), DMA((3,)), DMA((4,)), DMA((4,)),
+            DMA((2, 4)), DMA((2, 4)),
+            DMA((4, 2)), DMA((4, 2)),
+            DMA((3,)), DMA((3,)), DMA((4,)), DMA((4,)),
+            DMA((3,)), DMA((3,)), DMA((4,)), DMA((4,)),
+            DMA((2, 4)), DMA((2, 4)), DMA((2, 3)), DMA((2, 3)),
+            DMA,
+        ],
+        compiler_params=params(cid),
+    )(doc, owners, slots, xa, x, y, g4, gqk, cos, sin)
+
+
 def rms_norm(values, gain):
     return values * lax.rsqrt(jnp.mean(values * values, axis=-1, keepdims=True) + NORM_EPS) * gain
 
@@ -510,79 +868,39 @@
 
     tile = masters[0].T.astype(BF).reshape(GROUP, SLICE, D)
     slots = gather_slices(tile, 1).reshape(128, SLICE, D)
-    w_att = gather_group(jnp.take(slots, owners[:ATT], axis=0), 2).reshape(ATT, HD, D)
-    w_ffn = jnp.take(slots, owners[ATT:], axis=0).reshape(3, FFT * SLICE, D)
-    w_gate, w_up, w_down = w_ffn[0], w_ffn[1], w_ffn[2]
-    w_qkv = w_att[: HEADS + 2].reshape((HEADS + 2) * HD, D)
-    w_out = w_att[HEADS + 2 :].reshape(HEADS * HD, D)
-
     activ = inputs[0].astype(F32)
     local_pos = my_seq * TOK + jnp.arange(TOK, dtype=jnp.int32)
     normed_in = rms_norm(activ, g_apre).astype(BF)
-    raw = dot(normed_in, w_qkv, 1, 1)
-    queries_raw = raw[:, : HEADS * HD].reshape(TOK, HEADS, HD)
-    keys_raw = raw[:, HEADS * HD : HEADS * HD + HD]
-    values_raw = raw[:, HEADS * HD + HD :]
-
-    def query_path(values, gain):
-        return rotary(rms_norm(values, gain), local_pos)
-
-    queries_low = query_path(queries_raw, g_query).astype(BF)
-    keys_low = query_path(keys_raw, g_key).astype(BF)
-    values_low = values_raw.astype(BF)
-    pairs = send_ahead(jnp.stack([keys_low, values_low]), 3)
-    all_keys = pairs[:, 0].reshape(WINDOW + TOK, HD)
-    all_values = pairs[:, 1].reshape(WINDOW + TOK, HD)
-    key_pos = my_seq * TOK - WINDOW + jnp.arange(WINDOW + TOK, dtype=jnp.int32)
-    doc_table = doc_ids[0]
-    query_docs = doc_lookup(doc_table, local_pos)
-    key_docs = doc_lookup(doc_table, key_pos)
-    visible = (key_docs[None, :] == query_docs[:, None]) & (key_pos[None, :] <= local_pos[:, None])
-    visible = visible & (local_pos[:, None] - key_pos[None, :] < WINDOW) & (key_pos[None, :] >= 0)
-    score_scale = HD ** (-0.5)
-    scores = (
-        jnp.einsum("thc,kc->thk", queries_low, all_keys, preferred_element_type=F32) * score_scale
-    )
-    scores = jnp.where(visible[:, None, :], scores, -1e30)
-    row_top = jnp.max(scores, axis=-1, keepdims=True)
-    expo = jnp.exp(scores - row_top)
-    probs = expo / jnp.sum(expo, axis=-1, keepdims=True)
+    xa_all = gather_group(normed_in[None], 2)[0]
+    xa_all = xa_all.reshape(2, 2, 2, TOK, D).transpose(0, 2, 1, 3, 4).reshape(4, 2, TOK, D)
+    freq = jnp.exp(-jnp.log(THETA) * jnp.arange(HD // 2, dtype=F32) * 2.0 / HD)
+    angle = freq[:, None] * local_pos.astype(F32)[None, :]
+    g4 = jnp.stack([g_apre, g_apost, g_fpre, g_fpost])
+    gqk = jnp.stack([g_query, g_key], axis=1)
+    (layer_out, d_residual, d_proj_low, gg, raw, qt, k_all, vt, pt, wo, osl, t_ffn) = run_layer(
+        doc_ids, owners, slots, xa_all, inputs[0], out_grad[0], g4, gqk, jnp.cos(angle), jnp.sin(angle), 3
+    )
+    layer_out = layer_out[None]
+    w_att = gather_group(jnp.take(slots, owners[:ATT], axis=0), 12)
+    w_att = w_att.reshape(ATT, 2, 2, 2, SLICE, D).transpose(0, 1, 3, 2, 4, 5).reshape(ATT, HD, D)
+    w_qkv = w_att[: HEADS + 2].reshape((HEADS + 2) * HD, D)
+    w_out = wo.reshape(HEADS * HD, D)
+    raw = raw.reshape(6, HD, TOK).astype(F32)
+    queries_raw = raw[:HEADS].transpose(2, 0, 1)
+    keys_raw = raw[HEADS].T
+    queries_low = qt.reshape(HD, HEADS, TOK).transpose(2, 1, 0)
+    all_keys = k_all.reshape(WINDOW + TOK, HD)
+    all_values = vt.T
+    probs = pt.reshape(WINDOW + TOK, HEADS, TOK).transpose(2, 1, 0)
     probs_low = probs.astype(BF)
     attended = jnp.einsum("thk,kc->thc", probs_low, all_values, preferred_element_type=F32)
     attended = attended.astype(BF).reshape(TOK, HEADS * HD)
-    projected = dot(attended, w_out, 1, 0)
-    residual_one = activ + rms_norm(projected, g_apost)
-    normed_ffn = rms_norm(residual_one, g_fpre).astype(BF)
-
-    xf = gather_group(normed_ffn[None], 4).reshape(GROUP * TOK, D)
-    gate_pre = dot(xf, w_gate, 1, 1)
-    up_pre = dot(xf, w_up, 1, 1)
-    hidden = gate_product(gate_pre, up_pre).astype(BF)
-    down_part = dot(hidden, w_down, 1, 0).astype(BF)
-    down = sum_group(down_part.reshape(1, GROUP, TOK, D), 5)[0]
-    result = residual_one + rms_norm(down, g_fpost)
-    layer_out = result.astype(BF)[None]
-    cotangent = out_grad[0].astype(F32)
-    unused, pull = jax.vjp(rms_norm, down, g_fpost)
-    d_down, d_gfpost = pull(cotangent)
-    d_down_all = gather_group(d_down.astype(BF)[None], 6).reshape(GROUP * TOK, D)
-    d_hidden = dot(d_down_all, w_down, 1, 1)
-    unused, pull = jax.vjp(gate_product, gate_pre, up_pre)
-    d_gate, d_up = pull(d_hidden)
-    d_gate_low = d_gate.astype(BF)
-    d_up_low = d_up.astype(BF)
-    d_xf_part = (dot(d_gate_low, w_gate, 1, 0) + dot(d_up_low, w_up, 1, 0)).astype(BF)
-    d_normed_ffn = sum_group(d_xf_part.reshape(1, GROUP, TOK, D), 7)[0]
-    t_gate = dot(d_gate_low, xf, 0, 0).astype(BF)
-    t_up = dot(d_up_low, xf, 0, 0).astype(BF)
-    t_down = dot(hidden, d_down_all, 0, 0).astype(BF)
-
-    unused, pull = jax.vjp(rms_norm, residual_one, g_fpre)
-    d_res_part, d_gfpre = pull(d_normed_ffn)
-    d_residual = cotangent + d_res_part
-    unused, pull = jax.vjp(rms_norm, projected, g_apost)
-    d_projected, d_gapost = pull(d_residual)
-    d_proj_low = d_projected.astype(BF)
+    score_scale = HD ** (-0.5)
+
+    def query_path(values, gain):
+        return rotary(rms_norm(values, gain), local_pos)
+
+    d_gapost, d_gfpre, d_gfpost = gg[0], gg[1], gg[2]
     d_mixed = dot(d_proj_low, w_out, 1, 1).astype(BF)
     d_mixed_heads = d_mixed.reshape(TOK, HEADS, HD)
     d_probs = jnp.einsum("thc,kc->thk", d_mixed_heads, all_values, preferred_element_type=F32)
@@ -609,13 +927,12 @@
     t_att = jnp.concatenate(
         [dot(d_qkv, normed_in, 0, 0).astype(BF), dot(attended, d_proj_low, 0, 0).astype(BF)]
     )
+    t_att = t_att.reshape(ATT, 2, 2, 2, SLICE, D).transpose(0, 1, 3, 2, 4, 5)
     t_att = sum_group(t_att.reshape(ATT, GROUP, SLICE, D), 9).astype(BF)
     by_tile = jnp.concatenate(
         [
             t_att,
-            t_gate.reshape(FFT, SLICE, D),
-            t_up.reshape(FFT, SLICE, D),
-            t_down.reshape(FFT, SLICE, D),
+            t_ffn,
         ]
     )
     match = owners[None, :] == jnp.arange(128, dtype=jnp.int32)[:, None]

time: 571 us -> 519 us (0.909)
  Pallas kernels: 357 us -> 404 us
  matrix products: 74.7 us -> 29.1 us
  local copies, waits for them, and re-layouts: 66.5 us -> 40.7 us
  other arithmetic: 63.6 us -> 39.4 us
    pallas_call x1, Pallas kernels: 12.3 us -> 120 us  [run_layer(): pl.pallas_call(layer_body, out_shape=tuple((o[0] for o in outs)), in_spec...]
    pallas_call x3 -> x1, Pallas kernels: 83.2 us -> 40.4 us  [sum_group(): pl.pallas_call(sum_body, out_shape=jax.ShapeDtypeStruct(blk, F32), in_spe...]
    dot_general x17 -> x6, matrix products: 55.6 us -> 19.6 us  [dot(): lax.dot_general(a, b, (((da,), (db,)), ((), ())), preferred_element_type=...]
    pallas_call x3 -> x2, Pallas kernels: 81.1 us -> 62.3 us  [gather_group(): pl.pallas_call(gather_body, out_shape=jax.ShapeDtypeStruct((n, GROUP, r,...]
    gather x2 -> x1, local copies, waits for them, and re-layouts: 14.9 us -> 4.35 us  [local(): w_att = gather_group(jnp.take(slots, owners[:ATT], axis=0), 12)]
    unnamed x189 -> x60, local copies, waits for them, and re-layouts: 11.6 us -> 2.18 us
    reduce_sum x5 -> x2, other arithmetic: 10 us -> 1.42 us  [rms_norm(): values * lax.rsqrt(jnp.mean(values * values, axis=-1, keepdims=True) + NO...]
where the time goes in v2:
time: 519 us; the launch traced here: 515 us
  Pallas kernels  404 us (78%)
  local copies, waits for them, and re-layouts  40.7 us (8%)
  other arithmetic  39.4 us (8%)
  matrix products  29.1 us (6%)
    pallas_call x1, Pallas kernels, run_layer(): pl.pallas_call(layer_body, out_shape=tuple((o[0] for o in outs)), in_spec...  120 us
    pallas_call x1, Pallas kernels, sum_slices(): pl.pallas_call(grads_body, out_shape=(jax.ShapeDtypeStruct((GROUP, SLICE,...  88.2 us
    pallas_call x1, Pallas kernels, gather_slices(): pl.pallas_call(weights_body, out_shape=jax.ShapeDtypeStruct((4, 4, 2, 4,...  80.9 us
    pallas_call x2, Pallas kernels, gather_group(): pl.pallas_call(gather_body, out_shape=jax.ShapeDtypeStruct((n, GROUP, r,...  62.3 us
    pallas_call x1, Pallas kernels, sum_group(): pl.pallas_call(sum_body, out_shape=jax.ShapeDtypeStruct(blk, F32), in_spe...  40.4 us
    dot_general x6, matrix products, dot(): lax.dot_general(a, b, (((da,), (db,)), ((), ())), preferred_element_type=...  19.6 us
    pallas_call x1, Pallas kernels, send_back(): pl.pallas_call(back_body, out_shape=jax.ShapeDtypeStruct((4,) + pieces.sh...  12.1 us

profile of v2, /device:TPU:1, one launch (start us, length us, event | category | flops | bytes accessed | tf_op | source)
XLA Modules:
  0.0 514.9 jit_solution(11174585419014445303)
XLA Ops:
  0.7 1.2 multiply_cosine_fusion
  1.9 0.8 fusion.101
  3.4 1.1 fusion.42
  4.5 1.8 multiply_convert_fusion.x_ref
  6.3 21.5 %shard_map.180 = bf16[1,8,128,1152]{3,2,1,0:T(8,128)(2,1)} custom-call(bf16[1,128,1152]{2,1,0:T(8,128)(2,1)} %multiply_convert_fusion.x_ref), custom_call_target="tpu_custom_call" | custom-call | tf_op jit(solution)/shard_map/pallas_call | solution.py:111
  27.8 3.3 copy.69
  32.8 1.1 copy.68
  33.8 80.9 %shard_map.179 = bf16[4,4,2,4,32,1152]{5,4,3,2,1,0:T(8,128)(2,1)} custom-call(bf16[8,32,1152]{2,1,0:T(8,128)(2,1)} %bitcast.208), custom_call_target="tpu_custom_call" | custom-call | tf_op jit(solution)/shard_map/pallas_call | solution.py:241
  114.7 120.0 %shard_map.181 = (bf16[128,1152]{1,0:T(8,128)(2,1)}, f32[128,1152]{1,0:T(8,128)}, bf16[128,1152]{1,0:T(8,128)(2,1)}, f32[3,1152]{1,0:T(4,128)}, bf16[6,8,32,128]...) custom-call(s32[1,128]{1,0:T(1,128)} %doc_ref.1, ...), custom_call_target="tpu_custom_call" | custom-call | tf_op jit(solution)/shard_map/pallas_call | solution.py:774
  234.7 2.7 convolution_convert_fusion.3
  237.5 1.4 fusion.57
  239.3 3.5 fusion.26
  242.9 1.9 multiply_add_fusion.2
  244.7 0.9 slice.80
  245.6 1.2 copy.73
  247.0 1.3 fusion.55
  248.3 0.9 fusion.51
  249.2 1.8 copy.74
  251.0 1.1 copy.90
  252.1 3.2 fusion.23
  255.3 0.9 convert_element_type.100
  256.2 1.7 convert_element_type.101
  258.3 0.9 fusion.31.x_ref
  259.1 12.1 %shard_map.182 = bf16[4,2,128,256]{3,2,1,0:T(8,128)(2,1)} custom-call(bf16[4,2,128,256]{3,2,1,0:T(8,128)(2,1)} %fusion.31.x_ref), custom_call_target="tpu_custom_call" | custom-call | tf_op jit(solution)/shard_map/pallas_call | solution.py:446
  271.2 1.1 convert_reduce_fusion
  272.3 0.9 fusion.64
  273.7 0.9 slice.84
  275.3 4.3 gather_fusion
  279.7 1.0 broadcast_select_fusion.1.x_ref
  280.7 40.8 %shard_map.183 = bf16[10,8,32,1152]{3,2,1,0:T(8,128)(2,1)} custom-call(bf16[10,32,1152]{2,1,0:T(8,128)(2,1)} %broadcast_select_fusion.1.x_ref), custom_call_target="tpu_custom_call" | custom-call | tf_op jit(solution)/shard_map/pallas_call | solution.py:111
  321.5 3.5 copy.105
  326.0 2.2 fusion.39
  328.9 2.4 convolution_convert_fusion
  331.3 1.1 convolution_convert_fusion.4
  332.4 1.8 copy.83
  334.2 1.8 convolution_convert_fusion.1
  336.5 3.3 copy.104
  339.8 40.4 %shard_map.184 = f32[10,32,1152]{2,1,0:T(8,128)} custom-call(bf16[10,2,2,2,32,1152]{5,4,3,2,1,0:T(8,128)(2,1)} %bitcast.195), custom_call_target="tpu_custom_call" | custom-call | tf_op jit(solution)/shard_map/pallas_call | solution.py:164
  380.2 1.5 convert_element_type.108
  381.7 6.1 %pad_maximum_fusion = bf16[91,32,1152]{2,1,0:T(8,128)(2,1)} fusion(bf16[81,32,1152]{2,1,0:T(8,128)(2,1)} %get-tuple-element.30, bf16[10,32,1152]{2,1,0:T(8,128)(2,1)S(1)} %convert_element_type.108), kind=kLoop, calls=%fused_computation.5 | loop fusion | flops 3354624 | bytes 13418496 | tf_op jit(solution)/shard_map/concatenate | solution.py:932
  387.9 10.2 %gather_fusion.1 = bf16[128,32,1152]{2,1,0:T(8,128)(2,1)} fusion(bf16[91,32,1152]{2,1,0:T(8,128)(2,1)} %pad_maximum_fusion, s32[1024]{0:T(1024)S(1)} %pad_clamp_fusion), kind=kCustom, calls=%fused_computation.1 | custom fusion | bytes 18874880 | tf_op jit(solution)/shard_map/jit(_take)/gather | solution.py:940
  398.3 8.3 %broadcast_select_fusion.d_ref = bf16[4,4,2,4,32,1152]{5,4,3,2,1,0:T(8,128)(2,1)} fusion(bf16[4,4,2,4,32,1152]{5,4,3,2,1,0:T(8,128)(2,1)} %bitcast.194, pred[4,4,2,4]{3,2,1,0:T(4,128)(4,1)S(1)} %compare_and_fusion), kind=kLoop, calls=%fused_computation.3 | loop fusion | flops 4718592 | bytes 18874496 | tf_op jit(solution)/shard_map/jit(_take)/select_n | solution.py:940
  406.6 88.2 %shard_map.185 = (bf16[8,32,1152]{2,1,0:T(8,128)(2,1)}, f32[40,128]{1,0:T(8,128)}) custom-call(bf16[4,4,2,4,32,1152]{5,4,3,2,1,0:T(8,128)(2,1)} %broadcast_select_fusion.d_ref, f32[40,128]{1,0:T(8,128)} %bitcast.221), custom_call_target="tpu_custom_call" | custom-call | tf_op jit(solution)/shard_map/pallas_call | solution.py:359
  494.9 3.9 fusion.19
  499.4 4.1 fusion.29
  503.6 6.6 %fusion.5 = f32[1,1152,256]{2,1,0:T(8,128)} fusion(f32[1,1152,1152]{2,1,0:T(8,128)} %param.19, f32[1,1152,256]{2,1,0:T(8,128)S(1)} %copy-done.13, f32[1152,256]{1,0:T(8,128)S(1)} %fusion.19, f32[1,1152,256]{2,1,0:T(8,128)} %param.17, f32[1,1152,256]{2,1,0:T(8,128)} %param.18, pred[]{:T(512)} %compare_reduce_fusion, f32[1,256,256]{2,1,0:T(8,128)S(1)} %copy-done.18), kind=kOutput, calls=%fused_computation.15 | convolution fusion | flops 836878336 | bytes 11468801 | tf_op jit(solution)/shard_map/dot_general | solution.py:843
  510.2 1.4 multiply_subtract_fusion
  511.7 2.1 fusion.41
  (102 shorter events, 8.1 us)
Async XLA Ops:
  4.5 23.3 %copy-start.24 = (f32[128]{0:T(128)}, f32[128]{0:T(128)S(1)}, u32[]{:S(2)}) copy-start(f32[128]{0:T(128)S(1)} %fusion.42) | copy-start | bytes 1540
  27.8 4.9 copy-start.12
  234.7 2.7 copy-start.10
  237.4 1.5 copy-start.4
  239.3 12.8 %copy-start.2 = (f32[640,512]{0,1:T(8,128)}, f32[640,512]{0,1:T(8,128)S(1)}, u32[]{:S(2)}) copy-start(f32[640,512]{0,1:T(8,128)S(1)} %copy.89) | copy-start | bytes 3932164
  239.3 3.5 copy-start.19
  239.3 5.4 %copy-start.14 = (bf16[6,8,32,128]{3,2,1,0:T(8,128)(2,1)S(1)}, bf16[6,8,32,128]{3,2,1,0:T(8,128)(2,1)}, u32[]{:S(2)}) copy-start(bf16[6,8,32,128]{3,2,1,0:T(8,128)(2,1)} %get-tuple-element.28) | copy-start | bytes 1179652
  246.8 1.5 copy-start.7
  246.8 1.5 copy-start.8
  256.2 2.1 copy-start.5
  273.3 2.0 copy-start.23
  275.1 50.2 %copy-start.15 = (bf16[128,256]{0,1:T(8,128)(2,1)}, bf16[128,256]{0,1:T(8,128)(2,1)S(1)}, u32[]{:S(2)}) copy-start(bf16[128,256]{0,1:T(8,128)(2,1)S(1)} %copy.80) | copy-start | bytes 196612
  275.3 50.0 %copy-start.16 = (bf16[128,256]{0,1:T(8,128)(2,1)}, bf16[128,256]{0,1:T(8,128)(2,1)S(1)}, u32[]{:S(2)}) copy-start(bf16[128,256]{0,1:T(8,128)(2,1)S(1)} %copy.81) | copy-start | bytes 196612
  325.0 1.0 copy-start
  325.0 1.0 copy-start.9
  326.0 2.2 copy-start.22
  328.3 0.6 copy-start.21
  328.9 2.4 copy-start.3
  328.9 2.4 copy-start.11
  406.6 88.3 %copy-start.18 = (f32[1,256,256]{2,1,0:T(8,128)S(1)}, f32[1,256,256]{2,1,0:T(8,128)}, u32[]{:S(2)}) copy-start(f32[1,256,256]{2,1,0:T(8,128)} %param.20) | copy-start | bytes 786436
  499.4 4.1 copy-start.13
  503.5 6.7 %copy-start.20 = (f32[5120]{0:T(1024)S(1)}, f32[5120]{0:T(1024)}, u32[]{:S(2)}) copy-start(f32[5120]{0:T(1024)} %param.21) | copy-start | bytes 61444
  503.5 8.1 %copy-start.25 = (f32[128]{0:T(128)S(1)}, f32[128]{0:T(128)}, u32[]{:S(2)}) copy-start(f32[128]{0:T(128)} %copy-done.24) | copy-start | bytes 1540
  503.5 8.1 %copy-start.26 = (f32[128]{0:T(128)S(1)}, f32[128]{0:T(128)}, u32[]{:S(2)}) copy-start(f32[128]{0:T(128)} %get-tuple-element.37) | copy-start | bytes 1540
  503.5 8.1 %copy-start.1 = (bf16[1,128,1152]{2,1,0:T(8,128)(2,1)S(1)}, bf16[1,128,1152]{2,1,0:T(8,128)(2,1)}, u32[]{:S(2)}) copy-start(bf16[1,128,1152]{2,1,0:T(8,128)(2,1)} %param.12) | copy-start | bytes 884740
  503.5 8.1 %copy-start.6 = (f32[128,1152]{1,0:T(8,128)S(1)}, f32[128,1152]{1,0:T(8,128)}, u32[]{:S(2)}) copy-start(f32[128,1152]{1,0:T(8,128)} %get-tuple-element.64) | copy-start | bytes 1769476
  510.2 3.5 copy-start.17

commit v3 on v2

v3 whole, which is shorter than its diff:
```python
import functools

import jax
import jax.numpy as jnp
from jax import lax
from jax.experimental import pallas as pl
from jax.experimental.pallas import tpu as pltpu
from jax.sharding import Mesh
from jax.sharding import PartitionSpec as P

FF = 6912
HEADS = 4
WINDOW = 512
BLK = 64
STEP = 10
D = 1152
HD = 256
TOK = 128
GROUP = 8
SLICE = HD // GROUP
ATT = 2 * HEADS + 2
FFT = FF // HD

NORM_EPS = 1e-06
THETA = 10000.0
BETA_ONE = 0.5
BETA_TWO = 0.5
RATE = 0.02
GAIN_RATE = 0.4
DECAY = 0.01
ADAM_EPS = 1e-08

MESH = pl.DeviceIdType.MESH
AXES = ("y", "z", "xh", "core", "xl")
VMEM_LIMIT = 63 * 1024 * 1024
BF = jnp.bfloat16
F32 = jnp.float32


def here():
    y, z, xh, c, xl = [lax.axis_index(a) for a in AXES]
    return y, z, xh * 2 + xl, c


def place(y, z, x, c):
    return (y, z, x // 2, c, lax.rem(x, 2))


def member(x, c):
    return (x // 2) * 4 + c * 2 + lax.rem(x, 2)


def turn(a, d):
    return lax.rem(a + d, 4)


def greet(places):
    sem = pltpu.get_barrier_semaphore()
    for p in places:
        pl.semaphore_signal(sem, inc=1, device_id=p, device_id_type=MESH)
    pl.semaphore_wait(sem, len(places))


def remote(src, dst, send, recv, where):
    return pltpu.make_async_remote_copy(src, dst, send, recv, device_id=where, device_id_type=MESH)


def params(cid):
    return pltpu.CompilerParams(
        collective_id=cid, has_side_effects=True, vmem_limit_bytes=VMEM_LIMIT
    )


ANY = pl.BlockSpec(memory_space=pl.ANY)
INV = pl.BlockSpec(memory_space=pltpu.VMEM)
DMA = pltpu.SemaphoreType.DMA


def seq_place(s):
    return (s // 16, lax.rem(s // 4, 4), lax.rem(s // 2, 2), lax.rem(s, 2), lax.axis_index("xl"))


def seq_index():
    y, z, xh, c, xl = [lax.axis_index(a) for a in AXES]
    return ((y * 4 + z) * 2 + xh) * 2 + c


def norm_of(v, g):
    return v * lax.rsqrt(jnp.mean(v * v, axis=-1, keepdims=True) + NORM_EPS) * g


def norm_back(v, g, w):
    r = lax.rsqrt(jnp.mean(v * v, axis=-1, keepdims=True) + NORM_EPS)
    u = w * g
    dg = jnp.sum(w * (v * r), axis=0, keepdims=True)
    dv = r * u - v * (r * r * r * jnp.mean(u * v, axis=-1, keepdims=True))
    return dv, dg


def column(g_ref, i):
    row = g_ref[:, 4 * D + i * HD : 4 * D + (i + 1) * HD]
    return jnp.broadcast_to(row, (128, HD)).T[:, 0:1]


def rope_norm(v, g, cos, sin):
    n = v * lax.rsqrt(jnp.mean(v * v, axis=0, keepdims=True) + NORM_EPS) * g
    a, b = n[: HD // 2], n[HD // 2 :]
    return jnp.concatenate([a * cos - b * sin, b * cos + a * sin], axis=0)


def gelu_parts(g):
    k, a = 0.7978845608028654, 0.044715
    sq = g * g
    th = jnp.tanh(k * g * (1.0 + a * sq))
    half = 0.5 * (1.0 + th)
    slope = half + 0.5 * g * (1.0 - th * th) * (k * (1.0 + 3.0 * a * sq))
    return g * half, slope


def nn(a, b):
    return jnp.dot(a, b, preferred_element_type=F32)


def nt(a, b):
    return lax.dot_general(a, b, (((1,), (1,)), ((), ())), preferred_element_type=F32)


def start_body(
    own_ref, m_ref, x_ref, g_ref,
    o_ref, xa_ref, cos_ref, sin_ref, tile_ref,
    tile, own_sem, gs, gr, s1, r1, f1, q1, s2, r2, f2, q2, bxs, bxr, bcs, bcr,
):
    y, z, x, c = here()
    me = x * 2 + c
    mm = member(x, c)
    chips = {d: turn(x, d) for d in range(4)}
    peers = {d: place(y, z, chips[d], c) for d in (1, 2, 3)}
    twin = place(y, z, x, 1 - c)
    others = [(d, cc) for d in (1, 2, 3) for cc in range(2)]
    at = (z, y)
    ring = (
        {d: place(y, turn(z, d), x, c) for d in (1, 2, 3)},
        {d: place(turn(y, d), z, x, c) for d in (1, 2, 3)},
    )
    everyone = [place(y, z, chips[d], cc) for d, cc in others] + [twin]
    everyone = everyone + [ring[h][d] for h in (0, 1) for d in (1, 3)]
    sem = pltpu.get_barrier_semaphore()
    for p in everyone:
        pl.semaphore_signal(sem, inc=1, device_id=p, device_id_type=MESH)
    for h in range(2):
        tile[4 * h : 4 * h + 4] = m_ref[:, h * 128 : (h + 1) * 128].T.astype(BF).reshape(4, SLICE, D)
    pl.semaphore_wait(sem, len(everyone))

    sent = []

    def go(step):
        step.start()
        sent.append(step)
        return step

    mine = o_ref.at[y, z, mm // 4, lax.rem(mm, 4)]
    for d, cc in [(2, 0), (2, 1), (1, 0), (1, 1), (3, 0), (3, 1)]:
        go(remote(tile.at[chips[d] * 2 + cc], mine, gs.at[d, cc], gr.at[d, c], place(y, z, chips[d], cc)))
    go(remote(tile.at[x * 2 + 1 - c], mine, gs.at[0, 0], gr.at[0, c], twin))
    own = pltpu.make_async_copy(tile.at[me], mine, own_sem)
    own.start()
    xa_ref[x, c] = norm_of(x_ref[...].astype(F32), g_ref[:, 0:D]).astype(BF)
    mine_x = xa_ref.at[x, c]
    x_far = {d: remote(mine_x, mine_x, bxs.at[d - 1], bxr.at[d - 1], peers[d]) for d in (1, 3, 2)}
    for d in (1, 3, 2):
        go(x_far[d])
    x_near = [go(remote(mine_x, mine_x, bcs.at[0], bcr.at[0], twin))]
    own.wait()
    for d, cc in others:
        remote(tile.at[0], mine, gs.at[d, cc], gr.at[d, cc], twin).wait_recv()
    remote(tile.at[0], mine, gs.at[0, 0], gr.at[0, 1 - c], twin).wait_recv()

    def block(h, first, second):
        return o_ref.at[second, first, 0] if h == 0 else o_ref.at[first, second, 1]

    fc = {h: {d: turn(at[h], d) for d in range(4)} for h in (0, 1)}
    sc = {h: {d: turn(at[1 - h], d) for d in range(4)} for h in (0, 1)}
    ways = ((0, 1, 3), (1, 3, 1))
    one, two = {}, {}
    for h in (0, 1):
        b = block(h, fc[h][0], sc[h][0])
        for n, up, _ in ways:
            one[h, n] = go(remote(b, b, s1.at[h, n], r1.at[h, n], ring[h][up]))

    def second(k):
        for h in (0, 1):
            b = block(h, fc[h][k], sc[h][0])
            for n, up, _ in ways:
                two[h, k, n] = go(remote(b, b, s2.at[h, k, n], r2.at[h, k, n], ring[1 - h][up]))

    second(0)
    pos = (lax.axis_index("y") * 4 + z) * 4 + lax.axis_index("xh") * 2 + c
    pos = pos * TOK + lax.broadcasted_iota(jnp.int32, (HD // 2, TOK), 1)
    freq = lax.broadcasted_iota(jnp.int32, (HD // 2, TOK), 0).astype(F32)
    angle = pos.astype(F32) * jnp.exp(-jnp.log(THETA) * freq * 2.0 / HD)
    cos_ref[...] = jnp.cos(angle)
    sin_ref[...] = jnp.sin(angle)
    lane = lax.broadcasted_iota(jnp.int32, (1, 128), 1)

    def find(t, acc):
        return jnp.where(lane == own_ref[t], t, acc)

    tile_ref[...] = lax.fori_loop(0, ATT + 3 * FFT, find, jnp.zeros((1, 128), jnp.int32))
    far = {}
    for h in (0, 1):
        for n, up, down in ways:
            one[h, n].wait_recv()
            b = block(h, fc[h][down], sc[h][0]).at[2 * n : 2 * n + 2]
            far[h, n] = go(remote(b, b, f1.at[h, n], q1.at[h, n], ring[h][up]))
    second(3)
    second(1)
    for d in (1, 3, 2):
        x_far[d].wait_recv()
        src = xa_ref.at[chips[4 - d], c]
        x_near.append(go(remote(src, src, bcs.at[d], bcr.at[d], twin)))
    for h in (0, 1):
        for n in (0, 1):
            far[h, n].wait_recv()
    second(2)
    last = []
    for k in (0, 3, 1, 2):
        for h in (0, 1):
            for n, up, down in ways:
                two[h, k, n].wait_recv()
                b = block(h, fc[h][k], sc[h][down]).at[2 * n : 2 * n + 2]
                last.append(go(remote(b, b, f2.at[h, k, n], q2.at[h, k, n], ring[1 - h][up])))
    for step in x_near + last:
        step.wait_recv()
    for step in sent:
        step.wait_send()


def run_start(owners, master, x, gains, cid):
    f = jax.ShapeDtypeStruct
    smem = pl.BlockSpec(memory_space=pltpu.SMEM)
    return pl.pallas_call(
        start_body,
        out_shape=(
            f((4, 4, 2, 4, SLICE, D), BF),
            f((4, 2, TOK, D), BF),
            f((HD // 2, TOK), F32),
            f((HD // 2, TOK), F32),
            f((1, 128), jnp.int32),
        ),
        in_specs=[smem, INV, INV, INV],
        out_specs=(ANY, INV, INV, INV, INV),
        scratch_shapes=[
            pltpu.VMEM((GROUP, SLICE, D), BF),
            DMA,
            DMA((4, 2)), DMA((4, 2)),
            DMA((2, 2)), DMA((2, 2)), DMA((2, 2)), DMA((2, 2)),
            DMA((2, 4, 2)), DMA((2, 4, 2)), DMA((2, 4, 2)), DMA((2, 4, 2)),
            DMA((3,)), DMA((3,)), DMA((4,)), DMA((4,)),
        ],
        compiler_params=params(cid),
    )(owners, master, x, gains)


ORDER = (0, 3, 1, 2)


def layer_body(
    doc_ref, own_ref, wall_ref, xa_ref, x_ref, y_ref, g_ref, cos_ref, sin_ref,
    lo_ref, dr1_ref, dap_ref, gg_ref, raw_ref, qt_ref, k_ref, vt_ref, pt_ref, wo_ref, osl_ref, watt_ref, tg_ref,
    wall, wg, wu, wd, xa, sq, xf, dd, gb, ub, hb, dgb, dub, pbuf, sbuf, near, far, ptl, oto, dgt,
    load_sem, as_, ar, wxs, wxr, wcs, wcr, hs, hr, os_, or_, fxs, fxr, fcs, fcr, bxs, bxr, bcs, bcr,
    ss, sr, rs_, rr, out_sem,
):
    y, z, x, c = here()
    me = x * 2 + c
    twin = place(y, z, x, 1 - c)
    s = seq_index()
    chips = {d: turn(x, d) for d in range(4)}
    peers = {d: place(y, z, chips[d], c) for d in (1, 2, 3)}
    others = [(d, cc) for d in (1, 2, 3) for cc in range(2)]
    greet(
        [place(y, z, chips[d], cc) for d, cc in others]
        + [twin]
        + [seq_place(lax.rem(s + 64 + d, 64)) for d in (-4, -3, -2, -1, 1, 2, 3, 4)]
    )
    load_w = pltpu.make_async_copy(wall_ref, wall, load_sem.at[0])
    load_x = pltpu.make_async_copy(xa_ref, xa, load_sem.at[1])
    load_w.start()
    load_x.start()
    load_w.wait()

    for h in range(HEADS):
        wo_ref[h, me] = wall[own_ref[HEADS + 2 + h]]
    w_far = {}
    w_near = {}
    mine = wo_ref.at[:, me]
    for d in (1, 3, 2):
        w_far[d] = remote(mine, mine, wxs.at[d - 1], wxr.at[d - 1], peers[d])
    w_near[0] = remote(mine, mine, wcs.at[0], wcr.at[0], twin)

    watt = [wall[own_ref[t]] for t in range(HEADS + 2)]
    watt = jnp.concatenate(watt, axis=0)
    watt_ref[...] = watt
    load_x.wait()
    qkv = []
    for d in (2, 1, 3, 0):
        part = nt(watt, xa[chips[d]].reshape(2 * TOK, D)).astype(BF)
        for cc in range(2):
            sq[d, cc] = part[:, cc * TOK : (cc + 1) * TOK].reshape(HEADS + 2, SLICE, TOK)
        if d:
            for cc in range(2):
                step = remote(
                    sq.at[d, cc], raw_ref.at[:, me], as_.at[d, cc], ar.at[d, c], place(y, z, chips[d], cc)
                )
                step.start()
                qkv.append(step)
    step = remote(sq.at[0, 1 - c], raw_ref.at[:, me], as_.at[0, 0], ar.at[0, c], twin)
    step.start()
    qkv.append(step)
    raw_ref[:, me] = sq[0, c]
    for d in (1, 3, 2):
        w_far[d].start()
    w_near[0].start()

    def pack(t, carry):
        rows = pl.ds(pl.multiple_of(t * SLICE, SLICE), SLICE)
        wg[rows] = wall[own_ref[ATT + t]]
        wu[rows] = wall[own_ref[ATT + FFT + t]]
        wd[rows] = wall[own_ref[ATT + 2 * FFT + t]]
        return carry

    lax.fori_loop(0, FFT, pack, 0)
    for d in (1, 2, 3):
        for cc in range(2):
            remote(sq.at[d, cc], raw_ref.at[:, me], as_.at[d, cc], ar.at[d, cc], twin).wait_recv()
    remote(sq.at[0, 0], raw_ref.at[:, me], as_.at[0, 0], ar.at[0, 1 - c], twin).wait_recv()

    cos, sin = cos_ref[...], sin_ref[...]
    gain_q, gain_k = column(g_ref, 0), column(g_ref, 1)
    kt = rope_norm(
        raw_ref[HEADS].reshape(HD, TOK).astype(F32), gain_k, cos, sin
    )
    k_ref[4] = kt.T.astype(BF)
    vt_ref[:, 4 * TOK :] = raw_ref[HEADS + 1].reshape(HD, TOK)
    halo = []
    for d in (4, 3, 2, 1):
        to = seq_place(lax.rem(s + d, 64))
        a = remote(k_ref.at[4], k_ref.at[4 - d], hs.at[0, d - 1], hr.at[0, d - 1], to)
        b = remote(
            vt_ref.at[:, 4 * TOK :], vt_ref.at[:, (4 - d) * TOK : (5 - d) * TOK], hs.at[1, d - 1], hr.at[1, d - 1], to
        )
        a.start()
        b.start()
        halo.extend([a, b])
    for h in range(HEADS):
        q = rope_norm(raw_ref[h].reshape(HD, TOK).astype(F32), gain_q, cos, sin)
        qt_ref[:, h * TOK : (h + 1) * TOK] = q.astype(BF)
    row = lax.broadcasted_iota(jnp.int32, (WINDOW + TOK, TOK), 0)
    col = lax.broadcasted_iota(jnp.int32, (WINDOW + TOK, TOK), 1)
    seen = (row <= col + WINDOW) & (row > col) & (row >= WINDOW - s * TOK)
    half = lax.broadcasted_iota(jnp.int32, (BLK, TOK), 1) < BLK
    q_doc = jnp.where(half, doc_ref[0, 2 * s], doc_ref[0, 2 * s + 1])
    k_doc = jnp.concatenate(
        [
            jnp.full((BLK, TOK), doc_ref[0, jnp.maximum(2 * s - 8 + b, 0)], jnp.int32)
            for b in range(10)
        ],
        axis=0,
    )
    seen = seen & (k_doc == jnp.concatenate([q_doc] * 10, axis=0))
    for step in halo:
        step.wait_recv()
    keys = k_ref[...].reshape(WINDOW + TOK, HD)
    for h in range(HEADS):
        lanes = slice(h * TOK, (h + 1) * TOK)
        sc = nn(keys, qt_ref[:, lanes]) * (HD**-0.5)
        sc = jnp.where(seen, sc, -1e30)
        ex = jnp.exp(sc - jnp.max(sc, axis=0, keepdims=True))
        pr = ex / jnp.sum(ex, axis=0, keepdims=True)
        pt_ref[:, lanes] = pr
        ptl[:, lanes] = pr.astype(BF)
    ot = nn(vt_ref[...], ptl[...])
    oto[...] = ot.astype(BF)
    o_steps = []
    for d, cc in others:
        to = chips[d] * 2 + cc
        rows = pl.ds(pl.multiple_of(to * SLICE, SLICE), SLICE)
        step = remote(
            oto.at[rows], osl_ref.at[me], os_.at[d, cc], or_.at[d, c], place(y, z, chips[d], cc)
        )
        step.start()
        o_steps.append(step)
    rows = pl.ds(pl.multiple_of((x * 2 + 1 - c) * SLICE, SLICE), SLICE)
    step = remote(oto.at[rows], osl_ref.at[me], os_.at[0, 0], or_.at[0, c], twin)
    step.start()
    o_steps.append(step)
    osl_ref[me] = oto[pl.ds(pl.multiple_of(me * SLICE, SLICE), SLICE)]

    for d in (1, 3, 2):
        w_far[d].wait_recv()
        src = wo_ref.at[:, chips[4 - d] * 2 + c]
        w_near[d] = remote(src, src, wcs.at[d], wcr.at[d], twin)
        w_near[d].start()
    for step in w_near.values():
        step.wait()
    ap = jnp.zeros((TOK, D), F32)
    for h in range(HEADS):
        o = ot[:, h * TOK : (h + 1) * TOK].T.astype(BF)
        ap = ap + nn(o, wo_ref[h].reshape(HD, D))
    act = x_ref[...].astype(F32)
    r1 = act + norm_of(ap, g_ref[:, 1 * D : 2 * D])
    xf[x, c] = norm_of(r1, g_ref[:, 2 * D : 3 * D]).astype(BF)

    def gather_start(buf, xs, xr, cs, cr):
        own = buf.at[x, c]
        sends = {d: remote(own, own, xs.at[d - 1], xr.at[d - 1], peers[d]) for d in (1, 3, 2)}
        near_ = {0: remote(own, own, cs.at[0], cr.at[0], twin)}
        near_[0].start()
        for d in (1, 3, 2):
            sends[d].start()
        return sends, near_

    def gather_wait(buf, e, sends, near_, cs, cr):
        if e:
            d = 4 - e
            sends[d].wait_recv()
            src = buf.at[chips[e], c]
            near_[d] = remote(src, src, cs.at[d], cr.at[d], twin)
            near_[d].start()
            near_[d].wait_recv()
        else:
            near_[0].wait_recv()

    def gather_end(sends, near_):
        for step in list(sends.values()) + list(near_.values()):
            step.wait_send()

    def sum_swap(ph, e):
        step = remote(pbuf.at[e, 1 - c], near.at[ph, e], ss.at[ph, e], sr.at[ph, e], twin)
        step.start()
        return step

    def sum_send(ph, e, swap):
        swap.wait_recv()
        both = pbuf[e, c].astype(F32) + near[ph, e].astype(F32)
        if not e:
            return None, both
        sbuf[e - 1] = both.astype(BF)
        step = remote(sbuf.at[e - 1], far.at[ph, e - 1], rs_.at[ph, e - 1], rr.at[ph, e - 1], peers[e])
        step.start()
        return step, None

    def pipeline(ph, buf, xs, xr, cs, cr, block):
        sends, near_ = gather_start(buf, xs, xr, cs, cr)
        swaps, outs = {}, []
        for n, e in enumerate(ORDER):
            gather_wait(buf, e, sends, near_, cs, cr)
            pbuf[e] = block(e).astype(BF).reshape(2, TOK, D)
            swaps[e] = sum_swap(ph, e)
            if n >= 2:
                outs.append(sum_send(ph, ORDER[n - 1], swaps[ORDER[n - 1]])[0])
        outs.append(sum_send(ph, ORDER[3], swaps[ORDER[3]])[0])
        return sends, near_, swaps, outs

    def finish(ph, sends, near_, swaps, outs):
        _, total = sum_send(ph, 0, swaps[0])
        for step in outs:
            step.wait_recv()
        total = ((total + far[ph, 0].astype(F32)) + far[ph, 1].astype(F32)) + far[ph, 2].astype(F32)
        gather_end(sends, near_)
        for step in list(swaps.values()) + outs:
            step.wait_send()
        return total

    def forward(e):
        v = xf[chips[e]].reshape(2 * TOK, D)
        g = nt(v, wg[...])
        u = nt(v, wu[...])
        at = chips[e]
        gb[at] = g
        ub[at] = u
        h, _ = gelu_parts(g)
        hb[at] = (h * u).astype(BF)
        return nn(hb[at], wd[...])

    state = pipeline(0, xf, fxs, fxr, fcs, fcr, forward)
    dn = finish(0, *state)
    lo_ref[...] = (r1 + norm_of(dn, g_ref[:, 3 * D : 4 * D])).astype(BF)
    cot = y_ref[...].astype(F32)
    ddn, d_fpost = norm_back(dn, g_ref[:, 3 * D : 4 * D], cot)
    dd[x, c] = ddn.astype(BF)

    def backward(e):
        v = dd[chips[e]].reshape(2 * TOK, D)
        dh = nt(v, wd[...])
        at = chips[e]
        h, slope = gelu_parts(gb[at])
        dgb[at] = (dh * ub[at] * slope).astype(BF)
        dub[at] = (dh * h).astype(BF)
        return nn(dgb[at], wg[...]) + nn(dub[at], wu[...])

    state = pipeline(1, dd, bxs, bxr, bcs, bcr, backward)
    for i, (lhs, rhs) in enumerate(((dgb, xf), (dub, xf), (hb, dd))):
        for e in range(4):
            dgt[:, e * 2 * TOK : (e + 1) * 2 * TOK] = lhs[e].T
        for n in range(3):
            cols = slice(n * 384, (n + 1) * 384)
            g = nn(dgt[...], rhs[:, :, :, cols].reshape(GROUP * TOK, 384)).astype(BF)
            wall[i * FFT : (i + 1) * FFT, :, cols] = g.reshape(FFT, SLICE, 384)
    out = pltpu.make_async_copy(wall.at[0 : 3 * FFT], tg_ref, out_sem)
    out.start()
    dxf = finish(1, *state)
    e1, d_fpre = norm_back(r1, g_ref[:, 2 * D : 3 * D], dxf)
    dr1 = cot + e1
    dr1_ref[...] = dr1
    dap, d_apost = norm_back(ap, g_ref[:, 1 * D : 2 * D], dr1)
    dap_ref[...] = dap.astype(BF)
    gg_ref[0:1] = d_apost
    gg_ref[1:2] = d_fpre
    gg_ref[2:3] = d_fpost
    for d in (1, 2, 3):
        for cc in range(2):
            remote(oto.at[0:SLICE], osl_ref.at[me], os_.at[d, cc], or_.at[d, cc], twin).wait_recv()
    remote(oto.at[0:SLICE], osl_ref.at[me], os_.at[0, 0], or_.at[0, 1 - c], twin).wait_recv()
    for step in qkv + halo + o_steps + list(w_far.values()):
        step.wait_send()
    out.wait()


def run_layer(doc, owners, slots, xa, x, y, gains, cos, sin, cid):
    f = jax.ShapeDtypeStruct
    smem = pl.BlockSpec(memory_space=pltpu.SMEM)
    vm = pltpu.VMEM
    ffw = FFT * SLICE
    outs = [
        (f((TOK, D), BF), INV),
        (f((TOK, D), F32), INV),
        (f((TOK, D), BF), INV),
        (f((3, D), F32), INV),
        (f((HEADS + 2, GROUP, SLICE, TOK), BF), INV),
        (f((HD, HEADS * TOK), BF), INV),
        (f((5, TOK, HD), BF), INV),
        (f((HD, WINDOW + TOK), BF), INV),
        (f((WINDOW + TOK, HEADS * TOK), F32), INV),
        (f((HEADS, GROUP, SLICE, D), BF), INV),
        (f((GROUP, SLICE, HEADS * TOK), BF), INV),
        (f(((HEADS + 2) * SLICE, D), BF), INV),
        (f((3 * FFT, SLICE, D), BF), ANY),
    ]
    return pl.pallas_call(
        layer_body,
        out_shape=tuple(o[0] for o in outs),
        in_specs=[smem, smem, ANY, ANY, INV, INV, INV, INV, INV],
        out_specs=tuple(o[1] for o in outs),
        scratch_shapes=[
            vm((128, SLICE, D), BF),
            vm((ffw, D), BF),
            vm((ffw, D), BF),
            vm((ffw, D), BF),
            vm((4, 2, TOK, D), BF),
            vm((4, 2, HEADS + 2, SLICE, TOK), BF),
            vm((4, 2, TOK, D), BF),
            vm((4, 2, TOK, D), BF),
            vm((4, 2 * TOK, ffw), F32),
            vm((4, 2 * TOK, ffw), F32),
            vm((4, 2 * TOK, ffw), BF),
            vm((4, 2 * TOK, ffw), BF),
            vm((4, 2 * TOK, ffw), BF),
            vm((4, 2, TOK, D), BF),
            vm((3, TOK, D), BF),
            vm((2, 4, TOK, D), BF),
            vm((2, 3, TOK, D), BF),
            vm((WINDOW + TOK, HEADS * TOK), BF),
            vm((HD, HEADS * TOK), BF),
            vm((ffw, GROUP * TOK), BF),
            DMA((2,)),
            DMA((4, 2)), DMA((4, 2)),
            DMA((3,)), DMA((3,)), DMA((4,)), DMA((4,)),
            DMA((2, 4)), DMA((2, 4)),
            DMA((4, 2)), DMA((4, 2)),
            DMA((3,)), DMA((3,)), DMA((4,)), DMA((4,)),
            DMA((3,)), DMA((3,)), DMA((4,)), DMA((4,)),
            DMA((2, 4)), DMA((2, 4)), DMA((2, 3)), DMA((2, 3)),
            DMA,
        ],
        compiler_params=params(cid),
    )(doc, owners, slots, xa, x, y, gains, cos, sin)


def rope_norm_back(v, g, cos, sin, w):
    r = lax.rsqrt(jnp.mean(v * v, axis=0, keepdims=True) + NORM_EPS)
    a, b = w[: HD // 2], w[HD // 2 :]
    dn = jnp.concatenate([a * cos + b * sin, b * cos - a * sin], axis=0)
    dg = jnp.sum(dn * (v * r), axis=1, keepdims=True)
    u = dn * g
    dv = r * u - v * (r * r * r * jnp.mean(u * v, axis=0, keepdims=True))
    return dv, dg


def rows_add(dst, src, n):
    def step(i, carry):
        dst[i] = (dst[i].astype(F32) + src[i].astype(F32)).astype(BF)
        return carry

    lax.fori_loop(0, n, step, 0)


def back_layer_body(
    tile_ref, dap_ref, osl_ref, wo_ref, k_ref, vt_ref, pt_ref, qt_ref, raw_ref, cos_ref, sin_ref,
    dr1_ref, x_ref, g_ref, gg_ref, watt_ref, xa_ref, tg_ref, gf_ref, gs_ref,
    grad_ref, ig_ref, ng_ref, nf_ref, ns_ref,
    xa, tg, slots, t1, t2, sums, u1, u2, fin, dd, dot_, dst, ptl, hsend, hrec, dqk, drec, dsl,
    pbuf, sbuf, near, far, da, a1, amid, a2, att, gl, gin, gmid, gin2,
    load_sem, bxs, bxr, bcs, bcr, hs, hr, qs, qr, ss, sr, rs_, rr,
    g1s, g1r, g2s, g2r, k1s, k1r, k2s, k2r, a1s, a1r, a2s, a2r, b1s, b1r, b2s, b2r, fs, fr,
    gas, gar, gbs, gbr,
):
    y, z, x, c = here()
    me = x * 2 + c
    twin = place(y, z, x, 1 - c)
    s = seq_index()
    chips = {d: turn(x, d) for d in range(4)}
    peers = {d: place(y, z, chips[d], c) for d in (1, 2, 3)}
    others = [(d, cc) for d in (1, 2, 3) for cc in range(2)]
    at = (y, z)
    ring = (
        {d: place(turn(y, d), z, x, c) for d in (1, 2, 3)},
        {d: place(y, turn(z, d), x, c) for d in (1, 2, 3)},
    )
    greet(
        [place(y, z, chips[d], cc) for d, cc in others]
        + [twin]
        + [seq_place(lax.rem(s + 64 + d, 64)) for d in (-4, -3, -2, -1, 1, 2, 3, 4)]
        + list(ring[0].values())
        + list(ring[1].values())
    )
    load_t = pltpu.make_async_copy(tg_ref, tg, load_sem.at[0])
    load_x = pltpu.make_async_copy(xa_ref, xa, load_sem.at[1])
    load_t.start()
    load_x.start()
    dd[x, c] = dap_ref[...]
    own = dd.at[x, c]
    d_far = {d: remote(own, own, bxs.at[d - 1], bxr.at[d - 1], peers[d]) for d in (1, 3, 2)}
    d_near = {0: remote(own, own, bcs.at[0], bcr.at[0], twin)}
    d_near[0].start()
    for d in (1, 3, 2):
        d_far[d].start()

    load_t.wait()

    def fill(i, carry):
        t = jnp.clip(tile_ref[i] - ATT, 0, 3 * FFT - 1)
        slots[i // 32, lax.rem(i // 8, 4), lax.rem(i // 4, 2), lax.rem(i, 4)] = tg[t]
        return carry

    lax.fori_loop(0, 128, fill, 0)

    def part(h, first, second):
        return slots.at[first, second, 0] if h == 0 else slots.at[second, first, 1]

    sent = []

    def go(step):
        step.start()
        sent.append(step)
        return step

    here1 = {h: {d: turn(at[h], d) for d in range(4)} for h in (0, 1)}
    here2 = {h: {d: turn(at[1 - h], d) for d in range(4)} for h in (0, 1)}
    JS = (2, 1, 3, 0)
    s1 = {}
    for j in JS:
        for h in (0, 1):
            blk = part(h, here1[h][2], here2[h][j])
            s1[h, j, 0] = go(remote(blk.at[0:2], t1.at[h, j, 0], g1s.at[h, j, 0], g1r.at[h, j, 0], ring[h][1]))
            s1[h, j, 1] = go(remote(blk.at[2:4], t1.at[h, j, 1], g1s.at[h, j, 1], g1r.at[h, j, 1], ring[h][3]))

    wo = wo_ref[...].reshape(HEADS * HD, D)
    dmix = nt(wo, dap_ref[...]).astype(BF)
    for h in range(HEADS):
        dot_[:, h * TOK : (h + 1) * TOK] = dmix[h * HD : (h + 1) * HD]
    values = jnp.concatenate([vt_ref[:, b * TOK : (b + 1) * TOK].T for b in range(5)], axis=0)
    for h in range(HEADS):
        lanes = slice(h * TOK, (h + 1) * TOK)
        pr = pt_ref[:, lanes]
        dp = nn(values, dot_[:, lanes])
        inner = jnp.sum(pr * dp, axis=0, keepdims=True)
        dst[:, lanes] = (pr * (dp - inner) * (HD**-0.5)).astype(BF)
        ptl[:, lanes] = pr.astype(BF)
    dk = nt(qt_ref[...], dst[...])
    dv = nt(dot_[...], ptl[...])
    halo = []
    for d in (4, 3, 2, 1):
        lanes = slice((4 - d) * TOK, (5 - d) * TOK)
        hsend[d - 1, 0] = dk[:, lanes].astype(BF)
        hsend[d - 1, 1] = dv[:, lanes].astype(BF)
        step = remote(
            hsend.at[d - 1], hrec.at[d - 1], hs.at[d - 1], hr.at[d - 1], seq_place(lax.rem(s + 64 - d, 64))
        )
        halo.append(go(step))
    dk = dk[:, 4 * TOK :]
    dv = dv[:, 4 * TOK :]
    keys_t = jnp.concatenate([k_ref[b].T for b in range(5)], axis=1)
    cos, sin = cos_ref[...], sin_ref[...]
    gain_q, gain_k = column(g_ref, 0), column(g_ref, 1)
    dgq = jnp.zeros((HD, 1), F32)
    for h in range(HEADS):
        dq = nn(keys_t, dst[:, h * TOK : (h + 1) * TOK])
        raw = raw_ref[h].reshape(HD, TOK).astype(F32)
        dq, dg = rope_norm_back(raw, gain_q, cos, sin, dq)
        dqk[h] = dq.astype(BF).reshape(GROUP, SLICE, TOK)
        dgq = dgq + dg

    s2 = {}
    for j in JS:
        for h in (0, 1):
            s1[h, j, 0].wait_recv()
            blk = part(h, here1[h][1], here2[h][j])
            rows_add(blk.at[0:2], t1.at[h, j, 0], 2)
            s2[h, j, 0] = go(remote(blk, t2.at[h, j, 0], g2s.at[h, j, 0], g2r.at[h, j, 0], ring[h][1]))
            s1[h, j, 1].wait_recv()
            blk = part(h, here1[h][3], here2[h][j])
            rows_add(blk.at[2:4], t1.at[h, j, 1], 2)
            s2[h, j, 1] = go(remote(blk, t2.at[h, j, 1], g2s.at[h, j, 1], g2r.at[h, j, 1], ring[h][3]))

    for step in halo:
        step.wait_recv()
    for d in range(4):
        dk = dk + hrec[d, 0].astype(F32)
        dv = dv + hrec[d, 1].astype(F32)
    raw = raw_ref[HEADS].reshape(HD, TOK).astype(F32)
    dk, dgk = rope_norm_back(raw, gain_k, cos, sin, dk)
    dqk[HEADS] = dk.astype(BF).reshape(GROUP, SLICE, TOK)
    dqk[HEADS + 1] = dv.astype(BF).reshape(GROUP, SLICE, TOK)
    for d, cc in others:
        to = chips[d] * 2 + cc
        go(remote(dqk.at[:, to], drec.at[me], qs.at[d, cc], qr.at[d, c], place(y, z, chips[d], cc)))
    go(remote(dqk.at[:, x * 2 + 1 - c], drec.at[me], qs.at[0, 0], qr.at[0, c], twin))
    drec[me] = dqk[:, me]

    for d in (1, 3, 2):
        d_far[d].wait_recv()
        src = dd.at[chips[4 - d], c]
        d_near[d] = go(remote(src, src, bcs.at[d], bcr.at[d], twin))
    for d in (0, 1, 3, 2):
        d_near[d].wait_recv()
    da[...] = jnp.zeros_like(da)
    for h in range(HEADS):
        for p in range(GROUP):
            dsl[h * SLICE : (h + 1) * SLICE, p * TOK : (p + 1) * TOK] = osl_ref[p, :, h * TOK : (h + 1) * TOK]
    g = nn(dsl[0 : HEADS * SLICE], dd[...].reshape(GROUP * TOK, D)).astype(BF)
    for h in range(HEADS):
        da[(HEADS + 2 + h) // 4, (HEADS + 2 + h) % 4] = g[h * SLICE : (h + 1) * SLICE]

    for d, cc in others:
        remote(dqk.at[:, 0], drec.at[me], qs.at[d, cc], qr.at[d, cc], twin).wait_recv()
    remote(dqk.at[:, 0], drec.at[me], qs.at[0, 0], qr.at[0, 1 - c], twin).wait_recv()
    for p in range(GROUP):
        dsl[:, p * TOK : (p + 1) * TOK] = drec[p].reshape((HEADS + 2) * SLICE, TOK)
    load_x.wait()
    g = nn(dsl[...], xa[...].reshape(GROUP * TOK, D)).astype(BF)
    for t in range(HEADS + 2):
        da[t // 4, t % 4] = g[t * SLICE : (t + 1) * SLICE]

    v1 = []
    for i in (1, 0, 2):
        for h in (0, 1):
            src = dav(da, h, here1[h][i + 1], slice(h * 16, h * 16 + 16))
            v1.append(go(remote(src, a1.at[h, i], a1s.at[h, i], a1r.at[h, i], ring[h][i + 1])))

    swaps, outs = {}, []
    watt = watt_ref[...]

    def sum_send(e):
        swaps[e].wait_recv()
        both = pbuf[e, c].astype(F32) + near[e].astype(F32)
        if not e:
            return both
        sbuf[e - 1] = both.astype(BF)
        outs.append(go(remote(sbuf.at[e - 1], far.at[e - 1], rs_.at[e - 1], rr.at[e - 1], peers[e])))
        return None

    for n, e in enumerate(JS):
        for cc in range(2):
            block = drec[chips[e] * 2 + cc].reshape((HEADS + 2) * SLICE, TOK).T
            pbuf[e, cc] = nn(block, watt).astype(BF)
        swaps[e] = go(remote(pbuf.at[e, 1 - c], near.at[e], ss.at[e], sr.at[e], twin))
        if n:
            sum_send(JS[n - 1])

    for step in v1:
        step.wait_recv()
    v2 = []
    for i in (1, 0, 2, 3):
        for h in (0, 1):
            rows = slice(h * 16, h * 16 + 16)
            j = here2[h][(i + 1) % 4]
            mine = da[at[0], j, rows] if h == 0 else da[j, at[1], rows]
            tot = mine.astype(F32) + a1[h, 0, j].astype(F32)
            tot = (tot + a1[h, 1, j].astype(F32)) + a1[h, 2, j].astype(F32)
            amid[h, i] = tot.astype(BF)
            if i < 3:
                v2.append(go(remote(amid.at[h, i], a2.at[h, i], a2s.at[h, i], a2r.at[h, i], ring[1 - h][i + 1])))

    both = sum_send(0)
    for step in outs:
        step.wait_recv()
    dxa = ((both + far[0].astype(F32)) + far[1].astype(F32)) + far[2].astype(F32)
    act = x_ref[...].astype(F32)
    e2, d_apre = norm_back(act, g_ref[:, 0 * D : 1 * D], dxa)
    ig_ref[...] = dr1_ref[...] + e2
    for k in range(9):
        lanes = slice(k * 128, (k + 1) * 128)
        gl[k : k + 1] = d_apre[:, lanes]
        for m in range(3):
            gl[9 * (m + 1) + k : 9 * (m + 1) + k + 1] = gg_ref[m : m + 1, lanes]
    for m, dg in enumerate((dgq, dgk)):
        flat = jnp.broadcast_to(dg, (HD, 128)).T
        for k in range(2):
            gl[36 + 2 * m + k : 37 + 2 * m + k] = flat[0:1, k * 128 : (k + 1) * 128]
    for d, cc in others:
        go(remote(gl, gin.at[d, c], gas.at[d, cc], gar.at[d, c], place(y, z, chips[d], cc)))
    go(remote(gl, gin.at[0, c], gas.at[0, 0], gar.at[0, c], twin))

    for step in v2:
        step.wait_recv()
    mine = at[0] * 4 + at[1]
    for h in (0, 1):
        rows = slice(h * 16, h * 16 + 16)
        tot = amid[h, 3].astype(F32) + a2[h, 0].astype(F32)
        tot = (tot + a2[h, 1].astype(F32)) + a2[h, 2].astype(F32)
        att[mine, rows] = tot.astype(BF)
    w1 = {}
    for i in (0, 2, 1):
        for h in (0, 1):
            src = att.at[mine, h * 16 : h * 16 + 16]
            w1[h, i] = go(remote(src, src, b1s.at[h, i], b1r.at[h, i], ring[1 - h][i + 1]))
    w2 = []

    def onward(j):
        for h in (0, 1):
            k = at[0] * 4 + here2[h][j] if h == 0 else here2[h][j] * 4 + at[1]
            src = att.at[k, h * 16 : h * 16 + 16]
            for i in (0, 2, 1):
                w2.append(go(remote(src, src, b2s.at[h, j, i], b2r.at[h, j, i], ring[h][i + 1])))

    onward(0)
    for i in (0, 2, 1):
        for h in (0, 1):
            w1[h, i].wait_recv()
        onward(3 - i)

    def close(j):
        for h in (0, 1):
            s2[h, j, 0].wait_recv()
            s2[h, j, 1].wait_recv()
            blk = part(h, here1[h][0], here2[h][j])

            def step(i, carry, h=h, blk=blk):
                t = blk[i].astype(F32) + t2[h, j, 0, i].astype(F32)
                sums[h, j, i] = (t + t2[h, j, 1, i].astype(F32)).astype(BF)
                return carry

            lax.fori_loop(0, 4, step, 0)

    e1, e2_ = {}, {}
    close(2)
    for h in (0, 1):
        e1[h, 0] = go(remote(sums.at[h, 2, 0:2], u1.at[h, 0], k1s.at[h, 0], k1r.at[h, 0], ring[1 - h][1]))
        e1[h, 1] = go(remote(sums.at[h, 2, 2:4], u1.at[h, 1], k1s.at[h, 1], k1r.at[h, 1], ring[1 - h][3]))
    for n, j in ((0, 1), (1, 3)):
        close(j)
        for h in (0, 1):
            e1[h, n].wait_recv()
            rows_add(sums.at[h, j, 2 * n : 2 * n + 2], u1.at[h, n], 2)
            e2_[h, n] = go(remote(sums.at[h, j], u2.at[h, n], k2s.at[h, n], k2r.at[h, n], ring[1 - h][j]))
    close(0)

    for d, cc in others:
        remote(gl, gin.at[d, cc], gas.at[d, cc], gar.at[d, cc], twin).wait_recv()
    remote(gl, gin.at[0, 1 - c], gas.at[0, 0], gar.at[0, 1 - c], twin).wait_recv()
    gin[0, c] = gl[...]
    acc = gin[0, 0] + gin[0, 1]
    for d, cc in others:
        acc = acc + gin[d, cc]
    gmid[0] = acc
    for n in (0, 1):
        steps = [
            go(remote(gmid.at[n], gin2.at[n, d - 1], gbs.at[n, d - 1], gbr.at[n, d - 1], ring[1 - n][d]))
            for d in (1, 2, 3)
        ]
        for step in steps:
            step.wait_recv()
        acc = ((gmid[n] + gin2[n, 0]) + gin2[n, 1]) + gin2[n, 2]
        if n == 0:
            gmid[1] = acc
        else:
            first = BETA_ONE * gf_ref[...] + (1.0 - BETA_ONE) * acc
            second = BETA_TWO * gs_ref[...] + (1.0 - BETA_TWO) * acc * acc
            nf_ref[...] = first
            ns_ref[...] = second
            u = first / (1.0 - BETA_ONE**STEP) / (jnp.sqrt(second / (1.0 - BETA_TWO**STEP)) + ADAM_EPS)
            for k in range(40):
                lanes = slice(k * 128, (k + 1) * 128)
                ng_ref[k : k + 1] = g_ref[:, lanes] - GAIN_RATE * u[k : k + 1]

    for step in w2:
        step.wait_recv()
    for h in (0, 1):
        e2_[h, 0].wait_recv()
        e2_[h, 1].wait_recv()
        for i in range(4):
            t = sums[h, 0, i].astype(F32) + u2[h, 0, i].astype(F32)
            fin[h * 4 + i] = (t + u2[h, 1, i].astype(F32)).astype(BF)
    base = (y * 4 + z) * GROUP
    for q in range(GROUP):
        t = tile_ref[base + q]
        low = att[jnp.clip(t, 0, ATT - 1)]
        fin[q] = jnp.where(t < ATT, low, fin[q])
    for d, cc in others:
        go(
            remote(
                fin.at[member(chips[d], cc)], grad_ref.at[me], fs.at[d, cc], fr.at[d, c], place(y, z, chips[d], cc)
            )
        )
    go(remote(fin.at[member(x, 1 - c)], grad_ref.at[me], fs.at[0, 0], fr.at[0, c], twin))
    grad_ref[me] = fin[member(x, c)]
    for d, cc in others:
        remote(fin.at[0], grad_ref.at[me], fs.at[d, cc], fr.at[d, cc], twin).wait_recv()
    remote(fin.at[0], grad_ref.at[me], fs.at[0, 0], fr.at[0, 1 - c], twin).wait_recv()
    for step in sent + list(d_far.values()) + [d_near[0]]:
        step.wait_send()


def dav(da, h, to, rows):
    return da.at[to, :, rows] if h == 0 else da.at[:, to, rows]


def run_back(tile_of, dap, osl, wo, kk, vt, pt, qt, raw, cos, sin, dr1, x, gains, gg, watt, xa, tg, gf, gs, cid):
    f = jax.ShapeDtypeStruct
    smem = pl.BlockSpec(memory_space=pltpu.SMEM)
    vm = pltpu.VMEM
    return pl.pallas_call(
        back_layer_body,
        out_shape=(f((GROUP, SLICE, D), BF), f((TOK, D), F32)) + (f((40, 128), F32),) * 3,
        in_specs=[smem] + [INV] * 15 + [ANY, ANY, INV, INV],
        out_specs=(INV,) * 5,
        scratch_shapes=[
            vm((4, 2, TOK, D), BF),
            vm((3 * FFT, SLICE, D), BF),
            vm((4, 4, 2, 4, SLICE, D), BF),
            vm((2, 4, 2, 2, SLICE, D), BF),
            vm((2, 4, 2, 4, SLICE, D), BF),
            vm((2, 4, 4, SLICE, D), BF),
            vm((2, 2, 2, SLICE, D), BF),
            vm((2, 2, 4, SLICE, D), BF),
            vm((GROUP, SLICE, D), BF),
            vm((4, 2, TOK, D), BF),
            vm((HD, HEADS * TOK), BF),
            vm((WINDOW + TOK, HEADS * TOK), BF),
            vm((WINDOW + TOK, HEADS * TOK), BF),
            vm((4, 2, HD, TOK), BF),
            vm((4, 2, HD, TOK), BF),
            vm((HEADS + 2, GROUP, SLICE, TOK), BF),
            vm((GROUP, HEADS + 2, SLICE, TOK), BF),
            vm(((HEADS + 2) * SLICE, GROUP * TOK), BF),
            vm((4, 2, TOK, D), BF),
            vm((3, TOK, D), BF),
            vm((4, TOK, D), BF),
            vm((3, TOK, D), BF),
            vm((4, 4, SLICE, D), BF),
            vm((2, 3, 4, 16, D), BF),
            vm((2, 4, 16, D), BF),
            vm((2, 3, 16, D), BF),
            vm((16, SLICE, D), BF),
            vm((40, 128), F32),
            vm((4, 2, 40, 128), F32),
            vm((2, 40, 128), F32),
            vm((2, 3, 40, 128), F32),
            DMA((2,)),
            DMA((3,)), DMA((3,)), DMA((4,)), DMA((4,)),
            DMA((4,)), DMA((4,)),
            DMA((4, 2)), DMA((4, 2)),
            DMA((4,)), DMA((4,)), DMA((3,)), DMA((3,)),
            DMA((2, 4, 2)), DMA((2, 4, 2)), DMA((2, 4, 2)), DMA((2, 4, 2)),
            DMA((2, 2)), DMA((2, 2)), DMA((2, 2)), DMA((2, 2)),
            DMA((2, 3)), DMA((2, 3)), DMA((2, 3)), DMA((2, 3)),
            DMA((2, 3)), DMA((2, 3)), DMA((2, 4, 3)), DMA((2, 4, 3)),
            DMA((4, 2)), DMA((4, 2)),
            DMA((4, 2)), DMA((4, 2)),
            DMA((2, 3)), DMA((2, 3)),
        ],
        compiler_params=params(cid),
    )(tile_of, dap, osl, wo, kk, vt, pt, qt, raw, cos, sin, dr1, x, gains, gg, watt, xa, tg, gf, gs)


def step_body(
    own_ref, g_ref, l_hbm, r_hbm, m_hbm, f_hbm, s_hbm, mo_hbm, fo_hbm, so_hbm, lv, rv, mv, fv, sv, lb, sem
):
    y, z, x, c = here()
    slot = (y * 4 + z) * GROUP + member(x, c)
    ins = [
        pltpu.make_async_copy(a, b, sem.at[i])
        for i, (a, b) in enumerate(((l_hbm, lv), (r_hbm, rv), (f_hbm, fv), (s_hbm, sv), (m_hbm, mv)))
    ]
    for step in ins:
        step.start()
    owned = lax.fori_loop(0, ATT + 3 * FFT, lambda t, a: a + (own_ref[t] == slot).astype(jnp.int32), 0) > 0
    ins[0].wait()
    lb[...] = lv[...].astype(BF)
    rot = nn(g_ref[...].reshape(HD, D), lb[...])
    ins[1].wait()
    right = rv[...].astype(BF)
    rot = nn(rot.T.astype(BF), right)
    ins[2].wait()
    ins[3].wait()
    first = BETA_ONE * fv[...] + (1.0 - BETA_ONE) * rot
    second = BETA_TWO * sv[...] + (1.0 - BETA_TWO) * rot * rot
    u = first / (1.0 - BETA_ONE**STEP) / (jnp.sqrt(second / (1.0 - BETA_TWO**STEP)) + ADAM_EPS)
    fv[...] = jnp.where(owned, first, fv[...])
    sv[...] = jnp.where(owned, second, sv[...])
    outs = [pltpu.make_async_copy(fv, fo_hbm, sem.at[5]), pltpu.make_async_copy(sv, so_hbm, sem.at[6])]
    for step in outs:
        step.start()
    back = nn(lb[...], nt(u.astype(BF), right).astype(BF))
    ins[4].wait()
    w = mv[...]
    mv[...] = jnp.where(owned, w - RATE * (back + DECAY * w), w)
    outs.append(pltpu.make_async_copy(mv, mo_hbm, sem.at[7]))
    outs[2].start()
    for step in outs:
        step.wait()


def run_step(owners, grad, left, right, master, first, second):
    f = jax.ShapeDtypeStruct
    vm = pltpu.VMEM
    tile = f((D, HD), F32)
    return pl.pallas_call(
        step_body,
        out_shape=(tile, tile, tile),
        in_specs=[pl.BlockSpec(memory_space=pltpu.SMEM), INV, ANY, ANY, ANY, ANY, ANY],
        out_specs=(ANY, ANY, ANY),
        scratch_shapes=[
            vm((D, D), F32), vm((HD, HD), F32), vm((D, HD), F32), vm((D, HD), F32), vm((D, HD), F32), vm((D, D), BF),
            DMA((8,)),
        ],
        compiler_params=pltpu.CompilerParams(vmem_limit_bytes=VMEM_LIMIT),
    )(owners, grad, left, right, master, first, second)


def local(
    inputs,
    out_grad,
    doc_ids,
    owners,
    masters,
    first_old,
    second_old,
    left_basis,
    right_basis,
    gains,
    gain_first,
    gain_second,
):
    x = inputs[0]
    row = gains.reshape(1, 5120)
    slots, xa, cos, sin, tile_of = run_start(owners, masters[0], x, row, 1)
    (layer_out, dr1, dap, gg, raw, qt, kk, vt, pt, wo, osl, watt, t_ffn) = run_layer(
        doc_ids, owners, slots.reshape(128, SLICE, D), xa, x, out_grad[0], row, cos, sin, 2
    )
    grad, input_grad, new_gains, new_gain_first, new_gain_second = run_back(
        tile_of.reshape(128), dap, osl, wo, kk, vt, pt, qt, raw, cos, sin, dr1, x, row, gg, watt, xa, t_ffn,
        gain_first.reshape(40, 128), gain_second.reshape(40, 128), 3,
    )
    new_masters, new_first, new_second = run_step(
        owners, grad, left_basis[0], right_basis[0], masters[0], first_old[0], second_old[0]
    )
    return (
        layer_out[None],
        input_grad[None],
        new_masters[None],
        new_first[None],
        new_second[None],
        new_gains.reshape(5120),
        new_gain_first.reshape(5120),
        new_gain_second.reshape(5120),
    )


def solution(mesh):
    wide = Mesh(mesh.devices.reshape(4, 4, 2, 2, 2), AXES)
    tokens = P("xl", ("y", "z", "xh", "core"), None)
    held = P(AXES, None, None)
    return jax.shard_map(
        local,
        mesh=wide,
        in_specs=(tokens, tokens, P("xl", None), P(), held, held, held, held, held, P(), P(), P()),
        out_specs=(tokens, tokens, held, held, held, P(), P(), P()),
        check_vma=False,
    )
```

time: 519 us -> 315 us (0.61)
  Pallas kernels: 404 us -> 308 us
  other arithmetic: 39.4 us -> 0 us
  local copies, waits for them, and re-layouts: 40.7 us -> 3.38 us
  matrix products: 29.1 us -> 0 us
    pallas_call x6 -> x3, Pallas kernels: 284 us -> 189 us  [the longest x1 111 us: run_back(): pl.pallas_call(back_layer_body, out_shape=(f((GROUP, SLICE, D), BF), f((T...]
    dot_general x11 -> x0, matrix products: 29.1 us -> none  [the longest x6 19.6 us: dot(): lax.dot_general(a, b, (((da,), (db,)), ((), ())), preferred_element_type=...]
    gather x2 -> x0, local copies, waits for them, and re-layouts: 14.5 us -> none  [the longest x1 10.2 us: local(): by_slot = jnp.take(by_tile, tile_of, axis=0).reshape(4, 4, 2, 4, SLICE, D)]
    select_n x3 -> x0, other arithmetic: 9.35 us -> none  [the longest x2 8.34 us: local(): by_slot = jnp.take(by_tile, tile_of, axis=0).reshape(4, 4, 2, 4, SLICE, D)]
    reshape x4 -> x0, local copies, waits for them, and re-layouts: 8.25 us -> none  [the longest x1 3.46 us: local(): w_att.reshape(ATT, 2, 2, 2, SLICE, D).transpose(0, 1, 3, 2, 4, 5)]
    concatenate x2 -> x0, other arithmetic: 6.59 us -> none  [the longest x1 6.14 us: local(): by_tile = jnp.concatenate([t_att, t_ffn])]
    broadcast_in_dim x2 -> x0, other arithmetic: 6.15 us -> none  [the longest x1 4.08 us: local(): new_second = jnp.where(owned, second_new, second_old[0])[None]]
    another operation x7 -> x0, local copies, waits for them, and re-layouts: 6.04 us -> none  [the longest x1 3.32 us: local(): xa_all.reshape(2, 2, 2, TOK, D).transpose(0, 2, 1, 3, 4)]
where the time goes in v3:
time: 315 us; the launch traced here: 313 us
  Pallas kernels  308 us (98%)
  local copies, waits for them, and re-layouts  3.38 us (1%)
    pallas_call x1, Pallas kernels, run_layer(): pl.pallas_call(layer_body, out_shape=tuple((o[0] for o in outs)), in_spec...  119 us
    pallas_call x1, Pallas kernels, run_back(): pl.pallas_call(back_layer_body, out_shape=(f((GROUP, SLICE, D), BF), f((T...  111 us
    pallas_call x1, Pallas kernels, run_start(): pl.pallas_call(start_body, out_shape=(f((4, 4, 2, 4, SLICE, D), BF), f((4...  69.6 us
    pallas_call x1, Pallas kernels, run_step(): pl.pallas_call(step_body, out_shape=(tile, tile, tile), in_specs=[pl.Bloc...  8.71 us

profile of v3, /device:TPU:1, one launch (start us, length us, event | category | flops | bytes accessed | tf_op | source)
XLA Modules:
  0.0 312.7 jit_solution(14843465336803265542)
XLA Ops:
  0.6 69.6 %shard_map.179 = (bf16[4,4,2,4,32,1152]{5,4,3,2,1,0:T(8,128)(2,1)}, bf16[4,2,128,1152]{3,2,1,0:T(8,128)(2,1)}, f32[128,128]{1,0:T(8,128)}, f32[128,128]{1,0:T(8,128)}, s32[1,128]{1,0:T(1,128)}) custom-call(s32[91]{0:T(128)} %own_ref.5, f32[1152,256]{1,0:T(8,128)} %bitcast.22, bf16[128,1152]{1,0:T(8,128)(2,1)} %bitcast.24, f32[1,5120]{1,0:T(1,128)} %bitcast.33), custom_call_target="tpu_custom_call" | custom-call | tf_op jit(solution)/shard_map/pallas_call | solution.py:241
  70.3 119.4 %shard_map.180 = (bf16[128,1152]{1,0:T(8,128)(2,1)}, f32[128,1152]{1,0:T(8,128)}, bf16[128,1152]{1,0:T(8,128)(2,1)}, f32[3,1152]{1,0:T(4,128)}, bf16[6,8,32,128]...) custom-call(s32[1,128]{1,0:T(1,128)} %doc_ref.1, ...), custom_call_target="tpu_custom_call" | custom-call | tf_op jit(solution)/shard_map/pallas_call | solution.py:550
  189.7 110.7 %shard_map.181 = (bf16[8,32,1152]{2,1,0:T(8,128)(2,1)}, f32[128,1152]{1,0:T(8,128)}, f32[40,128]{1,0:T(8,128)}, f32[40,128]{1,0:T(8,128)}, f32[40,128]{1,0:T(8,128)}) custom-call(s32[128]{0:T(128)} %bitcast.41, bf16[128,1152]{1,0:T(8,128)(2,1)} %get-tuple-element.40.dap_ref, bf16[8,32,512]{2,1,0:T(8,128)(2,1)} %get-tuple-element.41.osl_ref, ...), custom_call_target="tpu_custom_call" | custom-call | tf_op jit(solution)/shard_map/pallas_call | solution.py:943
  300.4 0.0 copy-start.1
  300.4 0.0 copy-start
  300.4 8.7 %shard_map.182 = (f32[1152,256]{1,0:T(8,128)}, f32[1152,256]{1,0:T(8,128)}, f32[1152,256]{1,0:T(8,128)}) custom-call(s32[91]{0:T(128)} %own_ref.5, bf16[8,32,1152]{2,1,0:T(8,128)(2,1)} %get-tuple-element.53.g_ref, f32[1152,1152]{1,0:T(8,128)} %bitcast.21, f32[256,256]{1,0:T(8,128)} %bitcast.32, f32[1152,256]{1,0:T(8,128)} %bitcast.23, f32[1152,256]{1,0:T(8,128)} %bitcast.27, ...), custom_call_target="tpu_custom_call" | custom-call | tf_op jit(solution)/shard_map/pallas_call | solution.py:1039
  309.2 0.0 copy-start.4
  309.2 0.0 copy-start.3
  309.2 0.0 copy-start.2
  309.2 0.0 copy-done.1
  309.2 0.7 copy.25
  309.9 0.0 copy-done
  309.9 0.8 copy.26
  310.7 0.0 copy-done.4
  310.7 0.6 copy.27
  311.3 0.0 copy-done.3
  311.3 0.6 copy.28
  311.9 0.0 copy-done.2
  312.0 0.6 copy.29
Async XLA Ops:
  300.4 8.8 %copy-start.1 = (bf16[128,1152]{1,0:T(8,128)(2,1)S(1)}, bf16[128,1152]{1,0:T(8,128)(2,1)}, u32[]{:S(2)}) copy-start(bf16[128,1152]{1,0:T(8,128)(2,1)} %get-tuple-element.38) | copy-start | bytes 884740
  300.4 9.5 %copy-start = (f32[128,1152]{1,0:T(8,128)S(1)}, f32[128,1152]{1,0:T(8,128)}, u32[]{:S(2)}) copy-start(f32[128,1152]{1,0:T(8,128)} %get-tuple-element.52) | copy-start | bytes 1769476
  309.2 1.6 copy-start.4
  309.2 2.2 copy-start.3
  309.2 2.8 copy-start.2

commit v4 on v0

v4 whole, which is shorter than its diff:
```python
import functools

import jax
import jax.numpy as jnp
from jax import lax
from jax.experimental import pallas as pl
from jax.experimental.pallas import tpu as pltpu
from jax.sharding import Mesh
from jax.sharding import PartitionSpec as P

FF = 6912
HEADS = 4
WINDOW = 512
BLK = 64
STEP = 10
D = 1152
HD = 256
TOK = 128
GROUP = 8
SLICE = HD // GROUP
ATT = 2 * HEADS + 2
FFT = FF // HD

NORM_EPS = 1e-06
THETA = 10000.0
BETA_ONE = 0.5
BETA_TWO = 0.5
RATE = 0.02
GAIN_RATE = 0.4
DECAY = 0.01
ADAM_EPS = 1e-08

MESH = pl.DeviceIdType.MESH
AXES = ("y", "z", "xh", "core", "xl")
VMEM_LIMIT = 63 * 1024 * 1024
BF = jnp.bfloat16
F32 = jnp.float32


def here():
    y, z, xh, c, xl = [lax.axis_index(a) for a in AXES]
    return y, z, xh * 2 + xl, c


def place(y, z, x, c):
    return (y, z, x // 2, c, lax.rem(x, 2))


def member(x, c):
    return (x // 2) * 4 + c * 2 + lax.rem(x, 2)


def turn(a, d):
    return lax.rem(a + d, 4)


def remote(src, dst, send, recv, where):
    return pltpu.make_async_remote_copy(src, dst, send, recv, device_id=where, device_id_type=MESH)


def params(cid):
    return pltpu.CompilerParams(
        collective_id=cid, has_side_effects=True, vmem_limit_bytes=VMEM_LIMIT
    )


ANY = pl.BlockSpec(memory_space=pl.ANY)
INV = pl.BlockSpec(memory_space=pltpu.VMEM)
DMA = pltpu.SemaphoreType.DMA


def seq_place(s):
    return (s // 16, lax.rem(s // 4, 4), lax.rem(s // 2, 2), lax.rem(s, 2), lax.axis_index("xl"))


def seq_index():
    y, z, xh, c, xl = [lax.axis_index(a) for a in AXES]
    return ((y * 4 + z) * 2 + xh) * 2 + c


def norm_of(v, g):
    return v * lax.rsqrt(jnp.mean(v * v, axis=-1, keepdims=True) + NORM_EPS) * g


def norm_back(v, g, w):
    r = lax.rsqrt(jnp.mean(v * v, axis=-1, keepdims=True) + NORM_EPS)
    u = w * g
    dg = jnp.sum(w * (v * r), axis=0, keepdims=True)
    dv = r * u - v * (r * r * r * jnp.mean(u * v, axis=-1, keepdims=True))
    return dv, dg


def column(g_ref, i):
    row = g_ref[:, 4 * D + i * HD : 4 * D + (i + 1) * HD]
    return jnp.broadcast_to(row, (128, HD)).T[:, 0:1]


def rope_norm(v, g, cos, sin):
    n = v * lax.rsqrt(jnp.mean(v * v, axis=0, keepdims=True) + NORM_EPS) * g
    a, b = n[: HD // 2], n[HD // 2 :]
    return jnp.concatenate([a * cos - b * sin, b * cos + a * sin], axis=0)


def gelu_parts(g):
    k, a = 0.7978845608028654, 0.044715
    sq = g * g
    th = jnp.tanh(k * g * (1.0 + a * sq))
    half = 0.5 * (1.0 + th)
    slope = half + 0.5 * g * (1.0 - th * th) * (k * (1.0 + 3.0 * a * sq))
    return g * half, slope


def nn(a, b):
    return jnp.dot(a, b, preferred_element_type=F32)


def nt(a, b):
    return lax.dot_general(a, b, (((1,), (1,)), ((), ())), preferred_element_type=F32)


def rope_norm_back(v, g, cos, sin, w):
    r = lax.rsqrt(jnp.mean(v * v, axis=0, keepdims=True) + NORM_EPS)
    a, b = w[: HD // 2], w[HD // 2 :]
    dn = jnp.concatenate([a * cos + b * sin, b * cos - a * sin], axis=0)
    dg = jnp.sum(dn * (v * r), axis=1, keepdims=True)
    u = dn * g
    dv = r * u - v * (r * r * r * jnp.mean(u * v, axis=0, keepdims=True))
    return dv, dg


def rows_add(dst, srcs, n):
    def step(i, carry):
        t = dst[i].astype(F32)
        for s in srcs:
            t = t + s[i].astype(F32)
        dst[i] = t.astype(BF)
        return carry

    lax.fori_loop(0, n, step, 0)


ORDER = (0, 3, 1, 2)
JS = (2, 1, 3, 0)
FFW = FFT * SLICE
ROWS = TOK // SLICE


def layer_body(
    doc_ref, own_ref, m_ref, x_ref, y_ref, g_ref,
    lo_ref, ig_ref, gsum_ref, grad_ref, xa_hbm,
    tile, grp, tile_of, tile_ref, wall, wf, xf, dd, dap_all, ab, bb, sbuf, near, far, t1, t2, u1, u2, fin,
    wo, ptl, qt, kb, vt, raw, oto, osl, sq, watt, dst, dot_, hsend, hrec, dqk, drec, dsl,
    da, a1, amid, a2, att, gl, gin, gmid, gin2,
    load_sem, ts, tr, n1s, n1r, n2s, n2r, n3s, n3r, n4s, n4r, xxs, xxr, xcs, xcr, c1s, c1r, c2s, c2r, c3s, c3r, c4s, c4r,
    as_, ar, wxs, wxr, wcs, wcr, hs, hr, os_, or_, fxs, fxr, fcs, fcr, bxs, bxr, bcs, bcr,
    ss, sr, rs_, rr, axs, axr, acs, acr, hbs, hbr, qs, qr, g1s, g1r, g2s, g2r, k1s, k1r, k2s, k2r,
    fs, fr, gas, gar, gbs, gbr,
):
    y, z, x, c = here()
    me = x * 2 + c
    twin = place(y, z, x, 1 - c)
    s = seq_index()
    chips = {d: turn(x, d) for d in range(4)}
    peers = {d: place(y, z, chips[d], c) for d in (1, 2, 3)}
    others = [(d, cc) for d in (1, 2, 3) for cc in range(2)]
    field = [(o - 1, place(turn(y, o // 4), turn(z, o % 4), x, c)) for o in range(1, 16)]
    mine_k = y * 4 + z
    at = (y, z)
    ring = (
        {d: place(turn(y, d), z, x, c) for d in (1, 2, 3)},
        {d: place(y, turn(z, d), x, c) for d in (1, 2, 3)},
    )
    partners = (
        [place(y, z, chips[d], cc) for d, cc in others]
        + [twin]
        + [seq_place(lax.rem(s + 64 + d, 64)) for d in (-4, -3, -2, -1, 1, 2, 3, 4)]
        + [f[1] for f in field]
    )
    sem = pltpu.get_barrier_semaphore()
    for p in partners:
        pl.semaphore_signal(sem, inc=1, device_id=p, device_id_type=MESH)
    for h in range(2):
        tile[4 * h : 4 * h + 4] = m_ref[:, h * 128 : (h + 1) * 128].T.astype(BF).reshape(4, SLICE, D)
    pl.semaphore_wait(sem, len(partners))
    sent = []

    def go(step):
        step.start()
        sent.append(step)
        return step

    def settle(steps):
        for step in steps:
            step.wait_send()
        sent[:] = [a for a in sent if not any(a is b for b in steps)]

    mm = member(x, c)
    base = mine_k * GROUP
    for d, cc in [(2, 0), (2, 1), (1, 0), (1, 1), (3, 0), (3, 1)]:
        go(remote(tile.at[chips[d] * 2 + cc], grp.at[mm], ts.at[d, cc], tr.at[d, c], place(y, z, chips[d], cc)))
    go(remote(tile.at[x * 2 + 1 - c], grp.at[mm], ts.at[0, 0], tr.at[0, c], twin))
    grp[mm] = tile[me]
    dd[x, c] = norm_of(x_ref[...].astype(F32), g_ref[:, 0:D]).astype(BF)
    mine = dd.at[x, c]
    x_far = {d: go(remote(mine, mine, xxs.at[d - 1], xxr.at[d - 1], peers[d])) for d in (1, 3, 2)}
    x_near = {0: go(remote(mine, mine, xcs.at[0], xcr.at[0], twin))}
    pos = s * TOK + lax.broadcasted_iota(jnp.int32, (HD // 2, TOK), 1)
    freq = lax.broadcasted_iota(jnp.int32, (HD // 2, TOK), 0).astype(F32)
    angle = pos.astype(F32) * jnp.exp(-jnp.log(THETA) * freq * 2.0 / HD)
    cos, sin = jnp.cos(angle), jnp.sin(angle)
    lane = lax.broadcasted_iota(jnp.int32, (1, 128), 1)
    tile_of[...] = lax.fori_loop(
        0,
        ATT + 3 * FFT,
        lambda t, acc: jnp.where(lane == own_ref[t], t, acc),
        jnp.zeros((1, 128), jnp.int32),
    )
    to_scalars = pltpu.make_async_copy(tile_of, tile_ref, load_sem.at[0])
    to_scalars.start()
    for d, cc in others:
        remote(tile.at[0], grp.at[mm], ts.at[d, cc], tr.at[d, cc], twin).wait_recv()
    remote(tile.at[0], grp.at[mm], ts.at[0, 0], tr.at[0, 1 - c], twin).wait_recv()
    def halves(h):
        return slice(h * 16, h * 16 + 16)

    def lay(t, v):
        for k in range(9):
            da[t * 9 + k] = v[:, k * 128 : (k + 1) * 128]

    def taken(t):
        return jnp.concatenate([att[t * 9 + k] for k in range(9)], axis=1)

    def set_out(ph):
        steps = []
        for d in (2, 1, 3):
            for h in (0, 1):
                src = da.at[pl.ds(24 * turn(at[h], d), 24), halves(h)]
                steps.append(go(remote(src, a1.at[ph, h, d - 1], c1s.at[ph, h, d - 1], c1r.at[ph, h, d - 1], ring[h][d])))
        return steps

    def add_up(ph, first):
        for step in first:
            step.wait_recv()
        for h in (0, 1):
            tot = da[pl.ds(24 * at[h], 24), halves(h)].astype(F32)
            for i in range(3):
                tot = tot + a1[ph, h, i].astype(F32)
            amid[h] = tot.astype(BF)
        steps = []
        for d in (2, 1, 3):
            for h in (0, 1):
                src = amid.at[h, pl.ds(6 * turn(at[1 - h], d), 6)]
                dst = a2.at[ph, h, d - 1]
                steps.append(go(remote(src, dst, c2s.at[ph, h, d - 1], c2r.at[ph, h, d - 1], ring[1 - h][d])))
        return steps

    def give(ph, second):
        for step in second:
            step.wait_recv()
        steps = []
        for h in (0, 1):
            tot = amid[h, pl.ds(6 * at[1 - h], 6)].astype(F32)
            for i in range(3):
                tot = tot + a2[ph, h, i].astype(F32)
            att[pl.ds(24 * at[h] + 6 * at[1 - h], 6), halves(h)] = tot.astype(BF)
            src = att.at[pl.ds(24 * at[h] + 6 * at[1 - h], 6), halves(h)]
            for d in (2, 1, 3):
                steps.append(go(remote(src, src, c3s.at[ph, h, d - 1], c3r.at[ph, h, d - 1], ring[1 - h][d])))
        return steps

    def give_on(ph, third):
        for step in third:
            step.wait_recv()
        steps = []
        for h in (0, 1):
            src = att.at[pl.ds(24 * at[h], 24), halves(h)]
            for d in (2, 1, 3):
                steps.append(go(remote(src, src, c4s.at[ph, h, d - 1], c4r.at[ph, h, d - 1], ring[h][d])))
        return steps

    for t in range(ATT):
        rel = own_ref[t] - base
        v = grp[jnp.clip(rel, 0, GROUP - 1)]
        lay(t, jnp.where((rel >= 0) & (rel < GROUP), v, jnp.zeros_like(v)))

    routed = set_out(0)
    wall[pl.ds(base, GROUP)] = grp[...]

    w_at = (z, y)
    f_at = {h: {d: turn(w_at[h], d) for d in range(4)} for h in (0, 1)}
    s_at = {h: {d: turn(w_at[1 - h], d) for d in range(4)} for h in (0, 1)}
    ways = ((0, 1, 3), (1, 3, 1))

    def block(h, first, second):
        yy, zz = (second, first) if h == 0 else (first, second)
        return wall.at[pl.ds(((yy * 4 + zz) * 2 + h) * 4, 4)]

    one, two, far1 = {}, {}, {}
    for h in (0, 1):
        for n, up, _ in ways:
            src = grp.at[4 * h : 4 * h + 4]
            one[h, n] = go(remote(src, block(h, f_at[h][0], s_at[h][0]), n1s.at[h, n], n1r.at[h, n], ring[1 - h][up]))

    def second(k):
        for h in (0, 1):
            b = block(h, f_at[h][k], s_at[h][0])
            src = b if k else grp.at[4 * h : 4 * h + 4]
            for n, up, _ in ways:
                two[h, k, n] = go(remote(src, b, n2s.at[h, k, n], n2r.at[h, k, n], ring[h][up]))

    def onward(k):
        for h in (0, 1):
            for n, up, down in ways:
                two[h, k, n].wait_recv()
                b = block(h, f_at[h][k], s_at[h][down]).at[2 * n : 2 * n + 2]
                last.append(go(remote(b, b, n4s.at[h, k, n], n4r.at[h, k, n], ring[h][up])))

    last = []
    for d in (1, 3, 2):
        x_far[d].wait_recv()
        src = dd.at[chips[4 - d], c]
        x_near[d] = go(remote(src, src, xcs.at[d], xcr.at[d], twin))
    added = add_up(0, routed)
    second(0)
    for h in (0, 1):
        for n, up, down in ways:
            one[h, n].wait_recv()
            b = block(h, f_at[h][down], s_at[h][0]).at[2 * n : 2 * n + 2]
            far1[h, n] = go(remote(b, b, n3s.at[h, n], n3r.at[h, n], ring[1 - h][up]))
    given = give(0, added)
    for step in x_near.values():
        step.wait_recv()
    save_x = pltpu.make_async_copy(dd, xa_hbm, load_sem.at[1])
    save_x.start()
    given_on = give_on(0, given)
    second(3)
    for step in given_on:
        step.wait_recv()

    for t in range(HEADS + 2):
        watt[t * SLICE : (t + 1) * SLICE] = taken(t)
    for h in range(HEADS):
        wo[h, me] = taken(HEADS + 2 + h)
    for d in (2, 1, 3, 0):
        part = nt(watt[...], dd[chips[d]].reshape(2 * TOK, D)).astype(BF)
        for cc in range(2):
            sq[d, cc] = part[:, cc * TOK : (cc + 1) * TOK].reshape(HEADS + 2, SLICE, TOK)
        if d:
            for cc in range(2):
                go(remote(sq.at[d, cc], raw.at[:, me], as_.at[d, cc], ar.at[d, c], place(y, z, chips[d], cc)))
    go(remote(sq.at[0, 1 - c], raw.at[:, me], as_.at[0, 0], ar.at[0, c], twin))
    raw[:, me] = sq[0, c]
    for d, cc in others:
        remote(sq.at[d, cc], raw.at[:, me], as_.at[d, cc], ar.at[d, cc], twin).wait_recv()
    remote(sq.at[0, 0], raw.at[:, me], as_.at[0, 0], ar.at[0, 1 - c], twin).wait_recv()

    gain_q, gain_k = column(g_ref, 0), column(g_ref, 1)
    kt = rope_norm(raw[HEADS].reshape(HD, TOK).astype(F32), gain_k, cos, sin)
    kb[4] = kt.T.astype(BF)
    vt[:, 4 * TOK :] = raw[HEADS + 1].reshape(HD, TOK)
    halo = []
    for d in (4, 3, 2, 1):
        to = seq_place(lax.rem(s + d, 64))
        lanes = slice((4 - d) * TOK, (5 - d) * TOK)
        halo.append(go(remote(kb.at[4], kb.at[4 - d], hs.at[0, d - 1], hr.at[0, d - 1], to)))
        halo.append(go(remote(vt.at[:, 4 * TOK :], vt.at[:, lanes], hs.at[1, d - 1], hr.at[1, d - 1], to)))
    mine = wo.at[:, me]
    w_far = {d: go(remote(mine, mine, wxs.at[d - 1], wxr.at[d - 1], peers[d])) for d in (1, 3, 2)}
    w_near = {0: go(remote(mine, mine, wcs.at[0], wcr.at[0], twin))}
    second(1)
    for step in far1.values():
        step.wait_recv()
    second(2)
    for h in range(HEADS):
        q = rope_norm(raw[h].reshape(HD, TOK).astype(F32), gain_q, cos, sin)
        qt[:, h * TOK : (h + 1) * TOK] = q.astype(BF)
    row = lax.broadcasted_iota(jnp.int32, (WINDOW + TOK, TOK), 0)
    col = lax.broadcasted_iota(jnp.int32, (WINDOW + TOK, TOK), 1)
    seen = (row <= col + WINDOW) & (row > col) & (row >= WINDOW - s * TOK)
    half = lax.broadcasted_iota(jnp.int32, (BLK, TOK), 1) < BLK
    q_doc = jnp.where(half, doc_ref[0, 2 * s], doc_ref[0, 2 * s + 1])
    k_doc = jnp.concatenate(
        [jnp.full((BLK, TOK), doc_ref[0, jnp.maximum(2 * s - 8 + b, 0)], jnp.int32) for b in range(10)],
        axis=0,
    )
    seen = seen & (k_doc == jnp.concatenate([q_doc] * 10, axis=0))
    onward(0)
    for step in halo:
        step.wait_recv()
    keys = kb[...].reshape(WINDOW + TOK, HD)
    for h in range(HEADS):
        lanes = slice(h * TOK, (h + 1) * TOK)
        sc = nn(keys, qt[:, lanes]) * (HD**-0.5)
        sc = jnp.where(seen, sc, -1e30)
        ex = jnp.exp(sc - jnp.max(sc, axis=0, keepdims=True))
        ptl[:, lanes] = (ex / jnp.sum(ex, axis=0, keepdims=True)).astype(BF)
    ot = nn(vt[...], ptl[...])
    oto[...] = ot.astype(BF)
    for d, cc in others:
        rows = pl.ds(pl.multiple_of((chips[d] * 2 + cc) * SLICE, SLICE), SLICE)
        go(remote(oto.at[rows], osl.at[me], os_.at[d, cc], or_.at[d, c], place(y, z, chips[d], cc)))
    rows = pl.ds(pl.multiple_of((x * 2 + 1 - c) * SLICE, SLICE), SLICE)
    go(remote(oto.at[rows], osl.at[me], os_.at[0, 0], or_.at[0, c], twin))
    osl[me] = oto[pl.ds(pl.multiple_of(me * SLICE, SLICE), SLICE)]

    onward(3)
    onward(1)
    for d in (1, 3, 2):
        w_far[d].wait_recv()
        src = wo.at[:, chips[4 - d] * 2 + c]
        w_near[d] = go(remote(src, src, wcs.at[d], wcr.at[d], twin))
    for step in w_near.values():
        step.wait_recv()
    ap = jnp.zeros((TOK, D), F32)
    for h in range(HEADS):
        o = ot[:, h * TOK : (h + 1) * TOK].T.astype(BF)
        ap = ap + nn(o, wo[h].reshape(HD, D))
    act = x_ref[...].astype(F32)
    r1 = act + norm_of(ap, g_ref[:, 1 * D : 2 * D])
    xf[x, c] = norm_of(r1, g_ref[:, 2 * D : 3 * D]).astype(BF)

    def gather_start(buf, xs, xr, cs, cr):
        own = buf.at[x, c]
        near_ = {0: go(remote(own, own, cs.at[0], cr.at[0], twin))}
        sends = {d: go(remote(own, own, xs.at[d - 1], xr.at[d - 1], peers[d])) for d in (1, 3, 2)}
        return sends, near_

    def gather_wait(buf, e, sends, near_, cs, cr):
        if e:
            d = 4 - e
            sends[d].wait_recv()
            src = buf.at[chips[e], c]
            near_[d] = go(remote(src, src, cs.at[d], cr.at[d], twin))
            near_[d].wait_recv()
        else:
            near_[0].wait_recv()

    def pbuf(ph, e, cc):
        return (wall if ph < 2 else wf).at[pl.ds((2 * e + cc) * ROWS, ROWS)]

    def sum_swap(ph, n, e):
        return go(remote(pbuf(ph, e, 1 - c), near.at[n, e], ss.at[ph, e], sr.at[ph, e], twin))

    def sum_send(ph, n, e, swap):
        swap.wait_recv()
        both = pbuf(ph, e, c)[...].astype(F32) + near[n, e].astype(F32)
        if not e:
            return None, both
        sbuf[e - 1] = both.astype(BF)
        return go(remote(sbuf.at[e - 1], far.at[n, e - 1], rs_.at[ph, e - 1], rr.at[ph, e - 1], peers[e])), None

    def finish(n, swaps, outs, ph, total=None):
        if total is None:
            _, total = sum_send(ph, n, 0, swaps[0])
            settle(list(swaps.values()))
        for step in outs:
            step.wait_recv()
        total = ((total + far[n, 0].astype(F32)) + far[n, 1].astype(F32)) + far[n, 2].astype(F32)
        settle(outs)
        return total.reshape(TOK, D)

    def pipeline(ph, order, ready, block):
        swaps, outs = {}, []
        for n, e in enumerate(order):
            ready(e)
            part = block(e).astype(BF).reshape(2, ROWS, SLICE, D)
            for cc in range(2):
                pbuf(ph, e, cc)[...] = part[cc]
            swaps[e] = sum_swap(ph, ph % 2, e)
            if n and order[n - 1]:
                outs.append(sum_send(ph, ph % 2, order[n - 1], swaps[order[n - 1]])[0])
        if order[3]:
            outs.append(sum_send(ph, ph % 2, order[3], swaps[order[3]])[0])
        return swaps, outs, ph

    def put(k, e, v):
        cols = pl.ds(pl.multiple_of(chips[e] * 2 * TOK, 2 * TOK), 2 * TOK)
        wall[32 + k * FFT : 32 + (k + 1) * FFT, :, cols] = v.T.reshape(FFT, SLICE, 2 * TOK)

    def tiles(k):
        return wf[k * FFT : (k + 1) * FFT].reshape(FFW, D)

    def forward(e):
        v = xf[chips[e]].reshape(2 * TOK, D)
        g = nt(v, tiles(0))
        u = nt(v, tiles(1))
        h, slope = gelu_parts(g)
        ab[e] = (u * slope).astype(BF)
        bb[e] = h.astype(BF)
        hid = (h * u).astype(BF)
        put(2, e, hid)
        return nn(hid, tiles(2))

    sends, near_ = gather_start(xf, fxs, fxr, fcs, fcr)
    onward(2)
    for step in last:
        step.wait_recv()

    def pack(t, carry):
        wf[t] = wall[own_ref[ATT + t]]
        return carry

    lax.fori_loop(0, 3 * FFT, pack, 0)
    settle(list(two.values()) + list(far1.values()) + last + list(x_far.values()) + list(x_near.values()))
    save_x.wait()
    to_scalars.wait()
    settle(routed + added + given + given_on)
    state = pipeline(0, ORDER, lambda e: gather_wait(xf, e, sends, near_, fcs, fcr), forward)
    dn = finish(0, *state)
    lo_ref[...] = (r1 + norm_of(dn, g_ref[:, 3 * D : 4 * D])).astype(BF)
    cot = y_ref[...].astype(F32)
    ddn, d_fpost = norm_back(dn, g_ref[:, 3 * D : 4 * D], cot)
    dd[x, c] = ddn.astype(BF)

    def backward(e):
        v = dd[chips[e]].reshape(2 * TOK, D)
        dh = nt(v, tiles(2))
        dg = (dh * ab[e].astype(F32)).astype(BF)
        du = (dh * bb[e].astype(F32)).astype(BF)
        put(0, e, dg)
        put(1, e, du)
        return nn(dg, tiles(0)) + nn(du, tiles(1))

    sends_b, near_b = gather_start(dd, bxs, bxr, bcs, bcr)
    state = pipeline(1, ORDER, lambda e: gather_wait(dd, e, sends_b, near_b, bcs, bcr), backward)

    for k, rhs in enumerate((xf, xf, dd)):
        left = wall[32 + k * FFT : 32 + (k + 1) * FFT, :, 0 : GROUP * TOK].reshape(FFW, GROUP * TOK)
        for n in range(3):
            cols = slice(n * 384, (n + 1) * 384)
            g = nn(left, rhs[:, :, :, cols].reshape(GROUP * TOK, 384)).astype(BF)
            wf[k * FFT : (k + 1) * FFT, :, cols] = g.reshape(FFT, SLICE, 384)
    _, rest = sum_send(1, 1, 0, state[0][0])
    settle(list(state[0].values()))

    def fill(i, carry):
        wall[i] = wf[jnp.clip(tile_ref[0, i] - ATT, 0, 3 * FFT - 1)]
        return carry

    lax.fori_loop(0, 128, fill, 0)

    def part(h, first, second):
        yy, zz = (first, second) if h == 0 else (second, first)
        return wall.at[pl.ds(((yy * 4 + zz) * 2 + h) * 4, 4)]

    here1 = {h: {d: turn(at[h], d) for d in range(4)} for h in (0, 1)}
    here2 = {h: {d: turn(at[1 - h], d) for d in range(4)} for h in (0, 1)}
    s1 = {}
    for j in JS:
        for h in (0, 1):
            blk = part(h, here1[h][2], here2[h][j])
            s1[h, j, 0] = go(remote(blk.at[0:2], t1.at[h, j, 0], g1s.at[h, j, 0], g1r.at[h, j, 0], ring[h][1]))
            s1[h, j, 1] = go(remote(blk.at[2:4], t1.at[h, j, 1], g1s.at[h, j, 1], g1r.at[h, j, 1], ring[h][3]))

    dxf = finish(1, *state, rest)
    e1, d_fpre = norm_back(r1, g_ref[:, 2 * D : 3 * D], dxf)
    dr1 = cot + e1
    ig_ref[...] = dr1
    dap, d_apost = norm_back(ap, g_ref[:, 1 * D : 2 * D], dr1)
    dap_all[x, c] = dap.astype(BF)
    sends_a, near_a = gather_start(dap_all, axs, axr, acs, acr)

    dmix = nt(wo[...].reshape(HEADS * HD, D), dap.astype(BF)).astype(BF)
    for h in range(HEADS):
        dot_[:, h * TOK : (h + 1) * TOK] = dmix[h * HD : (h + 1) * HD]
    values = jnp.concatenate([vt[:, b * TOK : (b + 1) * TOK].T for b in range(5)], axis=0)
    for h in range(HEADS):
        lanes = slice(h * TOK, (h + 1) * TOK)
        pr = ptl[:, lanes].astype(F32)
        dp = nn(values, dot_[:, lanes])
        inner = jnp.sum(pr * dp, axis=0, keepdims=True)
        dst[:, lanes] = (pr * (dp - inner) * (HD**-0.5)).astype(BF)
    dk = nt(qt[...], dst[...])
    dv = nt(dot_[...], ptl[...])
    back = []
    for d in (4, 3, 2, 1):
        lanes = slice((4 - d) * TOK, (5 - d) * TOK)
        hsend[d - 1, 0] = dk[:, lanes].astype(BF)
        hsend[d - 1, 1] = dv[:, lanes].astype(BF)
        to = seq_place(lax.rem(s + 64 - d, 64))
        back.append(go(remote(hsend.at[d - 1], hrec.at[d - 1], hbs.at[d - 1], hbr.at[d - 1], to)))
    dk = dk[:, 4 * TOK :]
    dv = dv[:, 4 * TOK :]
    settle(list(sends.values()) + list(near_.values()))
    load_x = pltpu.make_async_copy(xa_hbm, xf, load_sem.at[2])
    load_x.start()
    keys_t = jnp.concatenate([kb[b].T for b in range(5)], axis=1)
    dgq = jnp.zeros((HD, 1), F32)
    for h in range(HEADS):
        dq = nn(keys_t, dst[:, h * TOK : (h + 1) * TOK])
        dq, dg = rope_norm_back(raw[h].reshape(HD, TOK).astype(F32), gain_q, cos, sin, dq)
        dqk[h] = dq.astype(BF).reshape(GROUP, SLICE, TOK)
        dgq = dgq + dg

    for step in back:
        step.wait_recv()
    for d in range(4):
        dk = dk + hrec[d, 0].astype(F32)
        dv = dv + hrec[d, 1].astype(F32)
    dk, dgk = rope_norm_back(raw[HEADS].reshape(HD, TOK).astype(F32), gain_k, cos, sin, dk)
    dqk[HEADS] = dk.astype(BF).reshape(GROUP, SLICE, TOK)
    dqk[HEADS + 1] = dv.astype(BF).reshape(GROUP, SLICE, TOK)
    for d, cc in others:
        to = chips[d] * 2 + cc
        go(remote(dqk.at[:, to], drec.at[me], qs.at[d, cc], qr.at[d, c], place(y, z, chips[d], cc)))
    go(remote(dqk.at[:, x * 2 + 1 - c], drec.at[me], qs.at[0, 0], qr.at[0, c], twin))
    drec[me] = dqk[:, me]

    s2 = {}

    def pass_on(j):
        for h in (0, 1):
            s1[h, j, 0].wait_recv()
            blk = part(h, here1[h][1], here2[h][j])
            rows_add(blk.at[0:2], [t1.at[h, j, 0]], 2)
            s2[h, j, 0] = go(remote(blk, t2.at[h, j, 0], g2s.at[h, j, 0], g2r.at[h, j, 0], ring[h][1]))
            s1[h, j, 1].wait_recv()
            blk = part(h, here1[h][3], here2[h][j])
            rows_add(blk.at[2:4], [t1.at[h, j, 1]], 2)
            s2[h, j, 1] = go(remote(blk, t2.at[h, j, 1], g2s.at[h, j, 1], g2r.at[h, j, 1], ring[h][3]))

    for e in (0, 3, 1, 2):
        gather_wait(dap_all, e, sends_a, near_a, acs, acr)
    for d, cc in others:
        remote(oto.at[0:SLICE], osl.at[me], os_.at[d, cc], or_.at[d, cc], twin).wait_recv()
    remote(oto.at[0:SLICE], osl.at[me], os_.at[0, 0], or_.at[0, 1 - c], twin).wait_recv()
    for h in range(HEADS):
        for p in range(GROUP):
            dsl[h * SLICE : (h + 1) * SLICE, p * TOK : (p + 1) * TOK] = osl[p, :, h * TOK : (h + 1) * TOK]
    g = nn(dsl[0 : HEADS * SLICE], dap_all[...].reshape(GROUP * TOK, D)).astype(BF)
    for h in range(HEADS):
        lay(HEADS + 2 + h, g[h * SLICE : (h + 1) * SLICE])

    pass_on(2)
    pass_on(1)
    for d, cc in others:
        remote(dqk.at[:, 0], drec.at[me], qs.at[d, cc], qr.at[d, cc], twin).wait_recv()
    remote(dqk.at[:, 0], drec.at[me], qs.at[0, 0], qr.at[0, 1 - c], twin).wait_recv()
    for p in range(GROUP):
        dsl[:, p * TOK : (p + 1) * TOK] = drec[p].reshape((HEADS + 2) * SLICE, TOK)
    load_x.wait()
    g = nn(dsl[...], xf[...].reshape(GROUP * TOK, D)).astype(BF)
    for t in range(HEADS + 2):
        lay(t, g[t * SLICE : (t + 1) * SLICE])

    routed = set_out(1)
    pass_on(3)
    pass_on(0)

    def inputs_back(e):
        pair = [
            nn(drec[chips[e] * 2 + cc].reshape((HEADS + 2) * SLICE, TOK).T, watt[...]) for cc in range(2)
        ]
        return jnp.concatenate(pair, axis=0)

    state = pipeline(2, JS, lambda e: None, inputs_back)

    added = add_up(1, routed)

    def close(j):
        for h in (0, 1):
            s2[h, j, 0].wait_recv()
            s2[h, j, 1].wait_recv()
            rows_add(part(h, here1[h][0], here2[h][j]), [t2.at[h, j, 0], t2.at[h, j, 1]], 4)

    e1, e2 = {}, {}
    close(2)
    for h in (0, 1):
        blk = part(h, here1[h][0], here2[h][2])
        e1[h, 0] = go(remote(blk.at[0:2], u1.at[h, 0], k1s.at[h, 0], k1r.at[h, 0], ring[1 - h][1]))
        e1[h, 1] = go(remote(blk.at[2:4], u1.at[h, 1], k1s.at[h, 1], k1r.at[h, 1], ring[1 - h][3]))

    close(1)
    close(3)
    given = give(1, added)
    for n, j in ((0, 1), (1, 3)):
        for h in (0, 1):
            blk = part(h, here1[h][0], here2[h][j])
            e1[h, n].wait_recv()
            rows_add(blk.at[2 * n : 2 * n + 2], [u1.at[h, n]], 2)
            e2[h, n] = go(remote(blk, u2.at[h, n], k2s.at[h, n], k2r.at[h, n], ring[1 - h][j]))

    given_on = give_on(1, given)
    dxa = finish(0, *state)
    ein, d_apre = norm_back(x_ref[...].astype(F32), g_ref[:, 0 * D : 1 * D], dxa)
    ig_ref[...] = ig_ref[...] + ein
    for k in range(9):
        lanes = slice(k * 128, (k + 1) * 128)
        for m, dg in enumerate((d_apre, d_apost, d_fpre, d_fpost)):
            gl[9 * m + k : 9 * m + k + 1] = dg[:, lanes]
    for m, dg in enumerate((dgq, dgk)):
        flat = jnp.broadcast_to(dg, (HD, 128)).T
        for k in range(2):
            gl[36 + 2 * m + k : 37 + 2 * m + k] = flat[0:1, k * 128 : (k + 1) * 128]
    for d, cc in others:
        go(remote(gl, gin.at[x, c], gas.at[d, cc], gar.at[d, c], place(y, z, chips[d], cc)))
    go(remote(gl, gin.at[x, c], gas.at[0, 0], gar.at[0, c], twin))
    gin[x, c] = gl[...]

    for d, cc in others:
        remote(gl, gin.at[x, c], gas.at[d, cc], gar.at[d, cc], twin).wait_recv()
    remote(gl, gin.at[x, c], gas.at[0, 0], gar.at[0, 1 - c], twin).wait_recv()
    acc = gin[0, 0]
    for p in range(1, GROUP):
        acc = acc + gin[p // 2, p % 2]
    gmid[...] = acc
    gin2[mine_k] = acc
    all_gains = [go(remote(gmid, gin2.at[mine_k], gbs.at[o], gbr.at[o], to)) for o, to in field]
    close(0)

    for step in given_on:
        step.wait_recv()
    for h in (0, 1):
        e2[h, 0].wait_recv()
        e2[h, 1].wait_recv()
        blk = part(h, here1[h][0], here2[h][0])
        rows_add(blk, [u2.at[h, 0], u2.at[h, 1]], 4)
    for q in range(GROUP):
        t = tile_ref[0, base + q]
        low = taken(jnp.clip(t, 0, ATT - 1))
        fin[q] = jnp.where(t < ATT, low, wall[base + q])
    for d, cc in others:
        src = fin.at[member(chips[d], cc)]
        go(remote(src, grad_ref.at[me], fs.at[d, cc], fr.at[d, c], place(y, z, chips[d], cc)))
    go(remote(fin.at[member(x, 1 - c)], grad_ref.at[me], fs.at[0, 0], fr.at[0, c], twin))
    grad_ref[me] = fin[member(x, c)]
    for step in all_gains:
        step.wait_recv()
    acc = gin2[0]
    for k in range(1, 16):
        acc = acc + gin2[k]
    gsum_ref[...] = acc
    for d, cc in others:
        remote(fin.at[0], grad_ref.at[me], fs.at[d, cc], fr.at[d, cc], twin).wait_recv()
    remote(fin.at[0], grad_ref.at[me], fs.at[0, 0], fr.at[0, 1 - c], twin).wait_recv()
    for step in sent:
        step.wait_send()


def run_layer(doc, owners, master, x, y, gains, cid):
    f = jax.ShapeDtypeStruct
    smem = pl.BlockSpec(memory_space=pltpu.SMEM)
    vm = pltpu.VMEM
    blocks = (TOK // SLICE, SLICE, D)
    lanes = HEADS * TOK
    seen = WINDOW + TOK
    qkv = HEADS + 2
    return pl.pallas_call(
        layer_body,
        out_shape=(
            f((TOK, D), BF),
            f((TOK, D), F32),
            f((40, 128), F32),
            f((GROUP, SLICE, D), BF),
            f((4, 2, TOK, D), BF),
        ),
        in_specs=[smem, smem, INV, INV, INV, INV],
        out_specs=(INV, INV, INV, INV, ANY),
        scratch_shapes=[
            vm((GROUP, SLICE, D), BF),
            vm((GROUP, SLICE, D), BF),
            vm((1, 128), jnp.int32),
            pltpu.SMEM((1, 128), jnp.int32),
            vm((128, SLICE, D), BF),
            vm((3 * FFT, SLICE, D), BF),
            vm((4, 2, TOK, D), BF),
            vm((4, 2, TOK, D), BF),
            vm((4, 2, TOK, D), BF),
            vm((4, 2 * TOK, FFW), BF),
            vm((4, 2 * TOK, FFW), BF),
            vm((3,) + blocks, BF),
            vm((2, 4) + blocks, BF),
            vm((2, 3) + blocks, BF),
            vm((2, 4, 2, 2, SLICE, D), BF),
            vm((2, 4, 2, 4, SLICE, D), BF),
            vm((2, 2, 2, SLICE, D), BF),
            vm((2, 2, 4, SLICE, D), BF),
            vm((GROUP, SLICE, D), BF),
            vm((HEADS, GROUP, SLICE, D), BF),
            vm((seen, lanes), BF),
            vm((HD, lanes), BF),
            vm((5, TOK, HD), BF),
            vm((HD, seen), BF),
            vm((qkv, GROUP, SLICE, TOK), BF),
            vm((HD, lanes), BF),
            vm((GROUP, SLICE, lanes), BF),
            vm((4, 2, qkv, SLICE, TOK), BF),
            vm((qkv * SLICE, D), BF),
            vm((seen, lanes), BF),
            vm((HD, lanes), BF),
            vm((4, 2, HD, TOK), BF),
            vm((4, 2, HD, TOK), BF),
            vm((qkv, GROUP, SLICE, TOK), BF),
            vm((GROUP, qkv, SLICE, TOK), BF),
            vm((qkv * SLICE, GROUP * TOK), BF),
            vm((96, SLICE, 128), BF),
            vm((2, 2, 3, 24, 16, 128), BF),
            vm((2, 24, 16, 128), BF),
            vm((2, 2, 3, 6, 16, 128), BF),
            vm((96, SLICE, 128), BF),
            vm((40, 128), F32),
            vm((4, 2, 40, 128), F32),
            vm((40, 128), F32),
            vm((16, 40, 128), F32),
            DMA((3,)),
            DMA((4, 2)), DMA((4, 2)),
            DMA((2, 2)), DMA((2, 2)), DMA((2, 4, 2)), DMA((2, 4, 2)),
            DMA((2, 2)), DMA((2, 2)), DMA((2, 4, 2)), DMA((2, 4, 2)),
            DMA((3,)), DMA((3,)), DMA((4,)), DMA((4,)),
            DMA((2, 2, 3)), DMA((2, 2, 3)), DMA((2, 2, 3)), DMA((2, 2, 3)),
            DMA((2, 2, 3)), DMA((2, 2, 3)), DMA((2, 2, 3)), DMA((2, 2, 3)),
            DMA((4, 2)), DMA((4, 2)),
            DMA((3,)), DMA((3,)), DMA((4,)), DMA((4,)),
            DMA((2, 4)), DMA((2, 4)),
            DMA((4, 2)), DMA((4, 2)),
            DMA((3,)), DMA((3,)), DMA((4,)), DMA((4,)),
            DMA((3,)), DMA((3,)), DMA((4,)), DMA((4,)),
            DMA((3, 4)), DMA((3, 4)), DMA((3, 3)), DMA((3, 3)),
            DMA((3,)), DMA((3,)), DMA((4,)), DMA((4,)),
            DMA((4,)), DMA((4,)),
            DMA((4, 2)), DMA((4, 2)),
            DMA((2, 4, 2)), DMA((2, 4, 2)), DMA((2, 4, 2)), DMA((2, 4, 2)),
            DMA((2, 2)), DMA((2, 2)), DMA((2, 2)), DMA((2, 2)),
            DMA((4, 2)), DMA((4, 2)),
            DMA((4, 2)), DMA((4, 2)),
            DMA((15,)), DMA((15,)),
        ],
        compiler_params=params(cid),
    )(doc, owners, master, x, y, gains)


def step_body(
    own_ref, g_ref, gsum_ref, gain_ref, gf_ref, gs_ref, lo_ref, ig_ref, l_hbm, r_hbm, m_hbm, f_hbm, s_hbm,
    mo_hbm, fo_hbm, so_hbm, ng_ref, nf_ref, ns_ref, lo_out, ig_out, lv, rv, mv, fv, sv, lb, sem,
):
    y, z, x, c = here()
    slot = (y * 4 + z) * GROUP + member(x, c)
    ins = [
        pltpu.make_async_copy(a, b, sem.at[i])
        for i, (a, b) in enumerate(((l_hbm, lv), (r_hbm, rv), (f_hbm, fv), (s_hbm, sv), (m_hbm, mv)))
    ]
    for step in ins:
        step.start()
    lo_out[...] = lo_ref[...]
    ig_out[...] = ig_ref[...]
    acc = gsum_ref[...]
    first = BETA_ONE * gf_ref[...] + (1.0 - BETA_ONE) * acc
    second = BETA_TWO * gs_ref[...] + (1.0 - BETA_TWO) * acc * acc
    nf_ref[...] = first
    ns_ref[...] = second
    u = first / (1.0 - BETA_ONE**STEP) / (jnp.sqrt(second / (1.0 - BETA_TWO**STEP)) + ADAM_EPS)
    ng_ref[...] = gain_ref[...] - GAIN_RATE * u
    owned = lax.fori_loop(0, ATT + 3 * FFT, lambda t, a: a + (own_ref[t] == slot).astype(jnp.int32), 0) > 0
    ins[0].wait()
    lb[...] = lv[...].astype(BF)
    rot = nn(g_ref[...].reshape(HD, D), lb[...])
    ins[1].wait()
    right = rv[...].astype(BF)
    rot = nn(rot.T.astype(BF), right)
    ins[2].wait()
    ins[3].wait()
    first = BETA_ONE * fv[...] + (1.0 - BETA_ONE) * rot
    second = BETA_TWO * sv[...] + (1.0 - BETA_TWO) * rot * rot
    u = first / (1.0 - BETA_ONE**STEP) / (jnp.sqrt(second / (1.0 - BETA_TWO**STEP)) + ADAM_EPS)
    fv[...] = jnp.where(owned, first, fv[...])
    sv[...] = jnp.where(owned, second, sv[...])
    outs = [pltpu.make_async_copy(fv, fo_hbm, sem.at[5]), pltpu.make_async_copy(sv, so_hbm, sem.at[6])]
    for step in outs:
        step.start()
    back = nn(lb[...], nt(u.astype(BF), right).astype(BF))
    ins[4].wait()
    w = mv[...]
    mv[...] = jnp.where(owned, w - RATE * (back + DECAY * w), w)
    outs.append(pltpu.make_async_copy(mv, mo_hbm, sem.at[7]))
    outs[2].start()
    for step in outs:
        step.wait()


def run_step(owners, grad, gsum, gains, gain_first, gain_second, lo, ig, left, right, master, first, second):
    f = jax.ShapeDtypeStruct
    vm = pltpu.VMEM
    tile = f((D, HD), F32)
    row = f((40, 128), F32)
    return pl.pallas_call(
        step_body,
        out_shape=(tile, tile, tile, row, row, row, f((TOK, D), BF), f((TOK, D), F32)),
        in_specs=[pl.BlockSpec(memory_space=pltpu.SMEM)] + [INV] * 7 + [ANY] * 5,
        out_specs=(ANY, ANY, ANY, INV, INV, INV, INV, INV),
        scratch_shapes=[
            vm((D, D), F32), vm((HD, HD), F32), vm((D, HD), F32), vm((D, HD), F32), vm((D, HD), F32), vm((D, D), BF),
            DMA((8,)),
        ],
        compiler_params=pltpu.CompilerParams(vmem_limit_bytes=VMEM_LIMIT),
    )(owners, grad, gsum, gains, gain_first, gain_second, lo, ig, left, right, master, first, second)


def local(
    inputs,
    out_grad,
    doc_ids,
    owners,
    masters,
    first_old,
    second_old,
    left_basis,
    right_basis,
    gains,
    gain_first,
    gain_second,
):
    x = inputs[0]
    row = gains.reshape(1, 5120)
    lo, ig, gsum, grad, _ = run_layer(doc_ids, owners, masters[0], x, out_grad[0], row, 1)
    square = [a.reshape(40, 128) for a in (gains, gain_first, gain_second)]
    new_masters, new_first, new_second, new_gains, new_gain_first, new_gain_second, layer_out, input_grad = run_step(
        owners, grad, gsum, *square, lo, ig, left_basis[0], right_basis[0], masters[0], first_old[0], second_old[0]
    )
    return (
        layer_out[None],
        input_grad[None],
        new_masters[None],
        new_first[None],
        new_second[None],
        new_gains.reshape(5120),
        new_gain_first.reshape(5120),
        new_gain_second.reshape(5120),
    )


def solution(mesh):
    wide = Mesh(mesh.devices.reshape(4, 4, 2, 2, 2), AXES)
    tokens = P("xl", ("y", "z", "xh", "core"), None)
    held = P(AXES, None, None)
    return jax.shard_map(
        local,
        mesh=wide,
        in_specs=(tokens, tokens, P("xl", None), P(), held, held, held, held, held, P(), P(), P()),
        out_specs=(tokens, tokens, held, held, held, P(), P(), P()),
        check_vma=False,
    )
```

time: 3210 us -> 271 us (0.08)
  waiting for transfers between devices: 2760 us -> 0 us
  Pallas kernels: 0 us -> 266 us
  matrix products: 197 us -> 0 us
  local copies, waits for them, and re-layouts: 91.6 us -> 0 us
  blocking collectives: 79 us -> 0 us
  other arithmetic: 51.5 us -> 0 us
    reduce_scatter x1 -> x0, waiting for transfers between devices: 2340 us -> none  [local(): lax.psum_scatter(jnp.where(present[:, None, None], jnp.einsum('std,tsc->s...]
    all_gather x1 -> x0, waiting for transfers between devices: 418 us -> none  [local(): gathered = lax.all_gather(low_masters, ('seq', 'rep'), axis=0, tiled=True)]
    pallas_call x0 -> x2, Pallas kernels: none -> 266 us  [the longest x1 256 us: run_layer(): pl.pallas_call(layer_body, out_shape=(f((TOK, D), BF), f((TOK, D), F32),...]
    dot_general x24 -> x0, matrix products: 195 us -> none  [the longest x1 67.6 us: local(): jnp.einsum('std,tsc->sdc', left_sel, right_sel, preferred_element_type=jn...]
    psum x1 -> x0, blocking collectives: 79 us -> none  [local(): gain_grads = lax.psum(gain_local, ('seq', 'rep'))]
    gather x3 -> x0, local copies, waits for them, and re-layouts: 59.8 us -> none  [the longest x1 36.3 us: local(): tiles = jnp.take(gathered, owners, axis=0)]
    select_n x3 -> x0, other arithmetic: 36.1 us -> none  [the longest x2 36.1 us: local(): tiles = jnp.take(gathered, owners, axis=0)]
  transfers between devices with their start and end apart: 10 -> 0, of which waited for: 2 -> 0; matrix products, arithmetic and copies ran while one was open for 1% -> 0% of each run, Pallas kernels for 0% -> 0%
where the time goes in v4:
time: 271 us; the launch traced here: 267 us
  Pallas kernels  266 us (98%)
    pallas_call x1, Pallas kernels, run_layer(): pl.pallas_call(layer_body, out_shape=(f((TOK, D), BF), f((TOK, D), F32),...  256 us
    pallas_call x1, Pallas kernels, run_step(): pl.pallas_call(step_body, out_shape=(tile, tile, tile, row, row, row, f((...  9.92 us

profile of v4, /device:TPU:1, one launch (start us, length us, event | category | flops | bytes accessed | tf_op | source)
XLA Modules:
  0.0 266.5 jit_solution(9655593501754796823)
XLA Ops:
  0.6 255.7 %shard_map.179 = (bf16[128,1152]{1,0:T(8,128)(2,1)}, f32[128,1152]{1,0:T(8,128)}, f32[40,128]{1,0:T(8,128)}, bf16[8,32,1152]{2,1,0:T(8,128)(2,1)}, bf16[4,2,128,1152]{3,2,1,0:T(8,128)(2,1)}) custom-call(s32[1,128]{1,0:T(1,128)} %doc_ref.1, s32[91]{0:T(128)} %own_ref.3, f32[1152,256]{1,0:T(8,128)} %bitcast.20, bf16[128,1152]{1,0:T(8,128)(2,1)} %bitcast.24, ...), custom_call_target="tpu_custom_call" | custom-call | tf_op jit(solution)/shard_map/pallas_call | solution.py:748
  256.3 9.9 %shard_map.180 = (f32[1152,256]{1,0:T(8,128)}, f32[1152,256]{1,0:T(8,128)}, f32[1152,256]{1,0:T(8,128)}, f32[40,128]{1,0:T(8,128)}, f32[40,128]{1,0:T(8,128)}, /...) custom-call(s32[91]{0:T(128)} %own_ref.3, bf16[8,32,1152]{2,1,0:T(8,128)(2,1)} %get-tuple-element.20.g_ref, ...), custom_call_target="tpu_custom_call" | custom-call | tf_op jit(solution)/shard_map/pallas_call | solution.py:885

commit v5 on v4

--- a/solution.py
+++ b/solution.py
@@ -332,8 +332,9 @@
         step.wait_recv()
     save_x = pltpu.make_async_copy(dd, xa_hbm, load_sem.at[1])
     save_x.start()
+    second(3)
     given_on = give_on(0, given)
-    second(3)
+    second(1)
     for step in given_on:
         step.wait_recv()
 
@@ -350,6 +351,10 @@
                 go(remote(sq.at[d, cc], raw.at[:, me], as_.at[d, cc], ar.at[d, c], place(y, z, chips[d], cc)))
     go(remote(sq.at[0, 1 - c], raw.at[:, me], as_.at[0, 0], ar.at[0, c], twin))
     raw[:, me] = sq[0, c]
+    mine = wo.at[:, me]
+    w_far = {d: go(remote(mine, mine, wxs.at[d - 1], wxr.at[d - 1], peers[d])) for d in (1, 3)}
+    w_near = {0: go(remote(mine, mine, wcs.at[0], wcr.at[0], twin))}
+    onward(0)
     for d, cc in others:
         remote(sq.at[d, cc], raw.at[:, me], as_.at[d, cc], ar.at[d, cc], twin).wait_recv()
     remote(sq.at[0, 0], raw.at[:, me], as_.at[0, 0], ar.at[0, 1 - c], twin).wait_recv()
@@ -364,13 +369,12 @@
         lanes = slice((4 - d) * TOK, (5 - d) * TOK)
         halo.append(go(remote(kb.at[4], kb.at[4 - d], hs.at[0, d - 1], hr.at[0, d - 1], to)))
         halo.append(go(remote(vt.at[:, 4 * TOK :], vt.at[:, lanes], hs.at[1, d - 1], hr.at[1, d - 1], to)))
-    mine = wo.at[:, me]
-    w_far = {d: go(remote(mine, mine, wxs.at[d - 1], wxr.at[d - 1], peers[d])) for d in (1, 3, 2)}
-    w_near = {0: go(remote(mine, mine, wcs.at[0], wcr.at[0], twin))}
-    second(1)
+    w_far[2] = go(remote(mine, mine, wxs.at[1], wxr.at[1], peers[2]))
     for step in far1.values():
         step.wait_recv()
     second(2)
+    onward(3)
+    onward(1)
     for h in range(HEADS):
         q = rope_norm(raw[h].reshape(HD, TOK).astype(F32), gain_q, cos, sin)
         qt[:, h * TOK : (h + 1) * TOK] = q.astype(BF)
@@ -384,7 +388,6 @@
         axis=0,
     )
     seen = seen & (k_doc == jnp.concatenate([q_doc] * 10, axis=0))
-    onward(0)
     for step in halo:
         step.wait_recv()
     keys = kb[...].reshape(WINDOW + TOK, HD)
@@ -403,8 +406,7 @@
     go(remote(oto.at[rows], osl.at[me], os_.at[0, 0], or_.at[0, c], twin))
     osl[me] = oto[pl.ds(pl.multiple_of(me * SLICE, SLICE), SLICE)]
 
-    onward(3)
-    onward(1)
+    onward(2)
     for d in (1, 3, 2):
         w_far[d].wait_recv()
         src = wo.at[:, chips[4 - d] * 2 + c]
@@ -419,10 +421,10 @@
     r1 = act + norm_of(ap, g_ref[:, 1 * D : 2 * D])
     xf[x, c] = norm_of(r1, g_ref[:, 2 * D : 3 * D]).astype(BF)
 
-    def gather_start(buf, xs, xr, cs, cr):
+    def gather_start(buf, xs, xr, cs, cr, first=(1, 3, 2)):
         own = buf.at[x, c]
         near_ = {0: go(remote(own, own, cs.at[0], cr.at[0], twin))}
-        sends = {d: go(remote(own, own, xs.at[d - 1], xr.at[d - 1], peers[d])) for d in (1, 3, 2)}
+        sends = {d: go(remote(own, own, xs.at[d - 1], xr.at[d - 1], peers[d])) for d in first}
         return sends, near_
 
     def gather_wait(buf, e, sends, near_, cs, cr):
@@ -492,7 +494,6 @@
         return nn(hid, tiles(2))
 
     sends, near_ = gather_start(xf, fxs, fxr, fcs, fcr)
-    onward(2)
     for step in last:
         step.wait_recv()
 
@@ -558,7 +559,7 @@
     ig_ref[...] = dr1
     dap, d_apost = norm_back(ap, g_ref[:, 1 * D : 2 * D], dr1)
     dap_all[x, c] = dap.astype(BF)
-    sends_a, near_a = gather_start(dap_all, axs, axr, acs, acr)
+    sends_a, near_a = gather_start(dap_all, axs, axr, acs, acr, (1, 3))
 
     dmix = nt(wo[...].reshape(HEADS * HD, D), dap.astype(BF)).astype(BF)
     for h in range(HEADS):
@@ -581,6 +582,23 @@
         back.append(go(remote(hsend.at[d - 1], hrec.at[d - 1], hbs.at[d - 1], hbr.at[d - 1], to)))
     dk = dk[:, 4 * TOK :]
     dv = dv[:, 4 * TOK :]
+    own = dap_all.at[x, c]
+    sends_a[2] = go(remote(own, own, axs.at[1], axr.at[1], peers[2]))
+
+    s2 = {}
+
+    def pass_on(j):
+        for h in (0, 1):
+            s1[h, j, 0].wait_recv()
+            blk = part(h, here1[h][1], here2[h][j])
+            rows_add(blk.at[0:2], [t1.at[h, j, 0]], 2)
+            s2[h, j, 0] = go(remote(blk, t2.at[h, j, 0], g2s.at[h, j, 0], g2r.at[h, j, 0], ring[h][1]))
+            s1[h, j, 1].wait_recv()
+            blk = part(h, here1[h][3], here2[h][j])
+            rows_add(blk.at[2:4], [t1.at[h, j, 1]], 2)
+            s2[h, j, 1] = go(remote(blk, t2.at[h, j, 1], g2s.at[h, j, 1], g2r.at[h, j, 1], ring[h][3]))
+
+    pass_on(2)
     settle(list(sends.values()) + list(near_.values()))
     load_x = pltpu.make_async_copy(xa_hbm, xf, load_sem.at[2])
     load_x.start()
@@ -592,6 +610,7 @@
         dqk[h] = dq.astype(BF).reshape(GROUP, SLICE, TOK)
         dgq = dgq + dg
 
+    pass_on(1)
     for step in back:
         step.wait_recv()
     for d in range(4):
@@ -606,19 +625,7 @@
     go(remote(dqk.at[:, x * 2 + 1 - c], drec.at[me], qs.at[0, 0], qr.at[0, c], twin))
     drec[me] = dqk[:, me]
 
-    s2 = {}
-
-    def pass_on(j):
-        for h in (0, 1):
-            s1[h, j, 0].wait_recv()
-            blk = part(h, here1[h][1], here2[h][j])
-            rows_add(blk.at[0:2], [t1.at[h, j, 0]], 2)
-            s2[h, j, 0] = go(remote(blk, t2.at[h, j, 0], g2s.at[h, j, 0], g2r.at[h, j, 0], ring[h][1]))
-            s1[h, j, 1].wait_recv()
-            blk = part(h, here1[h][3], here2[h][j])
-            rows_add(blk.at[2:4], [t1.at[h, j, 1]], 2)
-            s2[h, j, 1] = go(remote(blk, t2.at[h, j, 1], g2s.at[h, j, 1], g2r.at[h, j, 1], ring[h][3]))
-
+    pass_on(3)
     for e in (0, 3, 1, 2):
         gather_wait(dap_all, e, sends_a, near_a, acs, acr)
     for d, cc in others:
@@ -631,8 +638,7 @@
     for h in range(HEADS):
         lay(HEADS + 2 + h, g[h * SLICE : (h + 1) * SLICE])
 
-    pass_on(2)
-    pass_on(1)
+    pass_on(0)
     for d, cc in others:
         remote(dqk.at[:, 0], drec.at[me], qs.at[d, cc], qr.at[d, cc], twin).wait_recv()
     remote(dqk.at[:, 0], drec.at[me], qs.at[0, 0], qr.at[0, 1 - c], twin).wait_recv()
@@ -644,8 +650,6 @@
         lay(t, g[t * SLICE : (t + 1) * SLICE])
 
     routed = set_out(1)
-    pass_on(3)
-    pass_on(0)
 
     def inputs_back(e):
         pair = [
@@ -835,11 +839,14 @@
 ):
     y, z, x, c = here()
     slot = (y * 4 + z) * GROUP + member(x, c)
+    third = D // 3
+    cuts = [slice(k * third, (k + 1) * third) for k in range(3)]
+    pieces = [pltpu.make_async_copy(l_hbm.at[r], lv.at[r], sem.at[8 + k]) for k, r in enumerate(cuts)]
     ins = [
         pltpu.make_async_copy(a, b, sem.at[i])
-        for i, (a, b) in enumerate(((l_hbm, lv), (r_hbm, rv), (f_hbm, fv), (s_hbm, sv), (m_hbm, mv)))
+        for i, (a, b) in enumerate(((r_hbm, rv), (f_hbm, fv), (s_hbm, sv), (m_hbm, mv)))
     ]
-    for step in ins:
+    for step in pieces + ins:
         step.start()
     lo_out[...] = lo_ref[...]
     ig_out[...] = ig_ref[...]
@@ -851,14 +858,17 @@
     u = first / (1.0 - BETA_ONE**STEP) / (jnp.sqrt(second / (1.0 - BETA_TWO**STEP)) + ADAM_EPS)
     ng_ref[...] = gain_ref[...] - GAIN_RATE * u
     owned = lax.fori_loop(0, ATT + 3 * FFT, lambda t, a: a + (own_ref[t] == slot).astype(jnp.int32), 0) > 0
+    grad = g_ref[...].reshape(HD, D)
+    rot = jnp.zeros((HD, D), F32)
+    for step, r in zip(pieces, cuts):
+        step.wait()
+        lb[r] = lv[r].astype(BF)
+        rot = rot + nn(grad[:, r], lb[r])
     ins[0].wait()
-    lb[...] = lv[...].astype(BF)
-    rot = nn(g_ref[...].reshape(HD, D), lb[...])
-    ins[1].wait()
     right = rv[...].astype(BF)
     rot = nn(rot.T.astype(BF), right)
+    ins[1].wait()
     ins[2].wait()
-    ins[3].wait()
     first = BETA_ONE * fv[...] + (1.0 - BETA_ONE) * rot
     second = BETA_TWO * sv[...] + (1.0 - BETA_TWO) * rot * rot
     u = first / (1.0 - BETA_ONE**STEP) / (jnp.sqrt(second / (1.0 - BETA_TWO**STEP)) + ADAM_EPS)
@@ -867,12 +877,14 @@
     outs = [pltpu.make_async_copy(fv, fo_hbm, sem.at[5]), pltpu.make_async_copy(sv, so_hbm, sem.at[6])]
     for step in outs:
         step.start()
-    back = nn(lb[...], nt(u.astype(BF), right).astype(BF))
-    ins[4].wait()
-    w = mv[...]
-    mv[...] = jnp.where(owned, w - RATE * (back + DECAY * w), w)
-    outs.append(pltpu.make_async_copy(mv, mo_hbm, sem.at[7]))
-    outs[2].start()
+    turned = nt(u.astype(BF), right).astype(BF)
+    ins[3].wait()
+    for k, r in enumerate(cuts):
+        back = nn(lb[r], turned)
+        w = mv[r]
+        mv[r] = jnp.where(owned, w - RATE * (back + DECAY * w), w)
+        outs.append(pltpu.make_async_copy(mv.at[r], mo_hbm.at[r], sem.at[12 + k]))
+        outs[-1].start()
     for step in outs:
         step.wait()
 
@@ -889,7 +901,7 @@
         out_specs=(ANY, ANY, ANY, INV, INV, INV, INV, INV),
         scratch_shapes=[
             vm((D, D), F32), vm((HD, HD), F32), vm((D, HD), F32), vm((D, HD), F32), vm((D, HD), F32), vm((D, D), BF),
-            DMA((8,)),
+            DMA((16,)),
         ],
         compiler_params=pltpu.CompilerParams(vmem_limit_bytes=VMEM_LIMIT),
     )(owners, grad, gsum, gains, gain_first, gain_second, lo, ig, left, right, master, first, second)

time: 271 us -> 258 us (0.952)
  Pallas kernels: 266 us -> 253 us
    pallas_call x1, Pallas kernels: 256 us -> 244 us  [run_layer(): pl.pallas_call(layer_body, out_shape=(f((TOK, D), BF), f((TOK, D), F32),...]
where the time goes in v5:
time: 258 us; the launch traced here: 254 us
  Pallas kernels  253 us (98%)
    pallas_call x1, Pallas kernels, run_layer(): pl.pallas_call(layer_body, out_shape=(f((TOK, D), BF), f((TOK, D), F32),...  244 us
    pallas_call x1, Pallas kernels, run_step(): pl.pallas_call(step_body, out_shape=(tile, tile, tile, row, row, row, f((...  9.21 us

profile of v5, /device:TPU:1, one launch (start us, length us, event | category | flops | bytes accessed | tf_op | source)
XLA Modules:
  0.0 253.9 jit_solution(5998061235743892677)
XLA Ops:
  0.6 243.6 %shard_map.179 = (bf16[128,1152]{1,0:T(8,128)(2,1)}, f32[128,1152]{1,0:T(8,128)}, f32[40,128]{1,0:T(8,128)}, bf16[8,32,1152]{2,1,0:T(8,128)(2,1)}, bf16[4,2,128,1152]{3,2,1,0:T(8,128)(2,1)}) custom-call(s32[1,128]{1,0:T(1,128)} %doc_ref.1, s32[91]{0:T(128)} %own_ref.3, f32[1152,256]{1,0:T(8,128)} %bitcast.20, bf16[128,1152]{1,0:T(8,128)(2,1)} %bitcast.24, ...), custom_call_target="tpu_custom_call" | custom-call | tf_op jit(solution)/shard_map/pallas_call | solution.py:752
  244.2 9.2 %shard_map.180 = (f32[1152,256]{1,0:T(8,128)}, f32[1152,256]{1,0:T(8,128)}, f32[1152,256]{1,0:T(8,128)}, f32[40,128]{1,0:T(8,128)}, f32[40,128]{1,0:T(8,128)}, /...) custom-call(s32[91]{0:T(128)} %own_ref.3, bf16[8,32,1152]{2,1,0:T(8,128)(2,1)} %get-tuple-element.20.g_ref, ...), custom_call_target="tpu_custom_call" | custom-call | tf_op jit(solution)/shard_map/pallas_call | solution.py:897

commit v6 on v5

--- a/solution.py
+++ b/solution.py
@@ -162,7 +162,7 @@
     s = seq_index()
     chips = {d: turn(x, d) for d in range(4)}
     peers = {d: place(y, z, chips[d], c) for d in (1, 2, 3)}
-    others = [(d, cc) for d in (1, 2, 3) for cc in range(2)]
+    others = [(d, cc) for d in (2, 1, 3) for cc in range(2)]
     field = [(o - 1, place(turn(y, o // 4), turn(z, o % 4), x, c)) for o in range(1, 16)]
     mine_k = y * 4 + z
     at = (y, z)
@@ -196,7 +196,7 @@
 
     mm = member(x, c)
     base = mine_k * GROUP
-    for d, cc in [(2, 0), (2, 1), (1, 0), (1, 1), (3, 0), (3, 1)]:
+    for d, cc in others:
         go(remote(tile.at[chips[d] * 2 + cc], grp.at[mm], ts.at[d, cc], tr.at[d, c], place(y, z, chips[d], cc)))
     go(remote(tile.at[x * 2 + 1 - c], grp.at[mm], ts.at[0, 0], tr.at[0, c], twin))
     grp[mm] = tile[me]
@@ -651,16 +651,6 @@
 
     routed = set_out(1)
 
-    def inputs_back(e):
-        pair = [
-            nn(drec[chips[e] * 2 + cc].reshape((HEADS + 2) * SLICE, TOK).T, watt[...]) for cc in range(2)
-        ]
-        return jnp.concatenate(pair, axis=0)
-
-    state = pipeline(2, JS, lambda e: None, inputs_back)
-
-    added = add_up(1, routed)
-
     def close(j):
         for h in (0, 1):
             s2[h, j, 0].wait_recv()
@@ -673,6 +663,16 @@
         blk = part(h, here1[h][0], here2[h][2])
         e1[h, 0] = go(remote(blk.at[0:2], u1.at[h, 0], k1s.at[h, 0], k1r.at[h, 0], ring[1 - h][1]))
         e1[h, 1] = go(remote(blk.at[2:4], u1.at[h, 1], k1s.at[h, 1], k1r.at[h, 1], ring[1 - h][3]))
+
+    def inputs_back(e):
+        pair = [
+            nn(drec[chips[e] * 2 + cc].reshape((HEADS + 2) * SLICE, TOK).T, watt[...]) for cc in range(2)
+        ]
+        return jnp.concatenate(pair, axis=0)
+
+    state = pipeline(2, JS, lambda e: None, inputs_back)
+
+    added = add_up(1, routed)
 
     close(1)
     close(3)

time: 258 us -> 256 us (level)
  no operation moved by 1% of the time
where the time goes in v6:
time: 256 us; the launch traced here: 252 us
  Pallas kernels  251 us (98%)
    pallas_call x1, Pallas kernels, run_layer(): pl.pallas_call(layer_body, out_shape=(f((TOK, D), BF), f((TOK, D), F32),...  241 us
    pallas_call x1, Pallas kernels, run_step(): pl.pallas_call(step_body, out_shape=(tile, tile, tile, row, row, row, f((...  9.21 us

profile of v6, /device:TPU:1, one launch (start us, length us, event | category | flops | bytes accessed | tf_op | source)
XLA Modules:
  0.0 251.7 jit_solution(12355061513568413219)
XLA Ops:
  0.6 241.4 %shard_map.179 = (bf16[128,1152]{1,0:T(8,128)(2,1)}, f32[128,1152]{1,0:T(8,128)}, f32[40,128]{1,0:T(8,128)}, bf16[8,32,1152]{2,1,0:T(8,128)(2,1)}, bf16[4,2,128,1152]{3,2,1,0:T(8,128)(2,1)}) custom-call(s32[1,128]{1,0:T(1,128)} %doc_ref.1, s32[91]{0:T(128)} %own_ref.3, f32[1152,256]{1,0:T(8,128)} %bitcast.20, bf16[128,1152]{1,0:T(8,128)(2,1)} %bitcast.24, ...), custom_call_target="tpu_custom_call" | custom-call | tf_op jit(solution)/shard_map/pallas_call | solution.py:752
  242.1 9.2 %shard_map.180 = (f32[1152,256]{1,0:T(8,128)}, f32[1152,256]{1,0:T(8,128)}, f32[1152,256]{1,0:T(8,128)}, f32[40,128]{1,0:T(8,128)}, f32[40,128]{1,0:T(8,128)}, /...) custom-call(s32[91]{0:T(128)} %own_ref.3, bf16[8,32,1152]{2,1,0:T(8,128)(2,1)} %get-tuple-element.20.g_ref, ...), custom_call_target="tpu_custom_call" | custom-call | tf_op jit(solution)/shard_map/pallas_call | solution.py:897
